TPU v7x, 128 devices: a whole 4x4x4 slice. The times are simulated.
128 devices in a mesh: row: 8 (over x, core), col: 16 (over z, y).
Axes of the slice: x: 4, y: 4, z: 4, core: 2. Of those that a mesh axis runs over, the one named last changes fastest.
Arguments:
- panel: float32 [6, 2048, 2048], P(None, 'row', 'col'), may hold values from -0.0625 to 0.0625
- inverse_blocks: float32 [4, 2048, 2048], P(None, 'row', 'col'), may hold values from -1.5 to 1.5, as said below
- trailing_factor: float32 [12, 2048, 4, 2048], P(None, 'row', None, 'col'), may hold values from -0.0625 to 0.0625
- columns: float32 [4, 2048, 1024], P(None, 'row', 'col'), may hold values from -6 to 6
- trailing_columns: float32 [12, 2048, 1024], P(None, 'row', 'col'), may hold values from -6 to 6
Outputs:
- whitened: float32 [4, 2048, 1024], P(None, 'row', 'col')
- updated: float32 [12, 2048, 1024], P(None, 'row', 'col')
- variance_drop: float32 [1024], P('col')
Inputs may be any that keep to these rules, and one draw needn't show every extreme that they name: `inverse_blocks`: each block is lower triangular; its diagonal entries lie between 0.5 and 1.5.
All inputs are finite; a program needn't handle non-finite values.
Results may differ from a plain program's by a relative error of at most 0.00011.
Values sent between devices are 32-bit elements; how exact they have to be, the bound alone decides.
No kernel may reach another device: no remote copies, remote signals or barrier semaphores. Data moves between devices by JAX's collectives and lax.ppermute only.
A program may use at most 128 MiB of HBM per device.

v0:
```python
import jax
import jax.numpy as jnp
from jax import lax
from jax.sharding import PartitionSpec as P


def product(left, right):
    return jnp.dot(left, right, precision=lax.Precision.HIGHEST, preferred_element_type=jnp.float32)


def remap(block):
    full = lax.all_gather(block, "row", axis=0, tiled=True)
    spread = lax.all_to_all(full, "col", split_axis=0, concat_axis=1, tiled=True)
    return (full, spread)


def shards(panel, inverse_blocks, trailing_factor, columns, trailing_columns):
    steps = columns.shape[0]
    order = columns.shape[1] * lax.axis_size("row")
    solved = []
    fulls = []
    spreads = []
    for j in range(steps):
        reduced = columns[j]
        if j > 0:
            partial_value = product(panel[j * (j - 1) // 2], spreads[0])
            for i in range(1, j):
                partial_value = partial_value + product(panel[j * (j - 1) // 2 + i], spreads[i])
            reduced = reduced - lax.psum_scatter(
                partial_value, "col", scatter_dimension=1, tiled=True
            )
        unused, reduced_spread = remap(reduced)
        result = lax.psum_scatter(
            product(inverse_blocks[j], reduced_spread), "col", scatter_dimension=1, tiled=True
        )
        full, spread = remap(result)
        solved.append(result)
        fulls.append(full)
        spreads.append(spread)
    whitened = jnp.stack(solved)
    stacked = jnp.stack(spreads)
    summed = lax.psum_scatter(
        jnp.einsum(
            "tajb,jbm->mta",
            trailing_factor,
            stacked,
            precision=lax.Precision.HIGHEST,
            preferred_element_type=jnp.float32,
        ),
        "col",
        scatter_dimension=0,
        tiled=True,
    )
    updated = trailing_columns - jnp.transpose(summed, (1, 2, 0))
    local_squares = jnp.sum(whitened * whitened, axis=(0, 1))
    variance_drop = lax.psum(local_squares, "row") / (steps * order)
    return (whitened, updated, variance_drop)


def solution(mesh):
    return jax.shard_map(
        shards,
        mesh=mesh,
        in_specs=(
            P(None, "row", "col"),
            P(None, "row", "col"),
            P(None, "row", None, "col"),
            P(None, "row", "col"),
            P(None, "row", "col"),
        ),
        out_specs=(P(None, "row", "col"), P(None, "row", "col"), P("col")),
        check_vma=False,
    )
```

profile of v0, /device:TPU:1, one launch (start us, length us, event | category | flops | bytes accessed | tf_op | source)
XLA Modules:
  0.0 888.9 jit_solution(15506476801214860721)
XLA Ops:
  7.2 0.9 slice.43
  8.1 14.8 %all-gather = f32[1,2048,64]{1,2,0:T(8,128)S(1)} all-gather(f32[1,256,64]{1,2,0:T(8,128)S(1)} %slice.43), channel_id=2, replica_groups=mesh['row'=8,'col'=16] {'row'}, dimensions={1}, use_global_device_ids=true | all-gather | bytes 589824 | tf_op jit(solution)/shard_map/all_gather | solution.py:12
  23.2 18.5 %all_to_all.149 = f32[16,128,64]{1,2,0:T(8,128)S(1)} all-to-all(f32[16,128,64]{1,2,0:T(8,128)S(1)} %copy.30), channel_id=1, replica_groups=mesh['row'=8,'col'=16] {'col'}, dimensions={0} | all-to-all | bytes 1048576 | tf_op jit(solution)/shard_map/all_to_all | solution.py:13
  41.7 2.0 fusion.24
  43.7 69.2 %reduce-scatter.9.cloned.1.call-done = f32[256,64]{0,1:T(8,128)} async-done(((f32[256,1024]{0,1:T(8,128)}), f32[256,64]{0,1:T(8,128)}) %reduce-scatter.9.cloned.1.call-update) | async-done | bytes 65552 | tf_op jit(solution)/shard_map/reduce_scatter | solution.py:33
  112.9 15.7 %all_gather.25 = f32[2048,64]{0,1:T(8,128)S(1)} all-gather(f32[256,64]{0,1:T(8,128)} %reduce-scatter.9.cloned.1.call-done), channel_id=1, replica_groups=mesh['row'=8,'col'=16] {'row'}, dimensions={0}, use_global_device_ids=true | all-gather | bytes 589824 | tf_op jit(solution)/shard_map/all_gather | solution.py:12
  128.7 15.4 %all_to_all.150 = f32[16,128,64]{1,2,0:T(8,128)S(1)} all-to-all(f32[16,128,64]{1,2,0:T(8,128)S(1)} %copy_bitcast_fusion.6), channel_id=1, replica_groups=mesh['row'=8,'col'=16] {'col'}, dimensions={0} | all-to-all | bytes 1048576 | tf_op jit(solution)/shard_map/all_to_all | solution.py:13
  144.0 2.0 convolution_bitcast_fusion.3
  146.1 69.3 %reduce-scatter.11.cloned.1.call-done = f32[256,64]{0,1:T(8,128)} async-done(((f32[256,1024]{0,1:T(8,128)}), f32[256,64]{0,1:T(8,128)}) %reduce-scatter.11.cloned.1.call-update) | async-done | bytes 65552 | tf_op jit(solution)/shard_map/reduce_scatter | solution.py:29
  215.3 0.9 bitcast_subtract_fusion.3
  216.2 15.5 %all_gather.26 = f32[2048,64]{0,1:T(8,128)S(1)} all-gather(f32[256,64]{0,1:T(8,128)S(1)} %bitcast_subtract_fusion.3), channel_id=1, replica_groups=mesh['row'=8,'col'=16] {'row'}, dimensions={0}, use_global_device_ids=true | all-gather | bytes 589824 | tf_op jit(solution)/shard_map/all_gather | solution.py:12
  231.8 15.3 %all_to_all.151 = f32[16,128,64]{1,2,0:T(8,128)S(1)} all-to-all(f32[16,128,64]{1,2,0:T(8,128)S(1)} %copy_bitcast_fusion.5), channel_id=1, replica_groups=mesh['row'=8,'col'=16] {'col'}, dimensions={0} | all-to-all | bytes 1048576 | tf_op jit(solution)/shard_map/all_to_all | solution.py:13
  247.1 2.0 convolution_bitcast_fusion.2
  249.1 69.2 %reduce-scatter.13.cloned.1.call-done = f32[256,64]{0,1:T(8,128)} async-done(((f32[256,1024]{0,1:T(8,128)}), f32[256,64]{0,1:T(8,128)}) %reduce-scatter.13.cloned.1.call-update) | async-done | bytes 65552 | tf_op jit(solution)/shard_map/reduce_scatter | solution.py:33
  318.3 15.7 %all_gather.27 = f32[2048,64]{0,1:T(8,128)S(1)} all-gather(f32[256,64]{0,1:T(8,128)} %reduce-scatter.13.cloned.1.call-done), channel_id=1, replica_groups=mesh['row'=8,'col'=16] {'row'}, dimensions={0}, use_global_device_ids=true | all-gather | bytes 589824 | tf_op jit(solution)/shard_map/all_gather | solution.py:12
  334.0 0.8 copy_bitcast_fusion.4
  334.9 4.6 all-to-all-start.3
  339.6 1.0 fusion.20
  340.6 9.9 %all-to-all-done.3 = f32[16,128,64]{1,2,0:T(8,128)S(1)} async-done(((f32[16,128,64]{1,2,0:T(8,128)}), f32[16,128,64]{1,2,0:T(8,128)S(1)}, u32[]{:S(2)}, u32[]{:S(2)}) %all-to-all-start.3) | async-done | bytes 524320 | tf_op jit(solution)/shard_map/all_to_all | solution.py:13
  350.5 2.0 fusion.12
  352.5 69.2 %reduce-scatter.15.cloned.1.call-done = f32[256,64]{0,1:T(8,128)} async-done(((f32[256,1024]{0,1:T(8,128)}), f32[256,64]{0,1:T(8,128)}) %reduce-scatter.15.cloned.1.call-update) | async-done | bytes 65552 | tf_op jit(solution)/shard_map/reduce_scatter | solution.py:29
  421.7 0.9 bitcast_subtract_fusion.2
  422.5 15.5 %all_gather.28 = f32[2048,64]{0,1:T(8,128)S(1)} all-gather(f32[256,64]{0,1:T(8,128)S(1)} %bitcast_subtract_fusion.2), channel_id=1, replica_groups=mesh['row'=8,'col'=16] {'row'}, dimensions={0}, use_global_device_ids=true | all-gather | bytes 589824 | tf_op jit(solution)/shard_map/all_gather | solution.py:12
  438.1 15.3 %all_to_all.152 = f32[16,128,64]{1,2,0:T(8,128)S(1)} all-to-all(f32[16,128,64]{1,2,0:T(8,128)S(1)} %copy_bitcast_fusion.3), channel_id=1, replica_groups=mesh['row'=8,'col'=16] {'col'}, dimensions={0} | all-to-all | bytes 1048576 | tf_op jit(solution)/shard_map/all_to_all | solution.py:13
  453.4 2.0 convolution_bitcast_fusion.1
  455.4 69.3 %reduce-scatter.17.cloned.1.call-done = f32[256,64]{0,1:T(8,128)} async-done(((f32[256,1024]{0,1:T(8,128)}), f32[256,64]{0,1:T(8,128)}) %reduce-scatter.17.cloned.1.call-update) | async-done | bytes 65552 | tf_op jit(solution)/shard_map/reduce_scatter | solution.py:33
  524.7 15.9 %all_gather.29 = f32[2048,64]{0,1:T(8,128)S(1)} all-gather(f32[256,64]{0,1:T(8,128)} %reduce-scatter.17.cloned.1.call-done), channel_id=1, replica_groups=mesh['row'=8,'col'=16] {'row'}, dimensions={0}, use_global_device_ids=true | all-gather | bytes 589824 | tf_op jit(solution)/shard_map/all_gather | solution.py:12
  540.6 0.8 copy_bitcast_fusion.2
  541.4 4.6 all-to-all-start.5
  546.1 1.0 fusion.16
  547.1 1.0 convolution_add_fusion.1
  548.1 8.9 all-to-all-done.5
  557.0 2.0 fusion.11
  559.0 69.2 %reduce-scatter.19.cloned.1.call-done = f32[256,64]{0,1:T(8,128)} async-done(((f32[256,1024]{0,1:T(8,128)}), f32[256,64]{0,1:T(8,128)}) %reduce-scatter.19.cloned.1.call-update) | async-done | bytes 65552 | tf_op jit(solution)/shard_map/reduce_scatter | solution.py:29
  628.2 0.9 bitcast_subtract_fusion.1
  629.1 15.5 %all_gather.30 = f32[2048,64]{0,1:T(8,128)S(1)} all-gather(f32[256,64]{0,1:T(8,128)S(1)} %bitcast_subtract_fusion.1), channel_id=1, replica_groups=mesh['row'=8,'col'=16] {'row'}, dimensions={0}, use_global_device_ids=true | all-gather | bytes 589824 | tf_op jit(solution)/shard_map/all_gather | solution.py:12
  644.7 15.3 %all_to_all.153 = f32[16,128,64]{1,2,0:T(8,128)S(1)} all-to-all(f32[16,128,64]{1,2,0:T(8,128)S(1)} %copy_bitcast_fusion.1), channel_id=1, replica_groups=mesh['row'=8,'col'=16] {'col'}, dimensions={0} | all-to-all | bytes 1048576 | tf_op jit(solution)/shard_map/all_to_all | solution.py:13
  660.0 2.9 convolution_bitcast_fusion
  663.0 69.2 %reduce-scatter.21.cloned.1.call-done = f32[256,64]{0,1:T(8,128)} async-done(((f32[256,1024]{0,1:T(8,128)}), f32[256,64]{0,1:T(8,128)}) %reduce-scatter.21.cloned.1.call-update) | async-done | bytes 65552 | tf_op jit(solution)/shard_map/reduce_scatter | solution.py:33
  732.1 15.7 %all_gather.31 = f32[2048,64]{0,1:T(8,128)S(1)} all-gather(f32[256,64]{0,1:T(8,128)} %reduce-scatter.21.cloned.1.call-done), channel_id=1, replica_groups=mesh['row'=8,'col'=16] {'row'}, dimensions={0}, use_global_device_ids=true | all-gather | bytes 589824 | tf_op jit(solution)/shard_map/all_gather | solution.py:12
  747.9 15.3 %all_to_all.154 = f32[16,128,64]{1,2,0:T(8,128)S(1)} all-to-all(f32[16,128,64]{1,2,0:T(8,128)S(1)} %copy_bitcast_fusion), channel_id=1, replica_groups=mesh['row'=8,'col'=16] {'col'}, dimensions={0} | all-to-all | bytes 1048576 | tf_op jit(solution)/shard_map/all_to_all | solution.py:13
  763.3 24.4 %fusion.2 = f32[1024,12,256]{2,0,1:T(8,128)} fusion(f32[12,256,4,128]{3,2,1,0:T(4,128)} %param.7, f32[1,128,1024]{1,2,0:T(8,128)S(1)} %bitcast.149, f32[1,128,1024]{1,2,0:T(8,128)S(1)} %bitcast.148, f32[1,128,1024]{1,2,0:T(8,128)S(1)} %bitcast.146, f32[1,128,1024]{1,2,0:T(8,128)S(1)} %bitcast.143), kind=kOutput, calls=%fused_computation.2 | convolution fusion | flops 19328925696 | bytes 20971520 | tf_op jit(solution)/shard_map/tajb,jbm->mta/dot_general | solution.py:43
  787.7 0.8 copy-done.3
  788.6 0.8 multiply_reduce_fusion
  789.4 13.3 %psum.7 = f32[64]{0:T(128)S(1)} all-reduce(f32[64]{0:T(128)S(1)} %get-tuple-element.3), channel_id=1, replica_groups=mesh['row'=8,'col'=16] {'row'}, use_global_device_ids=true, to_apply=%region_9.0 | all-reduce | flops 64 | bytes 512 | tf_op jit(solution)/shard_map/psum | solution.py:56
  802.8 0.5 broadcast_multiply_fusion
  803.3 76.6 %reduce-scatter.23.cloned.1.call-done = f32[64,12,256]{2,0,1:T(8,128)} async-done(((f32[1024,12,256]{2,0,1:T(8,128)}), f32[64,12,256]{2,0,1:T(8,128)}) %reduce-scatter.23.cloned.1.call-update) | async-done | bytes 786448 | tf_op jit(solution)/shard_map/reduce_scatter | solution.py:42
  879.9 2.1 bitcast_subtract_fusion
  (36 shorter events, 1.1 us)
Async XLA Ops:
  7.2 34.5 %copy-start.2 = (f32[4,256,128]{2,1,0:T(8,128)S(1)}, f32[4,256,128]{2,1,0:T(8,128)}, u32[]{:S(2)}) copy-start(f32[4,256,128]{2,1,0:T(8,128)} %param.6) | copy-start | bytes 1572868
  7.2 105.7 %reduce-scatter.9.cloned.1.call-start = ((), (), s32[]{:S(2)}) async-start(), calls=%async_computation.16 | async-start | bytes 1114112 | tf_op jit(solution)/shard_map/reduce_scatter | solution.py:33
  43.6 100.4 %copy-start.1 = (f32[6,256,128]{2,1,0:T(8,128)S(1)}, f32[6,256,128]{2,1,0:T(8,128)}, u32[]{:S(2)}) copy-start(f32[6,256,128]{2,1,0:T(8,128)} %param.5) | copy-start | bytes 2359300
  43.6 171.7 %reduce-scatter.11.cloned.1.call-start = ((), (), s32[]{:S(2)}) async-start(), calls=%async_computation.17 | async-start | bytes 1114112 | tf_op jit(solution)/shard_map/reduce_scatter | solution.py:29
  146.0 172.3 %reduce-scatter.13.cloned.1.call-start = ((), (), s32[]{:S(2)}) async-start(), calls=%async_computation.18 | async-start | bytes 1114112 | tf_op jit(solution)/shard_map/reduce_scatter | solution.py:33
  334.9 15.6 %all-to-all-start.3 = ((f32[16,128,64]{1,2,0:T(8,128)}), f32[16,128,64]{1,2,0:T(8,128)S(1)}, u32[]{:S(2)}, u32[]{:S(2)}) async-start(f32[16,128,64]{1,2,0:T(8,128)} %copy_bitcast_fusion.4), calls=%async_computation.6 | async-start | bytes 1048576 | tf_op jit(solution)/shard_map/all_to_all | solution.py:13
  339.5 82.1 %reduce-scatter.15.cloned.1.call-start = ((), (), s32[]{:S(2)}) async-start(), calls=%async_computation.19 | async-start | bytes 1114112 | tf_op jit(solution)/shard_map/reduce_scatter | solution.py:29
  352.4 172.3 %reduce-scatter.17.cloned.1.call-start = ((), (), s32[]{:S(2)}) async-start(), calls=%async_computation.20 | async-start | bytes 1114112 | tf_op jit(solution)/shard_map/reduce_scatter | solution.py:33
  541.4 15.6 %all-to-all-start.5 = ((f32[16,128,64]{1,2,0:T(8,128)}), f32[16,128,64]{1,2,0:T(8,128)S(1)}, u32[]{:S(2)}, u32[]{:S(2)}) async-start(f32[16,128,64]{1,2,0:T(8,128)} %copy_bitcast_fusion.2), calls=%async_computation.10 | async-start | bytes 1048576 | tf_op jit(solution)/shard_map/all_to_all | solution.py:13
  546.1 82.1 %reduce-scatter.19.cloned.1.call-start = ((), (), s32[]{:S(2)}) async-start(), calls=%async_computation.21 | async-start | bytes 1114112 | tf_op jit(solution)/shard_map/reduce_scatter | solution.py:29
  559.0 173.2 %reduce-scatter.21.cloned.1.call-start = ((), (), s32[]{:S(2)}) async-start(), calls=%async_computation.22 | async-start | bytes 1114112 | tf_op jit(solution)/shard_map/reduce_scatter | solution.py:33
  662.9 217.0 %reduce-scatter.23.cloned.1.call-start = ((), (), s32[]{:S(2)}) async-start(), calls=%async_computation.23 | async-start | bytes 13369344 | tf_op jit(solution)/shard_map/reduce_scatter | solution.py:42
  787.7 0.8 copy-start.3
  787.7 0.9 copy-start.4
  787.7 0.9 copy-start.5
  787.7 0.9 copy-start.6
  787.7 92.2 %copy-start = (f32[12,256,64]{1,2,0:T(8,128)S(1)}, f32[12,256,64]{1,2,0:T(8,128)}, u32[]{:S(2)}) copy-start(f32[12,256,64]{1,2,0:T(8,128)} %param.9) | copy-start | bytes 2359300
Sparse Core Ops, SparseCore 0:
  43.8 69.1 reduce-scatter.8
  146.1 69.1 reduce-scatter.10
  249.2 69.0 reduce-scatter.12
  352.6 69.0 reduce-scatter.14
  455.5 69.1 reduce-scatter.16
  559.1 69.0 reduce-scatter.18
  663.0 69.0 reduce-scatter.20
  787.8 92.0 reduce-scatter.22
where the time goes:
time: 890 us; the launch traced here: 889 us
  waiting for transfers between devices  580 us (65%)
  blocking collectives  233 us (26%)
  matrix products  42 us (5%)
  between operations  14.3 us (2%)
  starting transfers between devices  9.62 us (1%)
    reduce_scatter x4, waiting for transfers between devices, shards(): lax.psum_scatter(product(inverse_blocks[j], reduced_spread), 'col', scatt...  277 us
    reduce_scatter x3, waiting for transfers between devices, shards(): lax.psum_scatter(partial_value, 'col', scatter_dimension=1, tiled=True)  208 us
    all_gather x8, blocking collectives, remap(): full = lax.all_gather(block, 'row', axis=0, tiled=True)  124 us
    all_to_all x6, blocking collectives, remap(): lax.all_to_all(full, 'col', split_axis=0, concat_axis=1, tiled=True)  95.1 us
    reduce_scatter x1, waiting for transfers between devices, shards(): lax.psum_scatter(jnp.einsum('tajb,jbm->mta', trailing_factor, stacked, pr...  76.6 us
    dot_general x1, matrix products, shards(): jnp.einsum('tajb,jbm->mta', trailing_factor, stacked, precision=lax.Preci...  24.4 us
    all_to_all x2, waiting for transfers between devices, remap(): lax.all_to_all(full, 'col', split_axis=0, concat_axis=1, tiled=True)  18.7 us
  transfers between devices with their start and end apart: 10, of which 10 were waited for; matrix products, arithmetic and copies ran while one was open for 0% of the time, Pallas kernels for 0%

commit v1 on v0

v1 whole, which is shorter than its diff:
```python
import jax
import jax.numpy as jnp
import numpy as np
from jax import lax
from jax.experimental import pallas as pl
from jax.experimental.pallas import tpu as pltpu
from jax.sharding import Mesh, PartitionSpec as P

ROW, COL = ("x", "core"), ("z", "y")
ALL = ROW + COL
NT = (((1,), (1,)), ((), ()))
RING = {s: [(i, (i + s) % 4) for i in range(4)] for s in (1, 2, 3)}
SWAP = [(0, 1), (1, 0)]
LOCAL = pl.BlockSpec(memory_space=pltpu.VMEM)


def both_cores(pieces):
    return pieces + [lax.ppermute(piece, "core", SWAP) for piece in pieces]


def row_gather(block):
    return both_cores([block] + [lax.ppermute(block, "x", RING[s]) for s in (1, 2, 3)])


def turned(s):
    pairs = []
    for a in range(4):
        for core in range(2):
            for b in range(4):
                for y in range(4):
                    source = ((a * 2 + core) * 4 + b) * 4 + y
                    target = ((((b - s) % 4) * 2 + core) * 4 + a) * 4 + y
                    pairs.append((source, target))
    return pairs


def slab_gather(block):
    return both_cores([lax.ppermute(block, ALL, turned(s)) for s in range(4)])


def y_gather(blocks):
    return [blocks] + [lax.ppermute(blocks, "y", RING[s]) for s in (1, 2, 3)]


def z_sum(parts):
    total = parts[0]
    for t in (1, 2, 3):
        total = total + lax.ppermute(parts[t], "z", RING[t])
    return total


def split(v):
    high = v.astype(jnp.bfloat16)
    return high, (v - high.astype(jnp.float32)).astype(jnp.bfloat16)


def three(v, doubled):
    high, low = split(v)
    return jnp.concatenate([high, high, low] if doubled else [high, low, high], axis=1)


def local_call(kernel, operands, shapes, scratch, name, flops):
    nbytes = 4 * sum(int(np.prod(v.shape)) for v in operands)
    return pl.pallas_call(
        kernel,
        out_shape=shapes,
        in_specs=[LOCAL] * len(operands),
        out_specs=jax.tree.map(lambda _: LOCAL, shapes),
        scratch_shapes=scratch,
        cost_estimate=pl.CostEstimate(flops=flops, bytes_accessed=nbytes, transcendentals=0),
        name=name,
    )(*operands)


def slab_product(factor, indices, gathered):
    n = len(indices)

    def kernel(*refs):
        f, pieces, out, (chunks, blocks) = refs[:4], refs[4:12], refs[12:16], refs[16:]
        x, z, y, core = (lax.axis_index(name) for name in ("x", "z", "y", "core"))
        for side, which in ((0, core), (4, 1 - core)):
            for h in range(2):
                for s in range(4):
                    chunks[which * 2 + h, s * 64 : s * 64 + 64] = pieces[side + s][:, h * 128 : h * 128 + 128]
        for at, index in enumerate(indices):
            value = jnp.zeros((256, 256), jnp.float32)
            for k in (0, 2):
                rows = jnp.concatenate([chunks[lax.rem(y - k - h + 4, 4)] for h in (0, 1)], axis=1)
                block = jnp.concatenate([f[k][index], f[k + 1][index]], axis=1)
                value += lax.dot_general(three(rows, False), three(block, True), NT, preferred_element_type=jnp.float32)
            blocks[at] = value.reshape(4, 64, 256)
        for t in range(4):
            for at in range(n):
                out[t][at] = blocks[at, lax.rem(t + z - x + 4, 4)]

    return local_call(
        kernel,
        [*factor, *gathered],
        [jax.ShapeDtypeStruct((n, 64, 256), jnp.float32)] * 4,
        [pltpu.VMEM((4, 256, 128), jnp.float32), pltpu.VMEM((n, 4, 64, 256), jnp.float32)],
        "slab_product",
        n * 2 * 3 * 256 * 256 * 512,
    )


def by_row(pieces):
    x, core = lax.axis_index("x"), lax.axis_index("core")
    for side, which in ((0, core), (4, 1 - core)):
        for k in range(4):
            yield lax.rem(x - k + 4, 4) * 2 + which, pieces[side + k]


def full_product(base, terms):
    n = len(terms)

    def kernel(*refs):
        scratch = refs[len(refs) - n :]
        out = refs[len(refs) - n - 1]
        both = jnp.zeros((128, 256), jnp.float32)
        cross = jnp.zeros((64, 256), jnp.float32)
        for term, chunks in enumerate(scratch):
            f, pieces = refs[9 * term], refs[9 * term + 1 : 9 * term + 9]
            for row, piece in by_row(pieces):
                chunks[row, :64], chunks[row, 64:] = split(piece[...])
            for q in range(8):
                high, low = split(jnp.concatenate([f[2 * q], f[2 * q + 1]], axis=1))
                rows = chunks[q]
                both += lax.dot_general(rows, high, NT, preferred_element_type=jnp.float32)
                cross += lax.dot_general(rows[:64], low, NT, preferred_element_type=jnp.float32)
        total = both[:64] + both[64:] + cross
        out[...] = total if base is None else refs[9 * n][...] - total

    operands = [v for block, gathered in terms for v in (block, *gathered)]
    return local_call(
        kernel,
        operands + ([] if base is None else [base]),
        jax.ShapeDtypeStruct((64, 256), jnp.float32),
        [pltpu.VMEM((8, 128, 256), jnp.bfloat16)] * n,
        "full_product",
        n * 2 * 3 * 64 * 256 * 2048,
    )


def spread_to(turn):
    return [(r * 16 + 2 * q + b, q * 16 + 2 * r + (b + turn) % 2) for r in range(8) for q in range(8) for b in range(2)]


def spread(blocks):
    n = blocks.shape[0]
    odd = lax.axis_index("y") % 2 == 1
    low, high = blocks[:, :, :128], blocks[:, :, 128:]
    same = lax.ppermute(jnp.where(odd, high, low), ALL, spread_to(0))
    cross = lax.ppermute(jnp.where(odd, low, high), ALL, spread_to(1))
    gathered = row_gather(jnp.concatenate([jnp.where(odd, cross, same), jnp.where(odd, same, cross)], axis=1))

    def kernel(*refs):
        out = refs[-1]
        for row, piece in by_row(refs[:8]):
            at = pl.ds(pl.multiple_of(row * 128, 128), 128)
            for j in range(n):
                one, two = split(piece[j])
                out[at, j * 128 : j * 128 + 128] = one
                out[at, (n + j) * 128 : (n + j + 1) * 128] = two

    return local_call(kernel, gathered, jax.ShapeDtypeStruct((1024, 2 * n * 128), jnp.bfloat16), [], "split_rows", 0)


def trailing_product(factor, early, last):
    def kernel(f, early, last, out, rows):
        @pl.when(pl.program_id(0) == 0)
        def _():
            for part, side in enumerate((0, 1, 0)):
                rows[:, part * 512 : part * 512 + 384] = early[:, side * 384 : side * 384 + 384]
                rows[:, part * 512 + 384 : part * 512 + 512] = last[:, side * 128 : side * 128 + 128]

        block = jnp.concatenate([f[0, pl.ds(j, 256, stride=4), :] for j in range(4)], axis=1)
        value = lax.dot_general(rows[...], three(block, True), NT, preferred_element_type=jnp.float32)
        out[:, 0] = value.reshape(16, 64, 256)

    return pl.pallas_call(
        kernel,
        grid=(12,),
        out_shape=jax.ShapeDtypeStruct((16, 12, 64, 256), jnp.float32),
        in_specs=[
            pl.BlockSpec((1, 1024, 128), lambda t: (t, 0, 0)),
            pl.BlockSpec((1024, 768), lambda t: (0, 0)),
            pl.BlockSpec((1024, 256), lambda t: (0, 0)),
        ],
        out_specs=pl.BlockSpec((16, 1, 64, 256), lambda t: (0, t, 0, 0)),
        scratch_shapes=[pltpu.VMEM((1024, 1536), jnp.bfloat16)],
        compiler_params=pltpu.CompilerParams(vmem_limit_bytes=56 * 1024 * 1024),
        cost_estimate=pl.CostEstimate(flops=2 * 3 * 1024 * 3072 * 512, bytes_accessed=20971520, transcendentals=0),
        name="trailing_product",
    )(factor, early, last)


def shards(panel, inverse_blocks, trailing_factor, columns, trailing_columns):
    columns_t = jnp.transpose(columns, (0, 2, 1))
    group = y_gather(jnp.concatenate([inverse_blocks[0:1], panel[1:2], panel[3:4]]))
    near = lax.all_gather(jnp.concatenate([panel[0:1], inverse_blocks[1:2], panel[2:3], inverse_blocks[2:3]]), COL, axis=0)
    far = lax.all_gather(jnp.concatenate([panel[4:6], inverse_blocks[3:4]]), COL, axis=0)

    first = z_sum(slab_product(group, (0,), slab_gather(columns_t[0])))[0]
    gathered = row_gather(first)
    later, gathered = lax.optimization_barrier((first, gathered))
    parts = slab_product(group, (1, 2), slab_gather(later))
    near, parts = lax.optimization_barrier((near, parts))
    bases = columns_t[2:4] - z_sum(parts)

    reduced = full_product(columns_t[1], [(near[:, 0], gathered)])
    second = full_product(None, [(near[:, 1], row_gather(reduced))])
    gathered_second = row_gather(second)
    reduced = full_product(bases[0], [(near[:, 2], gathered_second)])
    third = full_product(None, [(near[:, 3], row_gather(reduced))])
    gathered = row_gather(third)
    (first, second, third), gathered = lax.optimization_barrier(((first, second, third), gathered))
    early = spread(jnp.stack([first, second, third]))
    reduced = full_product(bases[1], [(far[:, 0], gathered_second), (far[:, 1], gathered)])
    fourth = full_product(None, [(far[:, 2], row_gather(reduced))])

    partial = trailing_product(trailing_factor.reshape(12, 1024, 128), early, spread(fourth[None]))
    updated = jnp.transpose(trailing_columns, (0, 2, 1)) - lax.psum_scatter(partial, COL, scatter_dimension=0)

    whitened_t = jnp.stack([first, second, third, fourth])
    local_squares = jnp.sum(whitened_t * whitened_t, axis=(0, 2))
    variance_drop = lax.psum(local_squares, ROW) / 8192
    return (jnp.transpose(whitened_t, (0, 2, 1)), jnp.transpose(updated, (0, 2, 1)), variance_drop)


def solution(mesh):
    mesh = Mesh(np.asarray(mesh.devices).reshape(4, 2, 4, 4), ("x", "core", "z", "y"))
    return jax.shard_map(
        shards,
        mesh=mesh,
        in_specs=(
            P(None, ROW, COL),
            P(None, ROW, COL),
            P(None, ROW, None, COL),
            P(None, ROW, COL),
            P(None, ROW, COL),
        ),
        out_specs=(P(None, ROW, COL), P(None, ROW, COL), P(COL)),
        check_vma=False,
    )
```

time: 890 us -> 353 us (0.40)
  waiting for transfers between devices: 580 us -> 117 us
  blocking collectives: 233 us -> 12 us
  starting transfers between devices: 9.62 us -> 128 us
  Pallas kernels: 0 us -> 48.5 us
  matrix products: 42 us -> 0 us
  local copies, waits for them, and re-layouts: 3.98 us -> 24.5 us
    reduce_scatter x8 -> x0, waiting for transfers between devices: 561 us -> none  [the longest x4 277 us: shards(): lax.psum_scatter(product(inverse_blocks[j], reduced_spread), 'col', scatt...]
    ppermute x0 -> x85, starting transfers between devices: none -> 128 us  [the longest x24 43.9 us: row_gather(): lax.ppermute(block, 'x', RING[s])]
    all_gather x8 -> x0, blocking collectives: 124 us -> none  [remap(): full = lax.all_gather(block, 'row', axis=0, tiled=True)]
    all_to_all x6 -> x0, blocking collectives: 95.1 us -> none  [remap(): lax.all_to_all(full, 'col', split_axis=0, concat_axis=1, tiled=True)]
    unnamed x8 -> x4, waiting for transfers between devices: 0.13 us -> 78 us
    pallas_call x0 -> x11, Pallas kernels: none -> 48.5 us  [the longest x10 31.1 us: local_call(): pl.pallas_call(kernel, out_shape=shapes, in_specs=[LOCAL] * len(operands)...]
    dot_general x11 -> x0, matrix products: 42 us -> none  [the longest x1 24.4 us: shards(): jnp.einsum('tajb,jbm->mta', trailing_factor, stacked, precision=lax.Preci...]
    ppermute x0 -> x85, waiting for transfers between devices: none -> 29.9 us  [the longest x24 11.7 us: row_gather(): lax.ppermute(block, 'x', RING[s])]
  transfers between devices with their start and end apart: 10 -> 88, of which waited for: 10 -> 28; matrix products, arithmetic and copies ran while one was open for 0% -> 5% of each run, Pallas kernels for 0% -> 7%
where the time goes in v1:
time: 353 us; the launch traced here: 352 us
  starting transfers between devices  128 us (36%)
  waiting for transfers between devices  117 us (33%)
  Pallas kernels  48.5 us (14%)
  local copies, waits for them, and re-layouts  24.5 us (7%)
  between operations  14.7 us (4%)
  blocking collectives  12 us (3%)
  other arithmetic  6.86 us (2%)
    unnamed x4, waiting for transfers between devices  78 us
    ppermute x24, starting transfers between devices, row_gather(): lax.ppermute(block, 'x', RING[s])  43.9 us
    ppermute x40, starting transfers between devices, both_cores(): return pieces + [lax.ppermute(piece, 'core', SWAP) for piece in pieces]  40.1 us
    pallas_call x10, Pallas kernels, local_call(): pl.pallas_call(kernel, out_shape=shapes, in_specs=[LOCAL] * len(operands)...  31.1 us
    ppermute x8, starting transfers between devices, slab_gather(): return both_cores([lax.ppermute(block, ALL, turned(s)) for s in range(4)])  19.5 us
    pallas_call x1, Pallas kernels, trailing_product(): pl.pallas_call(kernel, grid=(12,), out_shape=jax.ShapeDtypeStruct((16, 12...  17.5 us
    psum x1, blocking collectives, shards(): variance_drop = lax.psum(local_squares, ROW) / 8192  12 us
    ppermute x24, waiting for transfers between devices, row_gather(): lax.ppermute(block, 'x', RING[s])  11.7 us
  transfers between devices with their start and end apart: 88, of which 28 were waited for; matrix products, arithmetic and copies ran while one was open for 5% of the time, Pallas kernels for 7%

profile of v1, /device:TPU:1, one launch (start us, length us, event | category | flops | bytes accessed | tf_op | source)
XLA Modules:
  0.0 351.7 jit_solution(15036793253572958575)
XLA Ops:
  11.4 2.2 collective-permute-start
  13.5 2.6 collective-permute-start.1
  19.7 3.8 %collective-permute-done.6.refs_7_ = f32[64,256]{1,0:T(8,128)S(1)} collective-permute-done((f32[64,256]{1,0:T(8,128)S(1)}, f32[64,256]{1,0:T(8,128)S(1)}, u32[]{:S(2)}, u32[]{:S(2)}) %collective-permute-start.6) | collective-permute-done | bytes 65568 | tf_op jit(solution)/shard_map/ppermute | solution.py:38
  23.6 3.6 %collective-permute-start.4 = (f32[64,256]{1,0:T(8,128)S(1)}, f32[64,256]{1,0:T(8,128)S(1)}, u32[]{:S(2)}, u32[]{:S(2)}) collective-permute-start(f32[64,256]{1,0:T(8,128)S(1)} %get-tuple-element.87), channel_id=1, source_target_pairs={{0,96},{1,97},{2,98},{3,99},{4,0},{5,1},{6,2},{7,3},{8,32},{9,33},... | collective-permute-start | bytes 196616 | tf_op jit(solution)/shard_map/ppermute | solution.py:38
  27.2 6.0 %collective-permute-start.5 = (f32[64,256]{1,0:T(8,128)S(1)}, f32[64,256]{1,0:T(8,128)S(1)}, u32[]{:S(2)}, u32[]{:S(2)}) collective-permute-start(f32[64,256]{1,0:T(8,128)S(1)} %get-tuple-element.87), channel_id=1, source_target_pairs={{0,64},{1,65},{2,66},{3,67},{4,96},{5,97},{6,98},{7,99},{8,0},{9,1... | collective-permute-start | bytes 196616 | tf_op jit(solution)/shard_map/ppermute | solution.py:38
  33.2 3.3 collective-permute-start.10
  36.5 2.2 collective-permute-start.7
  42.5 2.6 slab_product.2
  46.7 2.1 collective-permute-start.12
  54.6 3.6 %collective-permute-start.15 = (f32[64,256]{1,0:T(8,128)S(1)}, f32[64,256]{1,0:T(8,128)S(1)}, u32[]{:S(2)}, u32[]{:S(2)}) collective-permute-start(f32[64,256]{1,0:T(8,128)S(1)} %add_bitcast_fusion.refs_1_), channel_id=1, source_target_pairs={{0,64},{32,96},{64,0},{96,32},{1,65},{33,97},{65,1},{97,33},{2,66}... | collective-permute-start | bytes 196616 | tf_op jit(solution)/shard_map/ppermute | solution.py:22
  58.2 6.2 %collective-permute-start.17 = (f32[64,256]{1,0:T(8,128)S(1)}, f32[64,256]{1,0:T(8,128)S(1)}, u32[]{:S(2)}, u32[]{:S(2)}) collective-permute-start(f32[64,256]{1,0:T(8,128)S(1)} %add_bitcast_fusion.refs_1_), channel_id=1, source_target_pairs={{0,16},{16,0},{1,17},{17,1},{2,18},{18,2},{3,19},{19,3},{4,20},{20... | collective-permute-start | bytes 196616 | tf_op jit(solution)/shard_map/ppermute | solution.py:18
  68.8 5.3 %collective-permute-start.22 = (f32[64,256]{1,0:T(8,128)S(1)}, f32[64,256]{1,0:T(8,128)S(1)}, u32[]{:S(2)}, u32[]{:S(2)}) collective-permute-start(f32[64,256]{1,0:T(8,128)S(1)} %add_bitcast_fusion.refs_1_), channel_id=1, source_target_pairs={{0,96},{1,97},{2,98},{3,99},{4,0},{5,1},{6,2},{7,3},{8,32},{9,33},... | collective-permute-start | bytes 196616 | tf_op jit(solution)/shard_map/ppermute | solution.py:38
  77.9 2.8 collective-permute-done.23.refs_6_
  80.6 3.2 collective-permute-start.27
  85.9 2.9 slab_product.3
  88.8 3.8 %all-gather.5.cloned.1.call-done = f32[64,256,128]{2,1,0:T(8,128)} async-done(((f32[4,256,128]{2,1,0:T(8,128)}), f32[64,256,128]{2,1,0:T(8,128)}) %all-gather.5.cloned.1.call-update) | async-done | bytes 8388624 | tf_op jit(solution)/shard_map/all_gather | solution.py:200
  92.6 7.1 %slice_bitcast_fusion.3 = (f32[16,256,128]{2,1,0:T(8,128)}, f32[16,256,128]{2,1,0:T(8,128)}, f32[16,256,128]{2,1,0:T(8,128)}, f32[16,256,128]{2,1,0:T(8,128)}) fusion(f32[16,4,256,128]{3,2,1,0:T(8,128)} %bitcast.49), kind=kLoop, calls=%fused_computation.3 | loop fusion | bytes 16777216 | tf_op jit(solution)/shard_map/squeeze | solution.py:213
  99.8 3.3 full_product.6.refs_1_
  104.2 2.4 collective-permute-start.30
  116.8 3.2 full_product.7.refs_1_
  122.3 1.9 collective-permute-start.38
  129.4 3.2 full_product.8.refs_1_
  134.1 2.5 collective-permute-start.47
  143.5 3.3 full_product.9.refs_10_
  146.7 2.6 collective-permute-start.54
  151.7 2.4 collective-permute-start.57
  154.7 5.3 %all-gather.7.cloned.1.call-done = f32[48,256,128]{2,1,0:T(8,128)} async-done(((f32[3,256,128]{2,1,0:T(8,128)}), f32[48,256,128]{2,1,0:T(8,128)}) %all-gather.7.cloned.1.call-update) | async-done | bytes 6291472 | tf_op jit(solution)/shard_map/all_gather | solution.py:201
  160.0 5.9 %slice_bitcast_fusion = (f32[16,256,128]{2,1,0:T(8,128)}, f32[16,256,128]{2,1,0:T(8,128)}, f32[16,256,128]{2,1,0:T(8,128)}) fusion(f32[16,3,256,128]{3,2,1,0:T(8,128)} %bitcast.50), kind=kLoop, calls=%fused_computation | loop fusion | bytes 12582912 | tf_op jit(solution)/shard_map/squeeze | solution.py:218
  166.1 3.1 collective-permute-start.67
  169.2 2.2 collective-permute-start.68
  171.4 4.7 %full_product.10.refs_1_ = f32[64,256]{1,0:T(8,128)} custom-call(f32[16,256,128]{2,1,0:T(8,128)} %get-tuple-element.74.refs_0_, f32[64,256]{1,0:T(8,128)} %full_product.7.refs_1_, f32[64,256]{1,0:T(8,128)} %copy-done.13, f32[64,256]{1,0:T(8,128)} %copy-done.14, f32[64,256]{1,0:T(8,128)} %copy-done.15, f32[64,256]{1,0:T(8,128)} %copy-done.16, ...), custom_call_target="tpu_custom_call" | custom-call | flops 402653184 | bytes 5308416 | tf_op jit(solution)/shard_map/full_product/pallas_call | solution.py:64
  176.1 2.9 collective-permute-start.60
  179.0 4.8 %collective-permute-start.61 = (f32[64,256]{1,0:T(8,128)}, f32[64,256]{1,0:T(8,128)S(1)}, u32[]{:S(2)}, u32[]{:S(2)}) collective-permute-start(f32[64,256]{1,0:T(8,128)} %full_product.10.refs_1_), channel_id=1, source_target_pairs={{0,64},{32,96},{64,0},{96,32},{1,65},{33,97},{65,1},{97,33},{2,66}... | collective-permute-start | bytes 196616 | tf_op jit(solution)/shard_map/ppermute | solution.py:22
  185.9 2.0 collective-permute-done.61.refs_3_
  190.4 3.2 full_product.11
  194.4 2.8 collective-permute-start.76
  197.3 2.5 collective-permute-start.77
  199.8 1.9 collective-permute-start.69
  201.8 5.4 %collective-permute-start.70 = (f32[3,128,128]{2,1,0:T(8,128)S(1)}, f32[3,128,128]{2,1,0:T(8,128)S(1)}, u32[]{:S(2)}, u32[]{:S(2)}) collective-permute-start(f32[3,128,128]{2,1,0:T(8,128)S(1)} %pad_maximum_fusion.5.refs_0_), channel_id=1, source_target_pairs={{0,64},{32,96},{64,0},{96,32},{1,65},{33,97},{65,1},{97,33},{2,66}... | collective-permute-start | bytes 589832 | tf_op jit(solution)/shard_map/ppermute | solution.py:22
  208.7 3.6 %collective-permute-start.79 = (f32[1,128,128]{2,1,0:T(8,128)S(1)}, f32[1,128,128]{2,1,0:T(8,128)S(1)}, u32[]{:S(2)}, u32[]{:S(2)}) collective-permute-start(f32[1,128,128]{2,1,0:T(8,128)S(1)} %pad_maximum_fusion.6.refs_0_), channel_id=1, source_target_pairs={{0,64},{32,96},{64,0},{96,32},{1,65},{33,97},{65,1},{97,33},{2,66}... | collective-permute-start | bytes 196616 | tf_op jit(solution)/shard_map/ppermute | solution.py:22
  212.3 5.8 %collective-permute-done.78.refs_1_ = f32[1,128,128]{2,1,0:T(8,128)S(1)} collective-permute-done((f32[1,128,128]{2,1,0:T(8,128)S(1)}, f32[1,128,128]{2,1,0:T(8,128)S(1)}, u32[]{:S(2)}, u32[]{:S(2)}) %collective-permute-start.78) | collective-permute-done | bytes 65568 | tf_op jit(solution)/shard_map/ppermute | solution.py:22
  219.2 2.0 collective-permute-done.80.refs_3_
  227.1 1.9 split_rows.3.last
  230.5 2.9 split_rows.2.early
  233.4 17.5 %trailing_product.1 = f32[16,12,64,256]{3,2,1,0:T(8,128)} custom-call(f32[12,1024,128]{2,1,0:T(8,128)} %bitcast.61, bf16[1024,768]{1,0:T(8,128)(2,1)} %split_rows.2.early, bf16[1024,256]{1,0:T(8,128)(2,1)} %split_rows.3.last), custom_call_target="tpu_custom_call" | custom-call | flops 9663676416 | bytes 20971520 | tf_op jit(solution)/shard_map/trailing_product/pallas_call | solution.py:180
  252.6 12.0 %psum.7 = f32[64]{0:T(128)S(1)} all-reduce(f32[64]{0:T(128)S(1)} %get-tuple-element.84), channel_id=1, replica_groups=mesh['x'=4,'core'=2,'z'=4,'y'=4] {'x','core'}, use_global_device_ids=true, to_apply=%region_2.3 | all-reduce | flops 64 | bytes 512 | tf_op jit(solution)/shard_map/psum | solution.py:226
  265.1 77.9 %reduce-scatter.4.cloned.1.call-done = f32[1,12,64,256]{3,2,1,0:T(8,128)} async-done(((f32[16,12,64,256]{3,2,1,0:T(8,128)}), f32[1,12,64,256]{3,2,1,0:T(8,128)}) %reduce-scatter.4.cloned.1.call-update) | async-done | bytes 786448
  343.0 2.1 fusion
  (348 shorter events, 76.8 us)
Async XLA Ops:
  7.2 85.4 %all-gather.5.cloned.1.call-start = ((), (), s32[]{:S(2)}) async-start(), calls=%async_computation.1 | async-start | bytes 8912896 | tf_op jit(solution)/shard_map/all_gather | solution.py:200
  10.4 149.6 %all-gather.7.cloned.1.call-start = ((), (), s32[]{:S(2)}) async-start(), calls=%async_computation.2 | async-start | bytes 6684672 | tf_op jit(solution)/shard_map/all_gather | solution.py:201
  11.3 331.8 %reduce-scatter.4.cloned.1.call-start = ((), (), s32[]{:S(2)}) async-start(), calls=%async_computation.3 | async-start | bytes 13369344
  11.4 29.5 %collective-permute-start = (f32[3,256,128]{2,1,0:T(8,128)S(1)}, f32[3,256,128]{2,1,0:T(8,128)S(1)}, u32[]{:S(2)}, u32[]{:S(2)}) collective-permute-start(f32[3,256,128]{2,1,0:T(8,128)S(1)} %pad_maximum_fusion.1.refs_0_), channel_id=1, source_target_pairs={{0,1},{1,2},{2,3},{3,0},{4,5},{5,6},{6,7},{7,4},{8,9},{9,10},{10,1... | collective-permute-start | bytes 1179656 | tf_op jit(solution)/shard_map/ppermute | solution.py:42
  13.5 27.3 %collective-permute-start.1 = (f32[3,256,128]{2,1,0:T(8,128)S(1)}, f32[3,256,128]{2,1,0:T(8,128)S(1)}, u32[]{:S(2)}, u32[]{:S(2)}) collective-permute-start(f32[3,256,128]{2,1,0:T(8,128)S(1)} %pad_maximum_fusion.1.refs_0_), channel_id=1, source_target_pairs={{0,2},{1,3},{2,0},{3,1},{4,6},{5,7},{6,4},{7,5},{8,10},{9,11},{10,... | collective-permute-start | bytes 1179656 | tf_op jit(solution)/shard_map/ppermute | solution.py:42
  16.2 24.7 %collective-permute-start.2 = (f32[3,256,128]{2,1,0:T(8,128)S(1)}, f32[3,256,128]{2,1,0:T(8,128)S(1)}, u32[]{:S(2)}, u32[]{:S(2)}) collective-permute-start(f32[3,256,128]{2,1,0:T(8,128)S(1)} %pad_maximum_fusion.1.refs_0_), channel_id=1, source_target_pairs={{0,3},{1,0},{2,1},{3,2},{4,7},{5,4},{6,5},{7,6},{8,11},{9,8},{10,9... | collective-permute-start | bytes 1179656 | tf_op jit(solution)/shard_map/ppermute | solution.py:42
  17.9 5.7 %collective-permute-start.6 = (f32[64,256]{1,0:T(8,128)S(1)}, f32[64,256]{1,0:T(8,128)S(1)}, u32[]{:S(2)}, u32[]{:S(2)}) collective-permute-start(f32[64,256]{1,0:T(8,128)S(1)} %get-tuple-element.87), channel_id=1, source_target_pairs={{0,32},{1,33},{2,34},{3,35},{4,64},{5,65},{6,66},{7,67},{8,96},{9,... | collective-permute-start | bytes 196616 | tf_op jit(solution)/shard_map/ppermute | solution.py:38
  19.1 8.1 %collective-permute-start.3 = (f32[64,256]{1,0:T(8,128)S(1)}, f32[64,256]{1,0:T(8,128)S(1)}, u32[]{:S(2)}, u32[]{:S(2)}) collective-permute-start(f32[64,256]{1,0:T(8,128)S(1)} %get-tuple-element.87), channel_id=1, source_target_pairs={{0,0},{1,1},{2,2},{3,3},{4,32},{5,33},{6,34},{7,35},{8,64},{9,65},... | collective-permute-start | bytes 196616 | tf_op jit(solution)/shard_map/ppermute | solution.py:38
  23.6 9.6 %collective-permute-start.4 = (f32[64,256]{1,0:T(8,128)S(1)}, f32[64,256]{1,0:T(8,128)S(1)}, u32[]{:S(2)}, u32[]{:S(2)}) collective-permute-start(f32[64,256]{1,0:T(8,128)S(1)} %get-tuple-element.87), channel_id=1, source_target_pairs={{0,96},{1,97},{2,98},{3,99},{4,0},{5,1},{6,2},{7,3},{8,32},{9,33},... | collective-permute-start | bytes 196616 | tf_op jit(solution)/shard_map/ppermute | solution.py:38
  27.2 9.3 %collective-permute-start.5 = (f32[64,256]{1,0:T(8,128)S(1)}, f32[64,256]{1,0:T(8,128)S(1)}, u32[]{:S(2)}, u32[]{:S(2)}) collective-permute-start(f32[64,256]{1,0:T(8,128)S(1)} %get-tuple-element.87), channel_id=1, source_target_pairs={{0,64},{1,65},{2,66},{3,67},{4,96},{5,97},{6,98},{7,99},{8,0},{9,1... | collective-permute-start | bytes 196616 | tf_op jit(solution)/shard_map/ppermute | solution.py:38
  53.3 11.1 %collective-permute-start.14 = (f32[64,256]{1,0:T(8,128)S(1)}, f32[64,256]{1,0:T(8,128)S(1)}, u32[]{:S(2)}, u32[]{:S(2)}) collective-permute-start(f32[64,256]{1,0:T(8,128)S(1)} %add_bitcast_fusion.refs_1_), channel_id=1, source_target_pairs={{0,32},{32,64},{64,96},{96,0},{1,33},{33,65},{65,97},{97,1},{2,34}... | collective-permute-start | bytes 196616 | tf_op jit(solution)/shard_map/ppermute | solution.py:22
  54.6 9.9 %collective-permute-start.15 = (f32[64,256]{1,0:T(8,128)S(1)}, f32[64,256]{1,0:T(8,128)S(1)}, u32[]{:S(2)}, u32[]{:S(2)}) collective-permute-start(f32[64,256]{1,0:T(8,128)S(1)} %add_bitcast_fusion.refs_1_), channel_id=1, source_target_pairs={{0,64},{32,96},{64,0},{96,32},{1,65},{33,97},{65,1},{97,33},{2,66}... | collective-permute-start | bytes 196616 | tf_op jit(solution)/shard_map/ppermute | solution.py:22
  58.1 7.8 %collective-permute-start.16 = (f32[64,256]{1,0:T(8,128)S(1)}, f32[64,256]{1,0:T(8,128)S(1)}, u32[]{:S(2)}, u32[]{:S(2)}) collective-permute-start(f32[64,256]{1,0:T(8,128)S(1)} %add_bitcast_fusion.refs_1_), channel_id=1, source_target_pairs={{0,96},{32,0},{64,32},{96,64},{1,97},{33,1},{65,33},{97,65},{2,98}... | collective-permute-start | bytes 196616 | tf_op jit(solution)/shard_map/ppermute | solution.py:22
  58.2 9.0 %collective-permute-start.17 = (f32[64,256]{1,0:T(8,128)S(1)}, f32[64,256]{1,0:T(8,128)S(1)}, u32[]{:S(2)}, u32[]{:S(2)}) collective-permute-start(f32[64,256]{1,0:T(8,128)S(1)} %add_bitcast_fusion.refs_1_), channel_id=1, source_target_pairs={{0,16},{16,0},{1,17},{17,1},{2,18},{18,2},{3,19},{19,3},{4,20},{20... | collective-permute-start | bytes 196616 | tf_op jit(solution)/shard_map/ppermute | solution.py:18
  68.1 8.0 %collective-permute-start.21 = (f32[64,256]{1,0:T(8,128)S(1)}, f32[64,256]{1,0:T(8,128)S(1)}, u32[]{:S(2)}, u32[]{:S(2)}) collective-permute-start(f32[64,256]{1,0:T(8,128)S(1)} %add_bitcast_fusion.refs_1_), channel_id=1, source_target_pairs={{0,0},{1,1},{2,2},{3,3},{4,32},{5,33},{6,34},{7,35},{8,64},{9,65},... | collective-permute-start | bytes 196616 | tf_op jit(solution)/shard_map/ppermute | solution.py:38
  68.8 8.6 %collective-permute-start.22 = (f32[64,256]{1,0:T(8,128)S(1)}, f32[64,256]{1,0:T(8,128)S(1)}, u32[]{:S(2)}, u32[]{:S(2)}) collective-permute-start(f32[64,256]{1,0:T(8,128)S(1)} %add_bitcast_fusion.refs_1_), channel_id=1, source_target_pairs={{0,96},{1,97},{2,98},{3,99},{4,0},{5,1},{6,2},{7,3},{8,32},{9,33},... | collective-permute-start | bytes 196616 | tf_op jit(solution)/shard_map/ppermute | solution.py:38
  74.1 6.5 %collective-permute-start.23 = (f32[64,256]{1,0:T(8,128)S(1)}, f32[64,256]{1,0:T(8,128)S(1)}, u32[]{:S(2)}, u32[]{:S(2)}) collective-permute-start(f32[64,256]{1,0:T(8,128)S(1)} %add_bitcast_fusion.refs_1_), channel_id=1, source_target_pairs={{0,64},{1,65},{2,66},{3,67},{4,96},{5,97},{6,98},{7,99},{8,0},{9,1... | collective-permute-start | bytes 196616 | tf_op jit(solution)/shard_map/ppermute | solution.py:38
  75.4 8.4 %collective-permute-start.24 = (f32[64,256]{1,0:T(8,128)S(1)}, f32[64,256]{1,0:T(8,128)S(1)}, u32[]{:S(2)}, u32[]{:S(2)}) collective-permute-start(f32[64,256]{1,0:T(8,128)S(1)} %add_bitcast_fusion.refs_1_), channel_id=1, source_target_pairs={{0,32},{1,33},{2,34},{3,35},{4,64},{5,65},{6,66},{7,67},{8,96},{9,... | collective-permute-start | bytes 196616 | tf_op jit(solution)/shard_map/ppermute | solution.py:38
  76.1 7.9 %collective-permute-start.25 = (f32[64,256]{1,0:T(8,128)S(1)}, f32[64,256]{1,0:T(8,128)S(1)}, u32[]{:S(2)}, u32[]{:S(2)}) collective-permute-start(f32[64,256]{1,0:T(8,128)S(1)} %collective-permute-done.21.refs_4_), channel_id=1, source_target_pairs={{0,16},{16,0},{1,17},{17,1},{2,18},{18,2},{3,19},{19,3},{4,20},{20... | collective-permute-start | bytes 196616 | tf_op jit(solution)/shard_map/ppermute | solution.py:18
  77.4 6.7 %collective-permute-start.26 = (f32[64,256]{1,0:T(8,128)S(1)}, f32[64,256]{1,0:T(8,128)S(1)}, u32[]{:S(2)}, u32[]{:S(2)}) collective-permute-start(f32[64,256]{1,0:T(8,128)S(1)} %collective-permute-done.22.refs_5_), channel_id=1, source_target_pairs={{0,16},{16,0},{1,17},{17,1},{2,18},{18,2},{3,19},{19,3},{4,20},{20... | collective-permute-start | bytes 196616 | tf_op jit(solution)/shard_map/ppermute | solution.py:18
  103.1 6.3 %collective-permute-start.29 = (f32[64,256]{1,0:T(8,128)}, f32[64,256]{1,0:T(8,128)S(1)}, u32[]{:S(2)}, u32[]{:S(2)}) collective-permute-start(f32[64,256]{1,0:T(8,128)} %full_product.6.refs_1_), channel_id=1, source_target_pairs={{0,32},{32,64},{64,96},{96,0},{1,33},{33,65},{65,97},{97,1},{2,34}... | collective-permute-start | bytes 196616 | tf_op jit(solution)/shard_map/ppermute | solution.py:22
  104.2 5.9 %collective-permute-start.30 = (f32[64,256]{1,0:T(8,128)}, f32[64,256]{1,0:T(8,128)S(1)}, u32[]{:S(2)}, u32[]{:S(2)}) collective-permute-start(f32[64,256]{1,0:T(8,128)} %full_product.6.refs_1_), channel_id=1, source_target_pairs={{0,64},{32,96},{64,0},{96,32},{1,65},{33,97},{65,1},{97,33},{2,66}... | collective-permute-start | bytes 196616 | tf_op jit(solution)/shard_map/ppermute | solution.py:22
  107.8 5.7 %collective-permute-start.32 = (f32[64,256]{1,0:T(8,128)}, f32[64,256]{1,0:T(8,128)S(1)}, u32[]{:S(2)}, u32[]{:S(2)}) collective-permute-start(f32[64,256]{1,0:T(8,128)} %full_product.6.refs_1_), channel_id=1, source_target_pairs={{0,16},{16,0},{1,17},{17,1},{2,18},{18,2},{3,19},{19,3},{4,20},{20... | collective-permute-start | bytes 196616 | tf_op jit(solution)/shard_map/ppermute | solution.py:18
  109.4 5.6 %collective-permute-start.33 = (f32[64,256]{1,0:T(8,128)S(1)}, f32[64,256]{1,0:T(8,128)S(1)}, u32[]{:S(2)}, u32[]{:S(2)}) collective-permute-start(f32[64,256]{1,0:T(8,128)S(1)} %collective-permute-done.29.refs_2_), channel_id=1, source_target_pairs={{0,16},{16,0},{1,17},{17,1},{2,18},{18,2},{3,19},{19,3},{4,20},{20... | collective-permute-start | bytes 196616 | tf_op jit(solution)/shard_map/ppermute | solution.py:18
  110.1 12.2 %collective-permute-start.43 = (f32[2,64,256]{2,1,0:T(8,128)S(1)}, f32[2,64,256]{2,1,0:T(8,128)S(1)}, u32[]{:S(2)}, u32[]{:S(2)}) collective-permute-start(f32[2,64,256]{2,1,0:T(8,128)S(1)} %copy-done.90), channel_id=1, source_target_pairs={{0,4},{4,8},{8,12},{12,0},{1,5},{5,9},{9,13},{13,1},{2,6},{6,10},{... | collective-permute-start | bytes 393224 | tf_op jit(solution)/shard_map/ppermute | solution.py:48
  110.1 14.0 %collective-permute-start.44 = (f32[2,64,256]{2,1,0:T(8,128)S(1)}, f32[2,64,256]{2,1,0:T(8,128)S(1)}, u32[]{:S(2)}, u32[]{:S(2)}) collective-permute-start(f32[2,64,256]{2,1,0:T(8,128)S(1)} %copy-done.89), channel_id=1, source_target_pairs={{0,8},{4,12},{8,0},{12,4},{1,9},{5,13},{9,1},{13,5},{2,10},{6,14},... | collective-permute-start | bytes 393224 | tf_op jit(solution)/shard_map/ppermute | solution.py:48
  111.7 13.5 %collective-permute-start.45 = (f32[2,64,256]{2,1,0:T(8,128)S(1)}, f32[2,64,256]{2,1,0:T(8,128)S(1)}, u32[]{:S(2)}, u32[]{:S(2)}) collective-permute-start(f32[2,64,256]{2,1,0:T(8,128)S(1)} %copy-done.88), channel_id=1, source_target_pairs={{0,12},{4,0},{8,4},{12,8},{1,13},{5,1},{9,5},{13,9},{2,14},{6,2},{... | collective-permute-start | bytes 393224 | tf_op jit(solution)/shard_map/ppermute | solution.py:48
  134.1 5.7 %collective-permute-start.47 = (f32[64,256]{1,0:T(8,128)}, f32[64,256]{1,0:T(8,128)S(1)}, u32[]{:S(2)}, u32[]{:S(2)}) collective-permute-start(f32[64,256]{1,0:T(8,128)} %full_product.8.refs_1_), channel_id=1, source_target_pairs={{0,64},{32,96},{64,0},{96,32},{1,65},{33,97},{65,1},{97,33},{2,66}... | collective-permute-start | bytes 196616 | tf_op jit(solution)/shard_map/ppermute | solution.py:22
  146.7 7.3 %collective-permute-start.54 = (f32[64,256]{1,0:T(8,128)}, f32[64,256]{1,0:T(8,128)S(1)}, u32[]{:S(2)}, u32[]{:S(2)}) collective-permute-start(f32[64,256]{1,0:T(8,128)} %full_product.9.refs_10_), channel_id=1, source_target_pairs={{0,64},{32,96},{64,0},{96,32},{1,65},{33,97},{65,1},{97,33},{2,66}... | collective-permute-start | bytes 196616 | tf_op jit(solution)/shard_map/ppermute | solution.py:22
  150.3 15.6 %collective-permute-start.56 = (f32[64,256]{1,0:T(8,128)}, f32[64,256]{1,0:T(8,128)S(1)}, u32[]{:S(2)}, u32[]{:S(2)}) collective-permute-start(f32[64,256]{1,0:T(8,128)} %full_product.9.refs_10_), channel_id=1, source_target_pairs={{0,16},{16,0},{1,17},{17,1},{2,18},{18,2},{3,19},{19,3},{4,20},{20... | collective-permute-start | bytes 196616 | tf_op jit(solution)/shard_map/ppermute | solution.py:18
  151.7 14.3 %collective-permute-start.57 = (f32[64,256]{1,0:T(8,128)S(1)}, f32[64,256]{1,0:T(8,128)S(1)}, u32[]{:S(2)}, u32[]{:S(2)}) collective-permute-start(f32[64,256]{1,0:T(8,128)S(1)} %collective-permute-done.53.refs_11_), channel_id=1, source_target_pairs={{0,16},{16,0},{1,17},{17,1},{2,18},{18,2},{3,19},{19,3},{4,20},{20... | collective-permute-start | bytes 196616 | tf_op jit(solution)/shard_map/ppermute | solution.py:18
  154.1 11.9 %collective-permute-start.58 = (f32[64,256]{1,0:T(8,128)S(1)}, f32[64,256]{1,0:T(8,128)S(1)}, u32[]{:S(2)}, u32[]{:S(2)}) collective-permute-start(f32[64,256]{1,0:T(8,128)S(1)} %collective-permute-done.54.refs_12_), channel_id=1, source_target_pairs={{0,16},{16,0},{1,17},{17,1},{2,18},{18,2},{3,19},{19,3},{4,20},{20... | collective-permute-start | bytes 196616 | tf_op jit(solution)/shard_map/ppermute | solution.py:18
  154.2 11.8 %collective-permute-start.59 = (f32[64,256]{1,0:T(8,128)S(1)}, f32[64,256]{1,0:T(8,128)S(1)}, u32[]{:S(2)}, u32[]{:S(2)}) collective-permute-start(f32[64,256]{1,0:T(8,128)S(1)} %collective-permute-done.55.refs_13_), channel_id=1, source_target_pairs={{0,16},{16,0},{1,17},{17,1},{2,18},{18,2},{3,19},{19,3},{4,20},{20... | collective-permute-start | bytes 196616 | tf_op jit(solution)/shard_map/ppermute | solution.py:18
  166.1 22.5 %collective-permute-start.67 = (f32[3,64,128]{2,1,0:T(8,128)S(1)}, f32[3,64,128]{2,1,0:T(8,128)S(1)}, u32[]{:S(2)}, u32[]{:S(2)}) collective-permute-start(f32[3,64,128]{2,1,0:T(8,128)S(1)} %get-tuple-element.90), channel_id=1, source_target_pairs={{0,1},{1,0},{2,17},{3,16},{4,33},{5,32},{6,49},{7,48},{8,65},{9,64... | collective-permute-start | bytes 294920 | tf_op jit(solution)/shard_map/ppermute | solution.py:153
  169.2 19.7 %collective-permute-start.68 = (f32[3,64,128]{2,1,0:T(8,128)S(1)}, f32[3,64,128]{2,1,0:T(8,128)S(1)}, u32[]{:S(2)}, u32[]{:S(2)}) collective-permute-start(f32[3,64,128]{2,1,0:T(8,128)S(1)} %get-tuple-element.91), channel_id=1, source_target_pairs={{0,0},{1,1},{2,16},{3,17},{4,32},{5,33},{6,48},{7,49},{8,64},{9,65... | collective-permute-start | bytes 294920 | tf_op jit(solution)/shard_map/ppermute | solution.py:152
  176.1 9.5 %collective-permute-start.60 = (f32[64,256]{1,0:T(8,128)}, f32[64,256]{1,0:T(8,128)S(1)}, u32[]{:S(2)}, u32[]{:S(2)}) collective-permute-start(f32[64,256]{1,0:T(8,128)} %full_product.10.refs_1_), channel_id=1, source_target_pairs={{0,32},{32,64},{64,96},{96,0},{1,33},{33,65},{65,97},{97,1},{2,34}... | collective-permute-start | bytes 196616 | tf_op jit(solution)/shard_map/ppermute | solution.py:22
  179.0 8.9 %collective-permute-start.61 = (f32[64,256]{1,0:T(8,128)}, f32[64,256]{1,0:T(8,128)S(1)}, u32[]{:S(2)}, u32[]{:S(2)}) collective-permute-start(f32[64,256]{1,0:T(8,128)} %full_product.10.refs_1_), channel_id=1, source_target_pairs={{0,64},{32,96},{64,0},{96,32},{1,65},{33,97},{65,1},{97,33},{2,66}... | collective-permute-start | bytes 196616 | tf_op jit(solution)/shard_map/ppermute | solution.py:22
  194.4 14.1 %collective-permute-start.76 = (f32[1,64,128]{2,1,0:T(8,128)S(1)}, f32[1,64,128]{2,1,0:T(8,128)S(1)}, u32[]{:S(2)}, u32[]{:S(2)}) collective-permute-start(f32[1,64,128]{2,1,0:T(8,128)S(1)} %get-tuple-element.96), channel_id=1, source_target_pairs={{0,1},{1,0},{2,17},{3,16},{4,33},{5,32},{6,49},{7,48},{8,65},{9,64... | collective-permute-start | bytes 98312 | tf_op jit(solution)/shard_map/ppermute | solution.py:153
  197.3 11.3 %collective-permute-start.77 = (f32[1,64,128]{2,1,0:T(8,128)S(1)}, f32[1,64,128]{2,1,0:T(8,128)S(1)}, u32[]{:S(2)}, u32[]{:S(2)}) collective-permute-start(f32[1,64,128]{2,1,0:T(8,128)S(1)} %get-tuple-element.97), channel_id=1, source_target_pairs={{0,0},{1,1},{2,16},{3,17},{4,32},{5,33},{6,48},{7,49},{8,64},{9,65... | collective-permute-start | bytes 98312 | tf_op jit(solution)/shard_map/ppermute | solution.py:152
  199.8 23.0 %collective-permute-start.69 = (f32[3,128,128]{2,1,0:T(8,128)S(1)}, f32[3,128,128]{2,1,0:T(8,128)S(1)}, u32[]{:S(2)}, u32[]{:S(2)}) collective-permute-start(f32[3,128,128]{2,1,0:T(8,128)S(1)} %pad_maximum_fusion.5.refs_0_), channel_id=1, source_target_pairs={{0,32},{32,64},{64,96},{96,0},{1,33},{33,65},{65,97},{97,1},{2,34}... | collective-permute-start | bytes 589832 | tf_op jit(solution)/shard_map/ppermute | solution.py:22
  201.8 21.5 %collective-permute-start.70 = (f32[3,128,128]{2,1,0:T(8,128)S(1)}, f32[3,128,128]{2,1,0:T(8,128)S(1)}, u32[]{:S(2)}, u32[]{:S(2)}) collective-permute-start(f32[3,128,128]{2,1,0:T(8,128)S(1)} %pad_maximum_fusion.5.refs_0_), channel_id=1, source_target_pairs={{0,64},{32,96},{64,0},{96,32},{1,65},{33,97},{65,1},{97,33},{2,66}... | collective-permute-start | bytes 589832 | tf_op jit(solution)/shard_map/ppermute | solution.py:22
  207.1 16.3 %collective-permute-start.71 = (f32[3,128,128]{2,1,0:T(8,128)S(1)}, f32[3,128,128]{2,1,0:T(8,128)S(1)}, u32[]{:S(2)}, u32[]{:S(2)}) collective-permute-start(f32[3,128,128]{2,1,0:T(8,128)S(1)} %pad_maximum_fusion.5.refs_0_), channel_id=1, source_target_pairs={{0,96},{32,0},{64,32},{96,64},{1,97},{33,1},{65,33},{97,65},{2,98}... | collective-permute-start | bytes 589832 | tf_op jit(solution)/shard_map/ppermute | solution.py:22
  208.6 9.5 %collective-permute-start.78 = (f32[1,128,128]{2,1,0:T(8,128)S(1)}, f32[1,128,128]{2,1,0:T(8,128)S(1)}, u32[]{:S(2)}, u32[]{:S(2)}) collective-permute-start(f32[1,128,128]{2,1,0:T(8,128)S(1)} %pad_maximum_fusion.6.refs_0_), channel_id=1, source_target_pairs={{0,32},{32,64},{64,96},{96,0},{1,33},{33,65},{65,97},{97,1},{2,34}... | collective-permute-start | bytes 196616 | tf_op jit(solution)/shard_map/ppermute | solution.py:22
  208.7 10.2 %collective-permute-start.79 = (f32[1,128,128]{2,1,0:T(8,128)S(1)}, f32[1,128,128]{2,1,0:T(8,128)S(1)}, u32[]{:S(2)}, u32[]{:S(2)}) collective-permute-start(f32[1,128,128]{2,1,0:T(8,128)S(1)} %pad_maximum_fusion.6.refs_0_), channel_id=1, source_target_pairs={{0,64},{32,96},{64,0},{96,32},{1,65},{33,97},{65,1},{97,33},{2,66}... | collective-permute-start | bytes 196616 | tf_op jit(solution)/shard_map/ppermute | solution.py:22
  222.8 6.3 %collective-permute-start.72 = (f32[3,128,128]{2,1,0:T(8,128)S(1)}, f32[3,128,128]{2,1,0:T(8,128)S(1)}, u32[]{:S(2)}, u32[]{:S(2)}) collective-permute-start(f32[3,128,128]{2,1,0:T(8,128)S(1)} %pad_maximum_fusion.5.refs_0_), channel_id=1, source_target_pairs={{0,16},{16,0},{1,17},{17,1},{2,18},{18,2},{3,19},{19,3},{4,20},{20... | collective-permute-start | bytes 589832 | tf_op jit(solution)/shard_map/ppermute | solution.py:18
  222.9 6.2 %collective-permute-start.73 = (f32[3,128,128]{2,1,0:T(8,128)S(1)}, f32[3,128,128]{2,1,0:T(8,128)S(1)}, u32[]{:S(2)}, u32[]{:S(2)}) collective-permute-start(f32[3,128,128]{2,1,0:T(8,128)S(1)} %collective-permute-done.69.refs_1_), channel_id=1, source_target_pairs={{0,16},{16,0},{1,17},{17,1},{2,18},{18,2},{3,19},{19,3},{4,20},{20... | collective-permute-start | bytes 589832 | tf_op jit(solution)/shard_map/ppermute | solution.py:18
  223.3 5.8 %collective-permute-start.74 = (f32[3,128,128]{2,1,0:T(8,128)S(1)}, f32[3,128,128]{2,1,0:T(8,128)S(1)}, u32[]{:S(2)}, u32[]{:S(2)}) collective-permute-start(f32[3,128,128]{2,1,0:T(8,128)S(1)} %collective-permute-done.70.refs_2_), channel_id=1, source_target_pairs={{0,16},{16,0},{1,17},{17,1},{2,18},{18,2},{3,19},{19,3},{4,20},{20... | collective-permute-start | bytes 589832 | tf_op jit(solution)/shard_map/ppermute | solution.py:18
  223.4 5.7 %collective-permute-start.75 = (f32[3,128,128]{2,1,0:T(8,128)S(1)}, f32[3,128,128]{2,1,0:T(8,128)S(1)}, u32[]{:S(2)}, u32[]{:S(2)}) collective-permute-start(f32[3,128,128]{2,1,0:T(8,128)S(1)} %collective-permute-done.71.refs_3_), channel_id=1, source_target_pairs={{0,16},{16,0},{1,17},{17,1},{2,18},{18,2},{3,19},{19,3},{4,20},{20... | collective-permute-start | bytes 589832 | tf_op jit(solution)/shard_map/ppermute | solution.py:18
  (132 other events, 909.9 us)
Sparse Core Ops, SparseCore 0:
  10.7 81.8 all-gather.4
  94.7 65.2 all-gather.6
  251.0 91.9 reduce-scatter.3

commit v2 on v1

--- a/solution.py
+++ b/solution.py
@@ -59,17 +59,40 @@
     return jnp.concatenate([high, high, low] if doubled else [high, low, high], axis=1)
 
 
+def in_vmem(shape, dtype=jnp.float32):
+    return pltpu.VMEM(shape, dtype)
+
+
 def local_call(kernel, operands, shapes, scratch, name, flops):
     nbytes = 4 * sum(int(np.prod(v.shape)) for v in operands)
     return pl.pallas_call(
         kernel,
         out_shape=shapes,
         in_specs=[LOCAL] * len(operands),
-        out_specs=jax.tree.map(lambda _: LOCAL, shapes),
+        out_specs=[LOCAL] * len(shapes) if isinstance(shapes, list) else LOCAL,
         scratch_shapes=scratch,
+        compiler_params=pltpu.CompilerParams(vmem_limit_bytes=16 * 1024 * 1024),
         cost_estimate=pl.CostEstimate(flops=flops, bytes_accessed=nbytes, transcendentals=0),
         name=name,
-    )(*operands)
+    )(*[pltpu.with_memory_space_constraint(v, pltpu.VMEM) for v in operands])
+
+
+def fetch(blocks, index):
+    def kernel(blocks_ref, out, sem):
+        copy = pltpu.make_async_copy(blocks_ref.at[:, index], out, sem)
+        copy.start()
+        copy.wait()
+
+    return pl.pallas_call(
+        kernel,
+        out_shape=in_vmem((16, 256, 128)),
+        in_specs=[pl.BlockSpec(memory_space=pl.ANY)],
+        out_specs=LOCAL,
+        scratch_shapes=[pltpu.SemaphoreType.DMA],
+        compiler_params=pltpu.CompilerParams(vmem_limit_bytes=8 * 1024 * 1024),
+        cost_estimate=pl.CostEstimate(flops=0, bytes_accessed=4194304, transcendentals=0),
+        name="fetch",
+    )(blocks)
 
 
 def slab_product(factor, indices, gathered):
@@ -96,7 +119,7 @@
     return local_call(
         kernel,
         [*factor, *gathered],
-        [jax.ShapeDtypeStruct((n, 64, 256), jnp.float32)] * 4,
+        [in_vmem((n, 64, 256))] * 4,
         [pltpu.VMEM((4, 256, 128), jnp.float32), pltpu.VMEM((n, 4, 64, 256), jnp.float32)],
         "slab_product",
         n * 2 * 3 * 256 * 256 * 512,
@@ -134,7 +157,7 @@
     return local_call(
         kernel,
         operands + ([] if base is None else [base]),
-        jax.ShapeDtypeStruct((64, 256), jnp.float32),
+        in_vmem((64, 256)),
         [pltpu.VMEM((8, 128, 256), jnp.bfloat16)] * n,
         "full_product",
         n * 2 * 3 * 64 * 256 * 2048,
@@ -162,7 +185,7 @@
                 out[at, j * 128 : j * 128 + 128] = one
                 out[at, (n + j) * 128 : (n + j + 1) * 128] = two
 
-    return local_call(kernel, gathered, jax.ShapeDtypeStruct((1024, 2 * n * 128), jnp.bfloat16), [], "split_rows", 0)
+    return local_call(kernel, gathered, in_vmem((1024, 2 * n * 128), jnp.bfloat16), [], "split_rows", 0)
 
 
 def trailing_product(factor, early, last):
@@ -196,27 +219,23 @@
 
 def shards(panel, inverse_blocks, trailing_factor, columns, trailing_columns):
     columns_t = jnp.transpose(columns, (0, 2, 1))
-    group = y_gather(jnp.concatenate([inverse_blocks[0:1], panel[1:2], panel[3:4]]))
-    near = lax.all_gather(jnp.concatenate([panel[0:1], inverse_blocks[1:2], panel[2:3], inverse_blocks[2:3]]), COL, axis=0)
+    group = y_gather(inverse_blocks[0:1])
+    below = y_gather(jnp.concatenate([panel[0:2], panel[3:4]]))
+    near = lax.all_gather(jnp.concatenate([inverse_blocks[1:2], panel[2:3], inverse_blocks[2:3]]), COL, axis=0)
     far = lax.all_gather(jnp.concatenate([panel[4:6], inverse_blocks[3:4]]), COL, axis=0)
 
     first = z_sum(slab_product(group, (0,), slab_gather(columns_t[0])))[0]
-    gathered = row_gather(first)
-    later, gathered = lax.optimization_barrier((first, gathered))
-    parts = slab_product(group, (1, 2), slab_gather(later))
-    near, parts = lax.optimization_barrier((near, parts))
-    bases = columns_t[2:4] - z_sum(parts)
-
-    reduced = full_product(columns_t[1], [(near[:, 0], gathered)])
-    second = full_product(None, [(near[:, 1], row_gather(reduced))])
+    bases = columns_t[1:4] - z_sum(slab_product(below, (0, 1, 2), slab_gather(first)))
+    second = full_product(None, [(fetch(near, 0), row_gather(bases[0]))])
     gathered_second = row_gather(second)
-    reduced = full_product(bases[0], [(near[:, 2], gathered_second)])
-    third = full_product(None, [(near[:, 3], row_gather(reduced))])
+    reduced = full_product(bases[1], [(fetch(near, 1), gathered_second)])
+    third = full_product(None, [(fetch(near, 2), row_gather(reduced))])
     gathered = row_gather(third)
     (first, second, third), gathered = lax.optimization_barrier(((first, second, third), gathered))
     early = spread(jnp.stack([first, second, third]))
-    reduced = full_product(bases[1], [(far[:, 0], gathered_second), (far[:, 1], gathered)])
-    fourth = full_product(None, [(far[:, 2], row_gather(reduced))])
+    early, far = lax.optimization_barrier((early, far))
+    reduced = full_product(bases[2], [(fetch(far, 0), gathered_second), (fetch(far, 1), gathered)])
+    fourth = full_product(None, [(fetch(far, 2), row_gather(reduced))])
 
     partial = trailing_product(trailing_factor.reshape(12, 1024, 128), early, spread(fourth[None]))
     updated = jnp.transpose(trailing_columns, (0, 2, 1)) - lax.psum_scatter(partial, COL, scatter_dimension=0)

time: 353 us -> 321 us (0.909)
  Pallas kernels: 48.5 us -> 24.9 us
  waiting for transfers between devices: 117 us -> 132 us
  local copies, waits for them, and re-layouts: 24.5 us -> 9.83 us
  starting transfers between devices: 128 us -> 122 us
    pallas_call x10 -> x9, Pallas kernels: 31.1 us -> 6.45 us  [local_call(): pl.pallas_call(kernel, out_shape=shapes, in_specs=[LOCAL] * len(operands)...]
    squeeze x4 -> x2, local copies, waits for them, and re-layouts: 14.3 us -> 0.02 us  [the longest x1 0.02 us: shards(): bases[2]]
    ppermute x24 -> x21, starting transfers between devices: 43.9 us -> 34.9 us  [row_gather(): lax.ppermute(block, 'x', RING[s])]
    ppermute x6, waiting for transfers between devices: 2.69 us -> 11.4 us  [z_sum(): total = total + lax.ppermute(parts[t], 'z', RING[t])]
    ppermute x2, waiting for transfers between devices: 0.01 us -> 8.49 us  [spread(): same = lax.ppermute(jnp.where(odd, high, low), ALL, spread_to(0))]
    ppermute x2, waiting for transfers between devices: 0.01 us -> 6.5 us  [spread(): cross = lax.ppermute(jnp.where(odd, low, high), ALL, spread_to(1))]
    all_gather x1, waiting for transfers between devices: 5.27 us -> 0.01 us  [shards(): lax.all_gather(jnp.concatenate([panel[4:6], inverse_blocks[3:4]]), COL, a...]
    ppermute x3 -> x6, waiting for transfers between devices: 0.01 us -> 3.9 us  [y_gather(): return [blocks] + [lax.ppermute(blocks, 'y', RING[s]) for s in (1, 2, 3)]]
  transfers between devices with their start and end apart: 88 -> 84, of which waited for: 28 -> 38; matrix products, arithmetic and copies ran while one was open for 5% -> 1% of each run, Pallas kernels for 7% -> 1%
where the time goes in v2:
time: 321 us
  waiting for transfers between devices  132 us (41%)
  starting transfers between devices  122 us (38%)
  Pallas kernels  24.9 us (8%)
  between operations  14.2 us (4%)
  blocking collectives  12.4 us (4%)
  local copies, waits for them, and re-layouts  9.83 us (3%)
  other arithmetic  5.23 us (2%)
    unnamed x4, waiting for transfers between devices  79.8 us
    ppermute x36, starting transfers between devices, both_cores(): return pieces + [lax.ppermute(piece, 'core', SWAP) for piece in pieces]  37.6 us
    ppermute x21, starting transfers between devices, row_gather(): lax.ppermute(block, 'x', RING[s])  34.9 us
    ppermute x8, starting transfers between devices, slab_gather(): return both_cores([lax.ppermute(block, ALL, turned(s)) for s in range(4)])  21.1 us
    pallas_call x1, Pallas kernels, trailing_product(): pl.pallas_call(kernel, grid=(12,), out_shape=jax.ShapeDtypeStruct((16, 12...  17.5 us
    psum x1, blocking collectives, shards(): variance_drop = lax.psum(local_squares, ROW) / 8192  12.4 us
    ppermute x6, waiting for transfers between devices, z_sum(): total = total + lax.ppermute(parts[t], 'z', RING[t])  11.4 us
    ppermute x6, starting transfers between devices, z_sum(): total = total + lax.ppermute(parts[t], 'z', RING[t])  11.1 us
  transfers between devices with their start and end apart: 84, of which 38 were waited for; matrix products, arithmetic and copies ran while one was open for 1% of the time, Pallas kernels for 1%

profile of v2, /device:TPU:1, one launch (start us, length us, event | category | flops | bytes accessed | tf_op | source)
XLA Modules:
  0.0 320.8 jit_solution(12067347056671463590)
XLA Ops:
  11.3 2.1 collective-permute-start.6
  15.4 2.6 collective-permute-start.1
  18.0 7.1 %collective-permute-start.4 = (f32[64,256]{1,0:T(8,128)S(1)}, f32[64,256]{1,0:T(8,128)S(1)}, u32[]{:S(2)}, u32[]{:S(2)}) collective-permute-start(f32[64,256]{1,0:T(8,128)S(1)} %slice_bitcast_fusion.3), channel_id=1, source_target_pairs={{0,96},{1,97},{2,98},{3,99},{4,0},{5,1},{6,2},{7,3},{8,32},{9,33},... | collective-permute-start | bytes 196616 | tf_op jit(solution)/shard_map/ppermute | solution.py:38
  25.1 1.6 collective-permute-start.5
  27.8 2.6 collective-permute-start.10
  30.8 1.9 collective-permute-start.7
  34.7 7.0 %collective-permute-start.12 = (f32[1,64,256]{2,1,0:T(8,128)S(1)}, f32[1,64,256]{2,1,0:T(8,128)S(1)}, u32[]{:S(2)}, u32[]{:S(2)}) collective-permute-start(f32[1,64,256]{2,1,0:T(8,128)S(1)} %get-tuple-element.26), channel_id=1, source_target_pairs={{0,8},{4,12},{8,0},{12,4},{1,9},{5,13},{9,1},{13,5},{2,10},{6,14},... | collective-permute-start | bytes 196616 | tf_op jit(solution)/shard_map/ppermute | solution.py:48
  41.8 1.5 collective-permute-start.15
  45.8 5.7 %collective-permute-start.18 = (f32[64,256]{1,0:T(8,128)S(1)}, f32[64,256]{1,0:T(8,128)S(1)}, u32[]{:S(2)}, u32[]{:S(2)}) collective-permute-start(f32[64,256]{1,0:T(8,128)S(1)} %add_bitcast_fusion), channel_id=1, source_target_pairs={{0,96},{1,97},{2,98},{3,99},{4,0},{5,1},{6,2},{7,3},{8,32},{9,33},... | collective-permute-start | bytes 196616 | tf_op jit(solution)/shard_map/ppermute | solution.py:38
  51.5 1.8 collective-permute-start.19
  53.3 1.5 collective-permute-start.20
  54.8 3.7 %collective-permute-done.19.refs_6_ = f32[64,256]{1,0:T(8,128)S(1)} collective-permute-done((f32[64,256]{1,0:T(8,128)S(1)}, f32[64,256]{1,0:T(8,128)S(1)}, u32[]{:S(2)}, u32[]{:S(2)}) %collective-permute-start.19) | collective-permute-done | bytes 65568 | tf_op jit(solution)/shard_map/ppermute | solution.py:38
  58.5 4.8 %collective-permute-start.21 = (f32[64,256]{1,0:T(8,128)S(1)}, f32[64,256]{1,0:T(8,128)S(1)}, u32[]{:S(2)}, u32[]{:S(2)}) collective-permute-start(f32[64,256]{1,0:T(8,128)S(1)} %collective-permute-done.17.refs_4_), channel_id=1, source_target_pairs={{0,16},{16,0},{1,17},{17,1},{2,18},{18,2},{3,19},{19,3},{4,20},{20... | collective-permute-start | bytes 196616 | tf_op jit(solution)/shard_map/ppermute | solution.py:18
  63.3 3.6 %collective-permute-start.22 = (f32[64,256]{1,0:T(8,128)S(1)}, f32[64,256]{1,0:T(8,128)S(1)}, u32[]{:S(2)}, u32[]{:S(2)}) collective-permute-start(f32[64,256]{1,0:T(8,128)S(1)} %collective-permute-done.18.refs_5_), channel_id=1, source_target_pairs={{0,16},{16,0},{1,17},{17,1},{2,18},{18,2},{3,19},{19,3},{4,20},{20... | collective-permute-start | bytes 196616 | tf_op jit(solution)/shard_map/ppermute | solution.py:18
  69.0 3.9 %collective-permute-done.16.refs_3_ = f32[3,256,128]{2,1,0:T(8,128)S(1)} collective-permute-done((f32[3,256,128]{2,1,0:T(8,128)S(1)}, f32[3,256,128]{2,1,0:T(8,128)S(1)}, u32[]{:S(2)}, u32[]{:S(2)}) %collective-permute-start.16) | collective-permute-done | bytes 393248 | tf_op jit(solution)/shard_map/ppermute | solution.py:42
  73.8 1.5 collective-permute-start.25
  75.4 2.5 collective-permute-start.27
  77.9 7.6 %collective-permute-done.25 = f32[3,64,256]{2,1,0:T(8,128)S(1)} collective-permute-done((f32[3,64,256]{2,1,0:T(8,128)S(1)}, f32[3,64,256]{2,1,0:T(8,128)S(1)}, u32[]{:S(2)}, u32[]{:S(2)}) %collective-permute-start.25) | collective-permute-done | bytes 196640 | tf_op jit(solution)/shard_map/ppermute | solution.py:48
  85.4 2.4 collective-permute-done.26
  89.0 2.4 collective-permute-start.30
  91.4 3.3 %collective-permute-start.31 = (f32[64,256]{1,0:T(8,128)S(1)}, f32[64,256]{1,0:T(8,128)S(1)}, u32[]{:S(2)}, u32[]{:S(2)}) collective-permute-start(f32[64,256]{1,0:T(8,128)S(1)} %get-tuple-element.57.refs_1_), channel_id=1, source_target_pairs={{0,16},{16,0},{1,17},{17,1},{2,18},{18,2},{3,19},{19,3},{4,20},{20... | collective-permute-start | bytes 196616 | tf_op jit(solution)/shard_map/ppermute | solution.py:18
  94.8 2.9 collective-permute-start.32
  98.6 2.8 copy-done.1
  103.5 2.2 collective-permute-start.36
  112.8 2.7 collective-permute-start.43
  117.2 1.8 collective-permute-start.46
  123.0 2.6 collective-permute-start.50
  127.1 1.6 collective-permute-start.53
  131.7 3.0 collective-permute-start.56
  134.7 1.9 collective-permute-start.57
  136.6 6.4 %collective-permute-done.56 = f32[3,64,128]{2,1,0:T(8,128)S(1)} collective-permute-done((f32[3,64,128]{2,1,0:T(8,128)S(1)}, f32[3,64,128]{2,1,0:T(8,128)S(1)}, u32[]{:S(2)}, u32[]{:S(2)}) %collective-permute-start.56) | collective-permute-done | bytes 98336 | tf_op jit(solution)/shard_map/ppermute | solution.py:176
  143.0 6.1 %collective-permute-done.57 = f32[3,64,128]{2,1,0:T(8,128)S(1)} collective-permute-done((f32[3,64,128]{2,1,0:T(8,128)S(1)}, f32[3,64,128]{2,1,0:T(8,128)S(1)}, u32[]{:S(2)}, u32[]{:S(2)}) %collective-permute-start.57) | collective-permute-done | bytes 98336 | tf_op jit(solution)/shard_map/ppermute | solution.py:175
  149.3 3.0 collective-permute-start.59
  153.3 3.4 %collective-permute-done.58.refs_1_ = f32[3,128,128]{2,1,0:T(8,128)S(1)} collective-permute-done((f32[3,128,128]{2,1,0:T(8,128)S(1)}, f32[3,128,128]{2,1,0:T(8,128)S(1)}, u32[]{:S(2)}, u32[]{:S(2)}) %collective-permute-start.58) | collective-permute-done | bytes 196640 | tf_op jit(solution)/shard_map/ppermute | solution.py:22
  156.7 3.2 collective-permute-done.59.refs_2_
  163.0 2.8 copy-done
  166.1 1.5 full_product.8.refs_1_
  169.0 1.5 collective-permute-start.66
  173.6 1.6 collective-permute-start.70
  177.6 4.2 %collective-permute-start.73 = (f32[1,64,128]{2,1,0:T(8,128)S(1)}, f32[1,64,128]{2,1,0:T(8,128)S(1)}, u32[]{:S(2)}, u32[]{:S(2)}) collective-permute-start(f32[1,64,128]{2,1,0:T(8,128)S(1)} %get-tuple-element.65), channel_id=1, source_target_pairs={{0,0},{1,1},{2,16},{3,17},{4,32},{5,33},{6,48},{7,49},{8,64},{9,65... | collective-permute-start | bytes 98312 | tf_op jit(solution)/shard_map/ppermute | solution.py:175
  182.0 2.3 collective-permute-done.73
  184.4 3.7 %collective-permute-start.74 = (f32[1,128,128]{2,1,0:T(8,128)S(1)}, f32[1,128,128]{2,1,0:T(8,128)S(1)}, u32[]{:S(2)}, u32[]{:S(2)}) collective-permute-start(f32[1,128,128]{2,1,0:T(8,128)S(1)} %pad_maximum_fusion.6.refs_0_), channel_id=1, source_target_pairs={{0,32},{32,64},{64,96},{96,0},{1,33},{33,65},{65,97},{97,1},{2,34}... | collective-permute-start | bytes 196616 | tf_op jit(solution)/shard_map/ppermute | solution.py:22
  188.1 7.5 %collective-permute-start.75 = (f32[1,128,128]{2,1,0:T(8,128)S(1)}, f32[1,128,128]{2,1,0:T(8,128)S(1)}, u32[]{:S(2)}, u32[]{:S(2)}) collective-permute-start(f32[1,128,128]{2,1,0:T(8,128)S(1)} %pad_maximum_fusion.6.refs_0_), channel_id=1, source_target_pairs={{0,64},{32,96},{64,0},{96,32},{1,65},{33,97},{65,1},{97,33},{2,66}... | collective-permute-start | bytes 196616 | tf_op jit(solution)/shard_map/ppermute | solution.py:22
  195.6 2.0 collective-permute-start.76
  201.1 17.5 %trailing_product.1 = f32[16,12,64,256]{3,2,1,0:T(8,128)} custom-call(f32[12,1024,128]{2,1,0:T(8,128)} %bitcast.47, bf16[1024,768]{1,0:T(8,128)(2,1)} %copy-done.3, bf16[1024,256]{1,0:T(8,128)(2,1)} %copy-done.4), custom_call_target="tpu_custom_call" | custom-call | flops 9663676416 | bytes 20971520 | tf_op jit(solution)/shard_map/trailing_product/pallas_call | solution.py:203
  219.5 12.4 %psum.7 = f32[64]{0:T(128)S(1)} all-reduce(f32[64]{0:T(128)S(1)} %get-tuple-element.53), channel_id=1, replica_groups=mesh['x'=4,'core'=2,'z'=4,'y'=4] {'x','core'}, use_global_device_ids=true, to_apply=%region_2.3 | all-reduce | flops 64 | bytes 512 | tf_op jit(solution)/shard_map/psum | solution.py:245
  232.4 79.7 %reduce-scatter.4.cloned.1.call-done = f32[1,12,64,256]{3,2,1,0:T(8,128)} async-done(((f32[16,12,64,256]{3,2,1,0:T(8,128)}), f32[1,12,64,256]{3,2,1,0:T(8,128)}) %reduce-scatter.4.cloned.1.call-update) | async-done | bytes 786448
  312.1 2.1 fusion
  (181 shorter events, 52.8 us)
Async XLA Ops:
  7.2 91.4 %all-gather.5.cloned.1.call-start = ((), (), s32[]{:S(2)}) async-start(), calls=%async_computation.1 | async-start | bytes 6684672 | tf_op jit(solution)/shard_map/all_gather | solution.py:224
  10.3 152.7 %all-gather.7.cloned.1.call-start = ((), (), s32[]{:S(2)}) async-start(), calls=%async_computation.2 | async-start | bytes 6684672 | tf_op jit(solution)/shard_map/all_gather | solution.py:225
  11.2 300.9 %reduce-scatter.4.cloned.1.call-start = ((), (), s32[]{:S(2)}) async-start(), calls=%async_computation.3 | async-start | bytes 13369344
  11.3 13.9 %collective-permute-start.6 = (f32[64,256]{1,0:T(8,128)S(1)}, f32[64,256]{1,0:T(8,128)S(1)}, u32[]{:S(2)}, u32[]{:S(2)}) collective-permute-start(f32[64,256]{1,0:T(8,128)S(1)} %slice_bitcast_fusion.3), channel_id=1, source_target_pairs={{0,32},{1,33},{2,34},{3,35},{4,64},{5,65},{6,66},{7,67},{8,96},{9,... | collective-permute-start | bytes 196616 | tf_op jit(solution)/shard_map/ppermute | solution.py:38
  13.4 13.3 %collective-permute-start.3 = (f32[64,256]{1,0:T(8,128)S(1)}, f32[64,256]{1,0:T(8,128)S(1)}, u32[]{:S(2)}, u32[]{:S(2)}) collective-permute-start(f32[64,256]{1,0:T(8,128)S(1)} %slice_bitcast_fusion.3), channel_id=1, source_target_pairs={{0,0},{1,1},{2,2},{3,3},{4,32},{5,33},{6,34},{7,35},{8,64},{9,65},... | collective-permute-start | bytes 196616 | tf_op jit(solution)/shard_map/ppermute | solution.py:38
  14.0 18.7 %collective-permute-start = (f32[1,256,128]{2,1,0:T(8,128)S(1)}, f32[1,256,128]{2,1,0:T(8,128)S(1)}, u32[]{:S(2)}, u32[]{:S(2)}) collective-permute-start(f32[1,256,128]{2,1,0:T(8,128)S(1)} %get-tuple-element.51.refs_0_), channel_id=1, source_target_pairs={{0,1},{1,2},{2,3},{3,0},{4,5},{5,6},{6,7},{7,4},{8,9},{9,10},{10,1... | collective-permute-start | bytes 393224 | tf_op jit(solution)/shard_map/ppermute | solution.py:42
  15.4 17.3 %collective-permute-start.1 = (f32[1,256,128]{2,1,0:T(8,128)S(1)}, f32[1,256,128]{2,1,0:T(8,128)S(1)}, u32[]{:S(2)}, u32[]{:S(2)}) collective-permute-start(f32[1,256,128]{2,1,0:T(8,128)S(1)} %get-tuple-element.51.refs_0_), channel_id=1, source_target_pairs={{0,2},{1,3},{2,0},{3,1},{4,6},{5,7},{6,4},{7,5},{8,10},{9,11},{10,... | collective-permute-start | bytes 393224 | tf_op jit(solution)/shard_map/ppermute | solution.py:42
  18.0 9.8 %collective-permute-start.4 = (f32[64,256]{1,0:T(8,128)S(1)}, f32[64,256]{1,0:T(8,128)S(1)}, u32[]{:S(2)}, u32[]{:S(2)}) collective-permute-start(f32[64,256]{1,0:T(8,128)S(1)} %slice_bitcast_fusion.3), channel_id=1, source_target_pairs={{0,96},{1,97},{2,98},{3,99},{4,0},{5,1},{6,2},{7,3},{8,32},{9,33},... | collective-permute-start | bytes 196616 | tf_op jit(solution)/shard_map/ppermute | solution.py:38
  25.1 5.7 %collective-permute-start.5 = (f32[64,256]{1,0:T(8,128)S(1)}, f32[64,256]{1,0:T(8,128)S(1)}, u32[]{:S(2)}, u32[]{:S(2)}) collective-permute-start(f32[64,256]{1,0:T(8,128)S(1)} %slice_bitcast_fusion.3), channel_id=1, source_target_pairs={{0,64},{1,65},{2,66},{3,67},{4,96},{5,97},{6,98},{7,99},{8,0},{9,1... | collective-permute-start | bytes 196616 | tf_op jit(solution)/shard_map/ppermute | solution.py:38
  26.7 6.5 %collective-permute-start.2 = (f32[1,256,128]{2,1,0:T(8,128)S(1)}, f32[1,256,128]{2,1,0:T(8,128)S(1)}, u32[]{:S(2)}, u32[]{:S(2)}) collective-permute-start(f32[1,256,128]{2,1,0:T(8,128)S(1)} %get-tuple-element.51.refs_0_), channel_id=1, source_target_pairs={{0,3},{1,0},{2,1},{3,2},{4,7},{5,4},{6,5},{7,6},{8,11},{9,8},{10,9... | collective-permute-start | bytes 393224 | tf_op jit(solution)/shard_map/ppermute | solution.py:42
  27.8 5.5 %collective-permute-start.10 = (f32[64,256]{1,0:T(8,128)S(1)}, f32[64,256]{1,0:T(8,128)S(1)}, u32[]{:S(2)}, u32[]{:S(2)}) collective-permute-start(f32[64,256]{1,0:T(8,128)S(1)} %collective-permute-done.6.refs_7_), channel_id=1, source_target_pairs={{0,16},{16,0},{1,17},{17,1},{2,18},{18,2},{3,19},{19,3},{4,20},{20... | collective-permute-start | bytes 196616 | tf_op jit(solution)/shard_map/ppermute | solution.py:18
  34.6 8.8 %collective-permute-start.11 = (f32[1,64,256]{2,1,0:T(8,128)S(1)}, f32[1,64,256]{2,1,0:T(8,128)S(1)}, u32[]{:S(2)}, u32[]{:S(2)}) collective-permute-start(f32[1,64,256]{2,1,0:T(8,128)S(1)} %get-tuple-element.25), channel_id=1, source_target_pairs={{0,4},{4,8},{8,12},{12,0},{1,5},{5,9},{9,13},{13,1},{2,6},{6,10},{... | collective-permute-start | bytes 196616 | tf_op jit(solution)/shard_map/ppermute | solution.py:48
  34.7 10.0 %collective-permute-start.12 = (f32[1,64,256]{2,1,0:T(8,128)S(1)}, f32[1,64,256]{2,1,0:T(8,128)S(1)}, u32[]{:S(2)}, u32[]{:S(2)}) collective-permute-start(f32[1,64,256]{2,1,0:T(8,128)S(1)} %get-tuple-element.26), channel_id=1, source_target_pairs={{0,8},{4,12},{8,0},{12,4},{1,9},{5,13},{9,1},{13,5},{2,10},{6,14},... | collective-permute-start | bytes 196616 | tf_op jit(solution)/shard_map/ppermute | solution.py:48
  41.7 27.3 %collective-permute-start.14 = (f32[3,256,128]{2,1,0:T(8,128)S(1)}, f32[3,256,128]{2,1,0:T(8,128)S(1)}, u32[]{:S(2)}, u32[]{:S(2)}) collective-permute-start(f32[3,256,128]{2,1,0:T(8,128)S(1)} %pad_maximum_fusion.1.refs_0_), channel_id=1, source_target_pairs={{0,1},{1,2},{2,3},{3,0},{4,5},{5,6},{6,7},{7,4},{8,9},{9,10},{10,1... | collective-permute-start | bytes 1179656 | tf_op jit(solution)/shard_map/ppermute | solution.py:42
  41.8 27.2 %collective-permute-start.15 = (f32[3,256,128]{2,1,0:T(8,128)S(1)}, f32[3,256,128]{2,1,0:T(8,128)S(1)}, u32[]{:S(2)}, u32[]{:S(2)}) collective-permute-start(f32[3,256,128]{2,1,0:T(8,128)S(1)} %pad_maximum_fusion.1.refs_0_), channel_id=1, source_target_pairs={{0,2},{1,3},{2,0},{3,1},{4,6},{5,7},{6,4},{7,5},{8,10},{9,11},{10,... | collective-permute-start | bytes 1179656 | tf_op jit(solution)/shard_map/ppermute | solution.py:42
  43.3 29.6 %collective-permute-start.16 = (f32[3,256,128]{2,1,0:T(8,128)S(1)}, f32[3,256,128]{2,1,0:T(8,128)S(1)}, u32[]{:S(2)}, u32[]{:S(2)}) collective-permute-start(f32[3,256,128]{2,1,0:T(8,128)S(1)} %pad_maximum_fusion.1.refs_0_), channel_id=1, source_target_pairs={{0,3},{1,0},{2,1},{3,2},{4,7},{5,4},{6,5},{7,6},{8,11},{9,8},{10,9... | collective-permute-start | bytes 1179656 | tf_op jit(solution)/shard_map/ppermute | solution.py:42
  45.1 6.4 %collective-permute-start.17 = (f32[64,256]{1,0:T(8,128)S(1)}, f32[64,256]{1,0:T(8,128)S(1)}, u32[]{:S(2)}, u32[]{:S(2)}) collective-permute-start(f32[64,256]{1,0:T(8,128)S(1)} %add_bitcast_fusion), channel_id=1, source_target_pairs={{0,0},{1,1},{2,2},{3,3},{4,32},{5,33},{6,34},{7,35},{8,64},{9,65},... | collective-permute-start | bytes 196616 | tf_op jit(solution)/shard_map/ppermute | solution.py:38
  45.8 7.5 %collective-permute-start.18 = (f32[64,256]{1,0:T(8,128)S(1)}, f32[64,256]{1,0:T(8,128)S(1)}, u32[]{:S(2)}, u32[]{:S(2)}) collective-permute-start(f32[64,256]{1,0:T(8,128)S(1)} %add_bitcast_fusion), channel_id=1, source_target_pairs={{0,96},{1,97},{2,98},{3,99},{4,0},{5,1},{6,2},{7,3},{8,32},{9,33},... | collective-permute-start | bytes 196616 | tf_op jit(solution)/shard_map/ppermute | solution.py:38
  51.5 7.0 %collective-permute-start.19 = (f32[64,256]{1,0:T(8,128)S(1)}, f32[64,256]{1,0:T(8,128)S(1)}, u32[]{:S(2)}, u32[]{:S(2)}) collective-permute-start(f32[64,256]{1,0:T(8,128)S(1)} %add_bitcast_fusion), channel_id=1, source_target_pairs={{0,64},{1,65},{2,66},{3,67},{4,96},{5,97},{6,98},{7,99},{8,0},{9,1... | collective-permute-start | bytes 196616 | tf_op jit(solution)/shard_map/ppermute | solution.py:38
  53.3 10.0 %collective-permute-start.20 = (f32[64,256]{1,0:T(8,128)S(1)}, f32[64,256]{1,0:T(8,128)S(1)}, u32[]{:S(2)}, u32[]{:S(2)}) collective-permute-start(f32[64,256]{1,0:T(8,128)S(1)} %add_bitcast_fusion), channel_id=1, source_target_pairs={{0,32},{1,33},{2,34},{3,35},{4,64},{5,65},{6,66},{7,67},{8,96},{9,... | collective-permute-start | bytes 196616 | tf_op jit(solution)/shard_map/ppermute | solution.py:38
  58.5 8.4 %collective-permute-start.21 = (f32[64,256]{1,0:T(8,128)S(1)}, f32[64,256]{1,0:T(8,128)S(1)}, u32[]{:S(2)}, u32[]{:S(2)}) collective-permute-start(f32[64,256]{1,0:T(8,128)S(1)} %collective-permute-done.17.refs_4_), channel_id=1, source_target_pairs={{0,16},{16,0},{1,17},{17,1},{2,18},{18,2},{3,19},{19,3},{4,20},{20... | collective-permute-start | bytes 196616 | tf_op jit(solution)/shard_map/ppermute | solution.py:18
  73.8 11.6 %collective-permute-start.25 = (f32[3,64,256]{2,1,0:T(8,128)S(1)}, f32[3,64,256]{2,1,0:T(8,128)S(1)}, u32[]{:S(2)}, u32[]{:S(2)}) collective-permute-start(f32[3,64,256]{2,1,0:T(8,128)S(1)} %get-tuple-element.29), channel_id=1, source_target_pairs={{0,4},{4,8},{8,12},{12,0},{1,5},{5,9},{9,13},{13,1},{2,6},{6,10},{... | collective-permute-start | bytes 589832 | tf_op jit(solution)/shard_map/ppermute | solution.py:48
  75.4 12.5 %collective-permute-start.26 = (f32[3,64,256]{2,1,0:T(8,128)S(1)}, f32[3,64,256]{2,1,0:T(8,128)S(1)}, u32[]{:S(2)}, u32[]{:S(2)}) collective-permute-start(f32[3,64,256]{2,1,0:T(8,128)S(1)} %get-tuple-element.30), channel_id=1, source_target_pairs={{0,8},{4,12},{8,0},{12,4},{1,9},{5,13},{9,1},{13,5},{2,10},{6,14},... | collective-permute-start | bytes 589832 | tf_op jit(solution)/shard_map/ppermute | solution.py:48
  75.4 13.2 %collective-permute-start.27 = (f32[3,64,256]{2,1,0:T(8,128)S(1)}, f32[3,64,256]{2,1,0:T(8,128)S(1)}, u32[]{:S(2)}, u32[]{:S(2)}) collective-permute-start(f32[3,64,256]{2,1,0:T(8,128)S(1)} %get-tuple-element.31), channel_id=1, source_target_pairs={{0,12},{4,0},{8,4},{12,8},{1,13},{5,1},{9,5},{13,9},{2,14},{6,2},{... | collective-permute-start | bytes 589832 | tf_op jit(solution)/shard_map/ppermute | solution.py:48
  88.7 6.1 %collective-permute-start.28 = (f32[64,256]{1,0:T(8,128)S(1)}, f32[64,256]{1,0:T(8,128)S(1)}, u32[]{:S(2)}, u32[]{:S(2)}) collective-permute-start(f32[64,256]{1,0:T(8,128)S(1)} %get-tuple-element.57.refs_1_), channel_id=1, source_target_pairs={{0,32},{32,64},{64,96},{96,0},{1,33},{33,65},{65,97},{97,1},{2,34}... | collective-permute-start | bytes 196616 | tf_op jit(solution)/shard_map/ppermute | solution.py:22
  88.8 8.9 %collective-permute-start.29 = (f32[64,256]{1,0:T(8,128)S(1)}, f32[64,256]{1,0:T(8,128)S(1)}, u32[]{:S(2)}, u32[]{:S(2)}) collective-permute-start(f32[64,256]{1,0:T(8,128)S(1)} %get-tuple-element.57.refs_1_), channel_id=1, source_target_pairs={{0,64},{32,96},{64,0},{96,32},{1,65},{33,97},{65,1},{97,33},{2,66}... | collective-permute-start | bytes 196616 | tf_op jit(solution)/shard_map/ppermute | solution.py:22
  89.0 8.7 %collective-permute-start.30 = (f32[64,256]{1,0:T(8,128)S(1)}, f32[64,256]{1,0:T(8,128)S(1)}, u32[]{:S(2)}, u32[]{:S(2)}) collective-permute-start(f32[64,256]{1,0:T(8,128)S(1)} %get-tuple-element.57.refs_1_), channel_id=1, source_target_pairs={{0,96},{32,0},{64,32},{96,64},{1,97},{33,1},{65,33},{97,65},{2,98}... | collective-permute-start | bytes 196616 | tf_op jit(solution)/shard_map/ppermute | solution.py:22
  91.4 10.1 %collective-permute-start.31 = (f32[64,256]{1,0:T(8,128)S(1)}, f32[64,256]{1,0:T(8,128)S(1)}, u32[]{:S(2)}, u32[]{:S(2)}) collective-permute-start(f32[64,256]{1,0:T(8,128)S(1)} %get-tuple-element.57.refs_1_), channel_id=1, source_target_pairs={{0,16},{16,0},{1,17},{17,1},{2,18},{18,2},{3,19},{19,3},{4,20},{20... | collective-permute-start | bytes 196616 | tf_op jit(solution)/shard_map/ppermute | solution.py:18
  94.8 6.8 %collective-permute-start.32 = (f32[64,256]{1,0:T(8,128)S(1)}, f32[64,256]{1,0:T(8,128)S(1)}, u32[]{:S(2)}, u32[]{:S(2)}) collective-permute-start(f32[64,256]{1,0:T(8,128)S(1)} %collective-permute-done.28.refs_2_), channel_id=1, source_target_pairs={{0,16},{16,0},{1,17},{17,1},{2,18},{18,2},{3,19},{19,3},{4,20},{20... | collective-permute-start | bytes 196616 | tf_op jit(solution)/shard_map/ppermute | solution.py:18
  102.4 5.1 %collective-permute-start.35 = (f32[64,256]{1,0:T(8,128)S(1)}, f32[64,256]{1,0:T(8,128)S(1)}, u32[]{:S(2)}, u32[]{:S(2)}) collective-permute-start(f32[64,256]{1,0:T(8,128)S(1)} %full_product.5.refs_1_), channel_id=1, source_target_pairs={{0,32},{32,64},{64,96},{96,0},{1,33},{33,65},{65,97},{97,1},{2,34}... | collective-permute-start | bytes 196616 | tf_op jit(solution)/shard_map/ppermute | solution.py:22
  103.5 5.7 %collective-permute-start.36 = (f32[64,256]{1,0:T(8,128)S(1)}, f32[64,256]{1,0:T(8,128)S(1)}, u32[]{:S(2)}, u32[]{:S(2)}) collective-permute-start(f32[64,256]{1,0:T(8,128)S(1)} %full_product.5.refs_1_), channel_id=1, source_target_pairs={{0,64},{32,96},{64,0},{96,32},{1,65},{33,97},{65,1},{97,33},{2,66}... | collective-permute-start | bytes 196616 | tf_op jit(solution)/shard_map/ppermute | solution.py:22
  106.0 5.0 %collective-permute-start.38 = (f32[64,256]{1,0:T(8,128)S(1)}, f32[64,256]{1,0:T(8,128)S(1)}, u32[]{:S(2)}, u32[]{:S(2)}) collective-permute-start(f32[64,256]{1,0:T(8,128)S(1)} %full_product.5.refs_1_), channel_id=1, source_target_pairs={{0,16},{16,0},{1,17},{17,1},{2,18},{18,2},{3,19},{19,3},{4,20},{20... | collective-permute-start | bytes 196616 | tf_op jit(solution)/shard_map/ppermute | solution.py:18
  112.5 4.7 %collective-permute-start.42 = (f32[64,256]{1,0:T(8,128)S(1)}, f32[64,256]{1,0:T(8,128)S(1)}, u32[]{:S(2)}, u32[]{:S(2)}) collective-permute-start(f32[64,256]{1,0:T(8,128)S(1)} %full_product.6.refs_1_), channel_id=1, source_target_pairs={{0,32},{32,64},{64,96},{96,0},{1,33},{33,65},{65,97},{97,1},{2,34}... | collective-permute-start | bytes 196616 | tf_op jit(solution)/shard_map/ppermute | solution.py:22
  112.8 6.2 %collective-permute-start.43 = (f32[64,256]{1,0:T(8,128)S(1)}, f32[64,256]{1,0:T(8,128)S(1)}, u32[]{:S(2)}, u32[]{:S(2)}) collective-permute-start(f32[64,256]{1,0:T(8,128)S(1)} %full_product.6.refs_1_), channel_id=1, source_target_pairs={{0,64},{32,96},{64,0},{96,32},{1,65},{33,97},{65,1},{97,33},{2,66}... | collective-permute-start | bytes 196616 | tf_op jit(solution)/shard_map/ppermute | solution.py:22
  116.2 4.7 %collective-permute-start.45 = (f32[64,256]{1,0:T(8,128)S(1)}, f32[64,256]{1,0:T(8,128)S(1)}, u32[]{:S(2)}, u32[]{:S(2)}) collective-permute-start(f32[64,256]{1,0:T(8,128)S(1)} %full_product.6.refs_1_), channel_id=1, source_target_pairs={{0,16},{16,0},{1,17},{17,1},{2,18},{18,2},{3,19},{19,3},{4,20},{20... | collective-permute-start | bytes 196616 | tf_op jit(solution)/shard_map/ppermute | solution.py:18
  122.4 4.7 %collective-permute-start.49 = (f32[64,256]{1,0:T(8,128)S(1)}, f32[64,256]{1,0:T(8,128)S(1)}, u32[]{:S(2)}, u32[]{:S(2)}) collective-permute-start(f32[64,256]{1,0:T(8,128)S(1)} %full_product.7.refs_10_), channel_id=1, source_target_pairs={{0,32},{32,64},{64,96},{96,0},{1,33},{33,65},{65,97},{97,1},{2,34}... | collective-permute-start | bytes 196616 | tf_op jit(solution)/shard_map/ppermute | solution.py:22
  123.0 5.7 %collective-permute-start.50 = (f32[64,256]{1,0:T(8,128)S(1)}, f32[64,256]{1,0:T(8,128)S(1)}, u32[]{:S(2)}, u32[]{:S(2)}) collective-permute-start(f32[64,256]{1,0:T(8,128)S(1)} %full_product.7.refs_10_), channel_id=1, source_target_pairs={{0,64},{32,96},{64,0},{96,32},{1,65},{33,97},{65,1},{97,33},{2,66}... | collective-permute-start | bytes 196616 | tf_op jit(solution)/shard_map/ppermute | solution.py:22
  131.7 11.3 %collective-permute-start.56 = (f32[3,64,128]{2,1,0:T(8,128)S(1)}, f32[3,64,128]{2,1,0:T(8,128)S(1)}, u32[]{:S(2)}, u32[]{:S(2)}) collective-permute-start(f32[3,64,128]{2,1,0:T(8,128)S(1)} %get-tuple-element.60), channel_id=1, source_target_pairs={{0,1},{1,0},{2,17},{3,16},{4,33},{5,32},{6,49},{7,48},{8,65},{9,64... | collective-permute-start | bytes 294920 | tf_op jit(solution)/shard_map/ppermute | solution.py:176
  134.7 14.4 %collective-permute-start.57 = (f32[3,64,128]{2,1,0:T(8,128)S(1)}, f32[3,64,128]{2,1,0:T(8,128)S(1)}, u32[]{:S(2)}, u32[]{:S(2)}) collective-permute-start(f32[3,64,128]{2,1,0:T(8,128)S(1)} %get-tuple-element.61), channel_id=1, source_target_pairs={{0,0},{1,1},{2,16},{3,17},{4,32},{5,33},{6,48},{7,49},{8,64},{9,65... | collective-permute-start | bytes 294920 | tf_op jit(solution)/shard_map/ppermute | solution.py:175
  149.2 7.5 %collective-permute-start.58 = (f32[3,128,128]{2,1,0:T(8,128)S(1)}, f32[3,128,128]{2,1,0:T(8,128)S(1)}, u32[]{:S(2)}, u32[]{:S(2)}) collective-permute-start(f32[3,128,128]{2,1,0:T(8,128)S(1)} %pad_maximum_fusion.5.refs_0_), channel_id=1, source_target_pairs={{0,32},{32,64},{64,96},{96,0},{1,33},{33,65},{65,97},{97,1},{2,34}... | collective-permute-start | bytes 589832 | tf_op jit(solution)/shard_map/ppermute | solution.py:22
  149.3 10.6 %collective-permute-start.59 = (f32[3,128,128]{2,1,0:T(8,128)S(1)}, f32[3,128,128]{2,1,0:T(8,128)S(1)}, u32[]{:S(2)}, u32[]{:S(2)}) collective-permute-start(f32[3,128,128]{2,1,0:T(8,128)S(1)} %pad_maximum_fusion.5.refs_0_), channel_id=1, source_target_pairs={{0,64},{32,96},{64,0},{96,32},{1,65},{33,97},{65,1},{97,33},{2,66}... | collective-permute-start | bytes 589832 | tf_op jit(solution)/shard_map/ppermute | solution.py:22
  152.2 7.9 %collective-permute-start.60 = (f32[3,128,128]{2,1,0:T(8,128)S(1)}, f32[3,128,128]{2,1,0:T(8,128)S(1)}, u32[]{:S(2)}, u32[]{:S(2)}) collective-permute-start(f32[3,128,128]{2,1,0:T(8,128)S(1)} %pad_maximum_fusion.5.refs_0_), channel_id=1, source_target_pairs={{0,96},{32,0},{64,32},{96,64},{1,97},{33,1},{65,33},{97,65},{2,98}... | collective-permute-start | bytes 589832 | tf_op jit(solution)/shard_map/ppermute | solution.py:22
  153.3 7.1 %collective-permute-start.61 = (f32[3,128,128]{2,1,0:T(8,128)S(1)}, f32[3,128,128]{2,1,0:T(8,128)S(1)}, u32[]{:S(2)}, u32[]{:S(2)}) collective-permute-start(f32[3,128,128]{2,1,0:T(8,128)S(1)} %pad_maximum_fusion.5.refs_0_), channel_id=1, source_target_pairs={{0,16},{16,0},{1,17},{17,1},{2,18},{18,2},{3,19},{19,3},{4,20},{20... | collective-permute-start | bytes 589832 | tf_op jit(solution)/shard_map/ppermute | solution.py:18
  167.6 4.7 %collective-permute-start.65 = (f32[64,256]{1,0:T(8,128)S(1)}, f32[64,256]{1,0:T(8,128)S(1)}, u32[]{:S(2)}, u32[]{:S(2)}) collective-permute-start(f32[64,256]{1,0:T(8,128)S(1)} %full_product.8.refs_1_), channel_id=1, source_target_pairs={{0,32},{32,64},{64,96},{96,0},{1,33},{33,65},{65,97},{97,1},{2,34}... | collective-permute-start | bytes 196616 | tf_op jit(solution)/shard_map/ppermute | solution.py:22
  170.4 4.8 %collective-permute-start.67 = (f32[64,256]{1,0:T(8,128)S(1)}, f32[64,256]{1,0:T(8,128)S(1)}, u32[]{:S(2)}, u32[]{:S(2)}) collective-permute-start(f32[64,256]{1,0:T(8,128)S(1)} %full_product.8.refs_1_), channel_id=1, source_target_pairs={{0,96},{32,0},{64,32},{96,64},{1,97},{33,1},{65,33},{97,65},{2,98}... | collective-permute-start | bytes 196616 | tf_op jit(solution)/shard_map/ppermute | solution.py:22
  177.6 6.7 %collective-permute-start.73 = (f32[1,64,128]{2,1,0:T(8,128)S(1)}, f32[1,64,128]{2,1,0:T(8,128)S(1)}, u32[]{:S(2)}, u32[]{:S(2)}) collective-permute-start(f32[1,64,128]{2,1,0:T(8,128)S(1)} %get-tuple-element.65), channel_id=1, source_target_pairs={{0,0},{1,1},{2,16},{3,17},{4,32},{5,33},{6,48},{7,49},{8,64},{9,65... | collective-permute-start | bytes 98312 | tf_op jit(solution)/shard_map/ppermute | solution.py:175
  184.4 13.2 %collective-permute-start.74 = (f32[1,128,128]{2,1,0:T(8,128)S(1)}, f32[1,128,128]{2,1,0:T(8,128)S(1)}, u32[]{:S(2)}, u32[]{:S(2)}) collective-permute-start(f32[1,128,128]{2,1,0:T(8,128)S(1)} %pad_maximum_fusion.6.refs_0_), channel_id=1, source_target_pairs={{0,32},{32,64},{64,96},{96,0},{1,33},{33,65},{65,97},{97,1},{2,34}... | collective-permute-start | bytes 196616 | tf_op jit(solution)/shard_map/ppermute | solution.py:22
  188.1 10.0 %collective-permute-start.75 = (f32[1,128,128]{2,1,0:T(8,128)S(1)}, f32[1,128,128]{2,1,0:T(8,128)S(1)}, u32[]{:S(2)}, u32[]{:S(2)}) collective-permute-start(f32[1,128,128]{2,1,0:T(8,128)S(1)} %pad_maximum_fusion.6.refs_0_), channel_id=1, source_target_pairs={{0,64},{32,96},{64,0},{96,32},{1,65},{33,97},{65,1},{97,33},{2,66}... | collective-permute-start | bytes 196616 | tf_op jit(solution)/shard_map/ppermute | solution.py:22
  (46 other events, 235.1 us)
Sparse Core Ops, SparseCore 0:
  10.4 78.4 all-gather.4
  91.6 69.8 all-gather.6
  218.8 93.2 reduce-scatter.3

commit v3 on v2

--- a/solution.py
+++ b/solution.py
@@ -20,6 +20,12 @@
 
 def row_gather(block):
     return both_cores([block] + [lax.ppermute(block, "x", RING[s]) for s in (1, 2, 3)])
+
+
+def row_gather_beside(block, beside):
+    pieces = [block] + [lax.ppermute(block, "x", RING[s]) for s in (1, 2, 3)]
+    own, beside = lax.optimization_barrier((block, beside))
+    return pieces + [lax.ppermute(piece, "core", SWAP) for piece in [own] + pieces[1:]], beside
 
 
 def turned(s):
@@ -78,21 +84,26 @@
 
 
 def fetch(blocks, index):
-    def kernel(blocks_ref, out, sem):
-        copy = pltpu.make_async_copy(blocks_ref.at[:, index], out, sem)
-        copy.start()
-        copy.wait()
+    def kernel(blocks_ref, out, sems):
+        copies = []
+        for i in range(4):
+            part = pl.ds(4 * i, 4)
+            copies.append(pltpu.make_async_copy(blocks_ref.at[part, index], out.at[part], sems.at[i]))
+        for copy in copies:
+            copy.start()
+        for copy in copies:
+            copy.wait()
 
     return pl.pallas_call(
         kernel,
         out_shape=in_vmem((16, 256, 128)),
         in_specs=[pl.BlockSpec(memory_space=pl.ANY)],
         out_specs=LOCAL,
-        scratch_shapes=[pltpu.SemaphoreType.DMA],
+        scratch_shapes=[pltpu.SemaphoreType.DMA((4,))],
         compiler_params=pltpu.CompilerParams(vmem_limit_bytes=8 * 1024 * 1024),
         cost_estimate=pl.CostEstimate(flops=0, bytes_accessed=4194304, transcendentals=0),
         name="fetch",
-    )(blocks)
+    )(pltpu.with_memory_space_constraint(blocks, pltpu.HBM))
 
 
 def slab_product(factor, indices, gathered):
@@ -196,20 +207,21 @@
                 rows[:, part * 512 : part * 512 + 384] = early[:, side * 384 : side * 384 + 384]
                 rows[:, part * 512 + 384 : part * 512 + 512] = last[:, side * 128 : side * 128 + 128]
 
-        block = jnp.concatenate([f[0, pl.ds(j, 256, stride=4), :] for j in range(4)], axis=1)
-        value = lax.dot_general(rows[...], three(block, True), NT, preferred_element_type=jnp.float32)
-        out[:, 0] = value.reshape(16, 64, 256)
+        for t in range(2):
+            block = jnp.concatenate([f[t, pl.ds(j, 256, stride=4), :] for j in range(4)], axis=1)
+            value = lax.dot_general(rows[...], three(block, True), NT, preferred_element_type=jnp.float32)
+            out[:, t] = value.reshape(16, 64, 256)
 
     return pl.pallas_call(
         kernel,
-        grid=(12,),
+        grid=(6,),
         out_shape=jax.ShapeDtypeStruct((16, 12, 64, 256), jnp.float32),
         in_specs=[
-            pl.BlockSpec((1, 1024, 128), lambda t: (t, 0, 0)),
+            pl.BlockSpec((2, 1024, 128), lambda t: (t, 0, 0)),
             pl.BlockSpec((1024, 768), lambda t: (0, 0)),
             pl.BlockSpec((1024, 256), lambda t: (0, 0)),
         ],
-        out_specs=pl.BlockSpec((16, 1, 64, 256), lambda t: (0, t, 0, 0)),
+        out_specs=pl.BlockSpec((16, 2, 64, 256), lambda t: (0, t, 0, 0)),
         scratch_shapes=[pltpu.VMEM((1024, 1536), jnp.bfloat16)],
         compiler_params=pltpu.CompilerParams(vmem_limit_bytes=56 * 1024 * 1024),
         cost_estimate=pl.CostEstimate(flops=2 * 3 * 1024 * 3072 * 512, bytes_accessed=20971520, transcendentals=0),
@@ -227,15 +239,17 @@
     first = z_sum(slab_product(group, (0,), slab_gather(columns_t[0])))[0]
     bases = columns_t[1:4] - z_sum(slab_product(below, (0, 1, 2), slab_gather(first)))
     second = full_product(None, [(fetch(near, 0), row_gather(bases[0]))])
-    gathered_second = row_gather(second)
-    reduced = full_product(bases[1], [(fetch(near, 1), gathered_second)])
-    third = full_product(None, [(fetch(near, 2), row_gather(reduced))])
+    gathered_second, block = row_gather_beside(second, fetch(near, 1))
+    reduced = full_product(bases[1], [(block, gathered_second)])
+    gathered, block = row_gather_beside(reduced, fetch(near, 2))
+    third = full_product(None, [(block, gathered)])
     gathered = row_gather(third)
     (first, second, third), gathered = lax.optimization_barrier(((first, second, third), gathered))
     early = spread(jnp.stack([first, second, third]))
     early, far = lax.optimization_barrier((early, far))
     reduced = full_product(bases[2], [(fetch(far, 0), gathered_second), (fetch(far, 1), gathered)])
-    fourth = full_product(None, [(fetch(far, 2), row_gather(reduced))])
+    gathered, block = row_gather_beside(reduced, fetch(far, 2))
+    fourth = full_product(None, [(block, gathered)])
 
     partial = trailing_product(trailing_factor.reshape(12, 1024, 128), early, spread(fourth[None]))
     updated = jnp.transpose(trailing_columns, (0, 2, 1)) - lax.psum_scatter(partial, COL, scatter_dimension=0)

time: 321 us -> 319 us (level)
  Pallas kernels: 24.9 us -> 30.6 us
  local copies, waits for them, and re-layouts: 9.83 us -> 4.23 us
    ppermute x0 -> x21, starting transfers between devices: none -> 19 us  [the longest x9 11.2 us: row_gather_beside(): pieces = [block] + [lax.ppermute(block, 'x', RING[s]) for s in (1, 2, 3)]]
    ppermute x36 -> x24, starting transfers between devices: 37.6 us -> 26.4 us  [both_cores(): return pieces + [lax.ppermute(piece, 'core', SWAP) for piece in pieces]]
    ppermute x21 -> x12, starting transfers between devices: 34.9 us -> 23.8 us  [row_gather(): lax.ppermute(block, 'x', RING[s])]
    pallas_call x6, Pallas kernels: 0.9 us -> 9.29 us  [fetch(): pl.pallas_call(kernel, out_shape=in_vmem((16, 256, 128)), in_specs=[pl.Bl...]
    unnamed x20 -> x10, local copies, waits for them, and re-layouts: 7.55 us -> 1.94 us
    ppermute x0 -> x21, waiting for transfers between devices: none -> 3.6 us  [the longest x12 2.7 us: row_gather_beside(): lax.ppermute(piece, 'core', SWAP)]
    ppermute x21 -> x12, waiting for transfers between devices: 9.82 us -> 7.6 us  [row_gather(): lax.ppermute(block, 'x', RING[s])]
    ppermute x36 -> x24, waiting for transfers between devices: 8.23 us -> 6.06 us  [both_cores(): return pieces + [lax.ppermute(piece, 'core', SWAP) for piece in pieces]]
  transfers between devices with their start and end apart: 84 -> 84, of which waited for: 38 -> 36; matrix products, arithmetic and copies ran while one was open for 1% -> 1% of each run, Pallas kernels for 1% -> 3%
where the time goes in v3:
time: 319 us; the launch traced here: 318 us
  waiting for transfers between devices  133 us (42%)
  starting transfers between devices  119 us (37%)
  Pallas kernels  30.6 us (10%)
  between operations  14.1 us (4%)
  blocking collectives  12.4 us (4%)
  other arithmetic  5.21 us (2%)
  local copies, waits for them, and re-layouts  4.23 us (1%)
    unnamed x4, waiting for transfers between devices  79.6 us
    ppermute x24, starting transfers between devices, both_cores(): return pieces + [lax.ppermute(piece, 'core', SWAP) for piece in pieces]  26.4 us
    ppermute x12, starting transfers between devices, row_gather(): lax.ppermute(block, 'x', RING[s])  23.8 us
    ppermute x8, starting transfers between devices, slab_gather(): return both_cores([lax.ppermute(block, ALL, turned(s)) for s in range(4)])  21.1 us
    pallas_call x1, Pallas kernels, trailing_product(): pl.pallas_call(kernel, grid=(6,), out_shape=jax.ShapeDtypeStruct((16, 12,...  14.9 us
    psum x1, blocking collectives, shards(): variance_drop = lax.psum(local_squares, ROW) / 8192  12.4 us
    ppermute x6, waiting for transfers between devices, z_sum(): total = total + lax.ppermute(parts[t], 'z', RING[t])  11.4 us
    ppermute x9, starting transfers between devices, row_gather_beside(): pieces = [block] + [lax.ppermute(block, 'x', RING[s]) for s in (1, 2, 3)]  11.2 us
  transfers between devices with their start and end apart: 84, of which 36 were waited for; matrix products, arithmetic and copies ran while one was open for 1% of the time, Pallas kernels for 3%

profile of v3, /device:TPU:1, one launch (start us, length us, event | category | flops | bytes accessed | tf_op | source)
XLA Modules:
  0.0 317.9 jit_solution(6839081970518013419)
XLA Ops:
  11.3 2.1 collective-permute-start.6
  15.4 2.6 collective-permute-start.1
  18.0 7.1 %collective-permute-start.4 = (f32[64,256]{1,0:T(8,128)S(1)}, f32[64,256]{1,0:T(8,128)S(1)}, u32[]{:S(2)}, u32[]{:S(2)}) collective-permute-start(f32[64,256]{1,0:T(8,128)S(1)} %slice_bitcast_fusion.3), channel_id=1, source_target_pairs={{0,96},{1,97},{2,98},{3,99},{4,0},{5,1},{6,2},{7,3},{8,32},{9,33},... | collective-permute-start | bytes 196616 | tf_op jit(solution)/shard_map/ppermute | solution.py:44
  25.1 1.6 collective-permute-start.5
  27.8 2.6 collective-permute-start.10
  30.8 1.9 collective-permute-start.7
  34.6 7.0 %collective-permute-start.12 = (f32[1,64,256]{2,1,0:T(8,128)S(1)}, f32[1,64,256]{2,1,0:T(8,128)S(1)}, u32[]{:S(2)}, u32[]{:S(2)}) collective-permute-start(f32[1,64,256]{2,1,0:T(8,128)S(1)} %get-tuple-element.32), channel_id=1, source_target_pairs={{0,8},{4,12},{8,0},{12,4},{1,9},{5,13},{9,1},{13,5},{2,10},{6,14},... | collective-permute-start | bytes 196616 | tf_op jit(solution)/shard_map/ppermute | solution.py:54
  45.8 5.7 %collective-permute-start.18 = (f32[64,256]{1,0:T(8,128)S(1)}, f32[64,256]{1,0:T(8,128)S(1)}, u32[]{:S(2)}, u32[]{:S(2)}) collective-permute-start(f32[64,256]{1,0:T(8,128)S(1)} %add_bitcast_fusion), channel_id=1, source_target_pairs={{0,96},{1,97},{2,98},{3,99},{4,0},{5,1},{6,2},{7,3},{8,32},{9,33},... | collective-permute-start | bytes 196616 | tf_op jit(solution)/shard_map/ppermute | solution.py:44
  51.5 1.8 collective-permute-start.19
  54.8 3.7 %collective-permute-done.19.refs_6_ = f32[64,256]{1,0:T(8,128)S(1)} collective-permute-done((f32[64,256]{1,0:T(8,128)S(1)}, f32[64,256]{1,0:T(8,128)S(1)}, u32[]{:S(2)}, u32[]{:S(2)}) %collective-permute-start.19) | collective-permute-done | bytes 65568 | tf_op jit(solution)/shard_map/ppermute | solution.py:44
  58.5 4.8 %collective-permute-start.21 = (f32[64,256]{1,0:T(8,128)S(1)}, f32[64,256]{1,0:T(8,128)S(1)}, u32[]{:S(2)}, u32[]{:S(2)}) collective-permute-start(f32[64,256]{1,0:T(8,128)S(1)} %collective-permute-done.17.refs_4_), channel_id=1, source_target_pairs={{0,16},{16,0},{1,17},{17,1},{2,18},{18,2},{3,19},{19,3},{4,20},{20... | collective-permute-start | bytes 196616 | tf_op jit(solution)/shard_map/ppermute | solution.py:18
  63.3 3.6 %collective-permute-start.22 = (f32[64,256]{1,0:T(8,128)S(1)}, f32[64,256]{1,0:T(8,128)S(1)}, u32[]{:S(2)}, u32[]{:S(2)}) collective-permute-start(f32[64,256]{1,0:T(8,128)S(1)} %collective-permute-done.18.refs_5_), channel_id=1, source_target_pairs={{0,16},{16,0},{1,17},{17,1},{2,18},{18,2},{3,19},{19,3},{4,20},{20... | collective-permute-start | bytes 196616 | tf_op jit(solution)/shard_map/ppermute | solution.py:18
  69.0 3.9 %collective-permute-done.16.refs_3_ = f32[3,256,128]{2,1,0:T(8,128)S(1)} collective-permute-done((f32[3,256,128]{2,1,0:T(8,128)S(1)}, f32[3,256,128]{2,1,0:T(8,128)S(1)}, u32[]{:S(2)}, u32[]{:S(2)}) %collective-permute-start.16) | collective-permute-done | bytes 393248 | tf_op jit(solution)/shard_map/ppermute | solution.py:48
  73.8 1.5 collective-permute-start.25
  75.4 2.5 collective-permute-start.27
  77.9 7.5 %collective-permute-done.25 = f32[3,64,256]{2,1,0:T(8,128)S(1)} collective-permute-done((f32[3,64,256]{2,1,0:T(8,128)S(1)}, f32[3,64,256]{2,1,0:T(8,128)S(1)}, u32[]{:S(2)}, u32[]{:S(2)}) %collective-permute-start.25) | collective-permute-done | bytes 196640 | tf_op jit(solution)/shard_map/ppermute | solution.py:54
  85.4 2.4 collective-permute-done.26
  89.0 2.4 collective-permute-start.30
  91.4 3.3 %collective-permute-start.31 = (f32[64,256]{1,0:T(8,128)S(1)}, f32[64,256]{1,0:T(8,128)S(1)}, u32[]{:S(2)}, u32[]{:S(2)}) collective-permute-start(f32[64,256]{1,0:T(8,128)S(1)} %get-tuple-element.69.refs_1_), channel_id=1, source_target_pairs={{0,16},{16,0},{1,17},{17,1},{2,18},{18,2},{3,19},{19,3},{4,20},{20... | collective-permute-start | bytes 196616 | tf_op jit(solution)/shard_map/ppermute | solution.py:18
  94.8 2.9 collective-permute-start.32
  98.6 1.5 fetch.6.refs_0_
  102.1 2.2 collective-permute-start.36
  104.6 1.5 fetch.7.refs_0_
  111.4 2.7 collective-permute-start.43
  114.8 1.5 fetch.8.refs_0_
  121.6 2.6 collective-permute-start.50
  125.7 1.6 collective-permute-start.53
  130.3 3.0 collective-permute-start.56
  133.3 1.9 collective-permute-start.57
  135.3 6.1 %collective-permute-done.56 = f32[3,64,128]{2,1,0:T(8,128)S(1)} collective-permute-done((f32[3,64,128]{2,1,0:T(8,128)S(1)}, f32[3,64,128]{2,1,0:T(8,128)S(1)}, u32[]{:S(2)}, u32[]{:S(2)}) %collective-permute-start.56) | collective-permute-done | bytes 98336 | tf_op jit(solution)/shard_map/ppermute | solution.py:187
  141.4 6.4 %collective-permute-done.57 = f32[3,64,128]{2,1,0:T(8,128)S(1)} collective-permute-done((f32[3,64,128]{2,1,0:T(8,128)S(1)}, f32[3,64,128]{2,1,0:T(8,128)S(1)}, u32[]{:S(2)}, u32[]{:S(2)}) %collective-permute-start.57) | collective-permute-done | bytes 98336 | tf_op jit(solution)/shard_map/ppermute | solution.py:186
  147.9 3.0 collective-permute-start.59
  151.9 3.4 %collective-permute-done.58.refs_1_ = f32[3,128,128]{2,1,0:T(8,128)S(1)} collective-permute-done((f32[3,128,128]{2,1,0:T(8,128)S(1)}, f32[3,128,128]{2,1,0:T(8,128)S(1)}, u32[]{:S(2)}, u32[]{:S(2)}) %collective-permute-start.58) | collective-permute-done | bytes 196640 | tf_op jit(solution)/shard_map/ppermute | solution.py:22
  155.3 3.2 collective-permute-done.59.refs_2_
  161.6 1.5 fetch.9.refs_0_
  163.1 1.6 fetch.10.refs_9_
  164.7 1.5 full_product.8.refs_1_
  170.1 1.5 fetch.11.refs_0_
  176.0 1.6 collective-permute-start.72
  177.6 2.9 collective-permute-start.73
  180.6 3.7 %collective-permute-done.73 = f32[1,64,128]{2,1,0:T(8,128)S(1)} collective-permute-done((f32[1,64,128]{2,1,0:T(8,128)S(1)}, f32[1,64,128]{2,1,0:T(8,128)S(1)}, u32[]{:S(2)}, u32[]{:S(2)}) %collective-permute-start.73) | collective-permute-done | bytes 32800 | tf_op jit(solution)/shard_map/ppermute | solution.py:186
  184.3 3.5 %collective-permute-start.74 = (f32[1,128,128]{2,1,0:T(8,128)S(1)}, f32[1,128,128]{2,1,0:T(8,128)S(1)}, u32[]{:S(2)}, u32[]{:S(2)}) collective-permute-start(f32[1,128,128]{2,1,0:T(8,128)S(1)} %pad_maximum_fusion.6.refs_0_), channel_id=1, source_target_pairs={{0,32},{32,64},{64,96},{96,0},{1,33},{33,65},{65,97},{97,1},{2,34}... | collective-permute-start | bytes 196616 | tf_op jit(solution)/shard_map/ppermute | solution.py:22
  187.8 7.8 %collective-permute-start.75 = (f32[1,128,128]{2,1,0:T(8,128)S(1)}, f32[1,128,128]{2,1,0:T(8,128)S(1)}, u32[]{:S(2)}, u32[]{:S(2)}) collective-permute-start(f32[1,128,128]{2,1,0:T(8,128)S(1)} %pad_maximum_fusion.6.refs_0_), channel_id=1, source_target_pairs={{0,64},{32,96},{64,0},{96,32},{1,65},{33,97},{65,1},{97,33},{2,66}... | collective-permute-start | bytes 196616 | tf_op jit(solution)/shard_map/ppermute | solution.py:22
  195.7 2.0 collective-permute-start.76
  201.1 14.9 %trailing_product.1 = f32[16,12,64,256]{3,2,1,0:T(8,128)} custom-call(f32[12,1024,128]{2,1,0:T(8,128)} %bitcast.45, bf16[1024,768]{1,0:T(8,128)(2,1)} %copy-done, bf16[1024,256]{1,0:T(8,128)(2,1)} %copy-done.1), custom_call_target="tpu_custom_call" | custom-call | flops 9663676416 | bytes 20971520 | tf_op jit(solution)/shard_map/trailing_product/pallas_call | solution.py:215
  216.8 12.4 %psum.7 = f32[64]{0:T(128)S(1)} all-reduce(f32[64]{0:T(128)S(1)} %get-tuple-element.65), channel_id=1, replica_groups=mesh['x'=4,'core'=2,'z'=4,'y'=4] {'x','core'}, use_global_device_ids=true, to_apply=%region_2.3 | all-reduce | flops 64 | bytes 512 | tf_op jit(solution)/shard_map/psum | solution.py:259
  229.7 79.5 %reduce-scatter.4.cloned.1.call-done = f32[1,12,64,256]{3,2,1,0:T(8,128)} async-done(((f32[16,12,64,256]{3,2,1,0:T(8,128)}), f32[1,12,64,256]{3,2,1,0:T(8,128)}) %reduce-scatter.4.cloned.1.call-update) | async-done | bytes 786448
  309.3 2.1 fusion
  (170 shorter events, 55.4 us)
Async XLA Ops:
  7.2 91.4 %all-gather.5.cloned.1.call-start = ((), (), s32[]{:S(2)}) async-start(), calls=%async_computation.1 | async-start | bytes 6684672 | tf_op jit(solution)/shard_map/all_gather | solution.py:236
  10.3 151.3 %all-gather.7.cloned.1.call-start = ((), (), s32[]{:S(2)}) async-start(), calls=%async_computation.2 | async-start | bytes 6684672 | tf_op jit(solution)/shard_map/all_gather | solution.py:237
  11.2 298.1 %reduce-scatter.4.cloned.1.call-start = ((), (), s32[]{:S(2)}) async-start(), calls=%async_computation.3 | async-start | bytes 13369344
  11.3 13.9 %collective-permute-start.6 = (f32[64,256]{1,0:T(8,128)S(1)}, f32[64,256]{1,0:T(8,128)S(1)}, u32[]{:S(2)}, u32[]{:S(2)}) collective-permute-start(f32[64,256]{1,0:T(8,128)S(1)} %slice_bitcast_fusion.3), channel_id=1, source_target_pairs={{0,32},{1,33},{2,34},{3,35},{4,64},{5,65},{6,66},{7,67},{8,96},{9,... | collective-permute-start | bytes 196616 | tf_op jit(solution)/shard_map/ppermute | solution.py:44
  13.4 13.3 %collective-permute-start.3 = (f32[64,256]{1,0:T(8,128)S(1)}, f32[64,256]{1,0:T(8,128)S(1)}, u32[]{:S(2)}, u32[]{:S(2)}) collective-permute-start(f32[64,256]{1,0:T(8,128)S(1)} %slice_bitcast_fusion.3), channel_id=1, source_target_pairs={{0,0},{1,1},{2,2},{3,3},{4,32},{5,33},{6,34},{7,35},{8,64},{9,65},... | collective-permute-start | bytes 196616 | tf_op jit(solution)/shard_map/ppermute | solution.py:44
  14.0 18.7 %collective-permute-start = (f32[1,256,128]{2,1,0:T(8,128)S(1)}, f32[1,256,128]{2,1,0:T(8,128)S(1)}, u32[]{:S(2)}, u32[]{:S(2)}) collective-permute-start(f32[1,256,128]{2,1,0:T(8,128)S(1)} %get-tuple-element.63.refs_0_), channel_id=1, source_target_pairs={{0,1},{1,2},{2,3},{3,0},{4,5},{5,6},{6,7},{7,4},{8,9},{9,10},{10,1... | collective-permute-start | bytes 393224 | tf_op jit(solution)/shard_map/ppermute | solution.py:48
  15.4 17.3 %collective-permute-start.1 = (f32[1,256,128]{2,1,0:T(8,128)S(1)}, f32[1,256,128]{2,1,0:T(8,128)S(1)}, u32[]{:S(2)}, u32[]{:S(2)}) collective-permute-start(f32[1,256,128]{2,1,0:T(8,128)S(1)} %get-tuple-element.63.refs_0_), channel_id=1, source_target_pairs={{0,2},{1,3},{2,0},{3,1},{4,6},{5,7},{6,4},{7,5},{8,10},{9,11},{10,... | collective-permute-start | bytes 393224 | tf_op jit(solution)/shard_map/ppermute | solution.py:48
  18.0 9.8 %collective-permute-start.4 = (f32[64,256]{1,0:T(8,128)S(1)}, f32[64,256]{1,0:T(8,128)S(1)}, u32[]{:S(2)}, u32[]{:S(2)}) collective-permute-start(f32[64,256]{1,0:T(8,128)S(1)} %slice_bitcast_fusion.3), channel_id=1, source_target_pairs={{0,96},{1,97},{2,98},{3,99},{4,0},{5,1},{6,2},{7,3},{8,32},{9,33},... | collective-permute-start | bytes 196616 | tf_op jit(solution)/shard_map/ppermute | solution.py:44
  25.1 5.7 %collective-permute-start.5 = (f32[64,256]{1,0:T(8,128)S(1)}, f32[64,256]{1,0:T(8,128)S(1)}, u32[]{:S(2)}, u32[]{:S(2)}) collective-permute-start(f32[64,256]{1,0:T(8,128)S(1)} %slice_bitcast_fusion.3), channel_id=1, source_target_pairs={{0,64},{1,65},{2,66},{3,67},{4,96},{5,97},{6,98},{7,99},{8,0},{9,1... | collective-permute-start | bytes 196616 | tf_op jit(solution)/shard_map/ppermute | solution.py:44
  26.7 6.5 %collective-permute-start.2 = (f32[1,256,128]{2,1,0:T(8,128)S(1)}, f32[1,256,128]{2,1,0:T(8,128)S(1)}, u32[]{:S(2)}, u32[]{:S(2)}) collective-permute-start(f32[1,256,128]{2,1,0:T(8,128)S(1)} %get-tuple-element.63.refs_0_), channel_id=1, source_target_pairs={{0,3},{1,0},{2,1},{3,2},{4,7},{5,4},{6,5},{7,6},{8,11},{9,8},{10,9... | collective-permute-start | bytes 393224 | tf_op jit(solution)/shard_map/ppermute | solution.py:48
  27.8 5.5 %collective-permute-start.10 = (f32[64,256]{1,0:T(8,128)S(1)}, f32[64,256]{1,0:T(8,128)S(1)}, u32[]{:S(2)}, u32[]{:S(2)}) collective-permute-start(f32[64,256]{1,0:T(8,128)S(1)} %collective-permute-done.6.refs_7_), channel_id=1, source_target_pairs={{0,16},{16,0},{1,17},{17,1},{2,18},{18,2},{3,19},{19,3},{4,20},{20... | collective-permute-start | bytes 196616 | tf_op jit(solution)/shard_map/ppermute | solution.py:18
  34.6 8.8 %collective-permute-start.11 = (f32[1,64,256]{2,1,0:T(8,128)S(1)}, f32[1,64,256]{2,1,0:T(8,128)S(1)}, u32[]{:S(2)}, u32[]{:S(2)}) collective-permute-start(f32[1,64,256]{2,1,0:T(8,128)S(1)} %get-tuple-element.31), channel_id=1, source_target_pairs={{0,4},{4,8},{8,12},{12,0},{1,5},{5,9},{9,13},{13,1},{2,6},{6,10},{... | collective-permute-start | bytes 196616 | tf_op jit(solution)/shard_map/ppermute | solution.py:54
  34.6 10.0 %collective-permute-start.12 = (f32[1,64,256]{2,1,0:T(8,128)S(1)}, f32[1,64,256]{2,1,0:T(8,128)S(1)}, u32[]{:S(2)}, u32[]{:S(2)}) collective-permute-start(f32[1,64,256]{2,1,0:T(8,128)S(1)} %get-tuple-element.32), channel_id=1, source_target_pairs={{0,8},{4,12},{8,0},{12,4},{1,9},{5,13},{9,1},{13,5},{2,10},{6,14},... | collective-permute-start | bytes 196616 | tf_op jit(solution)/shard_map/ppermute | solution.py:54
  41.7 27.3 %collective-permute-start.14 = (f32[3,256,128]{2,1,0:T(8,128)S(1)}, f32[3,256,128]{2,1,0:T(8,128)S(1)}, u32[]{:S(2)}, u32[]{:S(2)}) collective-permute-start(f32[3,256,128]{2,1,0:T(8,128)S(1)} %pad_maximum_fusion.1.refs_0_), channel_id=1, source_target_pairs={{0,1},{1,2},{2,3},{3,0},{4,5},{5,6},{6,7},{7,4},{8,9},{9,10},{10,1... | collective-permute-start | bytes 1179656 | tf_op jit(solution)/shard_map/ppermute | solution.py:48
  41.8 27.2 %collective-permute-start.15 = (f32[3,256,128]{2,1,0:T(8,128)S(1)}, f32[3,256,128]{2,1,0:T(8,128)S(1)}, u32[]{:S(2)}, u32[]{:S(2)}) collective-permute-start(f32[3,256,128]{2,1,0:T(8,128)S(1)} %pad_maximum_fusion.1.refs_0_), channel_id=1, source_target_pairs={{0,2},{1,3},{2,0},{3,1},{4,6},{5,7},{6,4},{7,5},{8,10},{9,11},{10,... | collective-permute-start | bytes 1179656 | tf_op jit(solution)/shard_map/ppermute | solution.py:48
  43.3 29.6 %collective-permute-start.16 = (f32[3,256,128]{2,1,0:T(8,128)S(1)}, f32[3,256,128]{2,1,0:T(8,128)S(1)}, u32[]{:S(2)}, u32[]{:S(2)}) collective-permute-start(f32[3,256,128]{2,1,0:T(8,128)S(1)} %pad_maximum_fusion.1.refs_0_), channel_id=1, source_target_pairs={{0,3},{1,0},{2,1},{3,2},{4,7},{5,4},{6,5},{7,6},{8,11},{9,8},{10,9... | collective-permute-start | bytes 1179656 | tf_op jit(solution)/shard_map/ppermute | solution.py:48
  45.1 6.4 %collective-permute-start.17 = (f32[64,256]{1,0:T(8,128)S(1)}, f32[64,256]{1,0:T(8,128)S(1)}, u32[]{:S(2)}, u32[]{:S(2)}) collective-permute-start(f32[64,256]{1,0:T(8,128)S(1)} %add_bitcast_fusion), channel_id=1, source_target_pairs={{0,0},{1,1},{2,2},{3,3},{4,32},{5,33},{6,34},{7,35},{8,64},{9,65},... | collective-permute-start | bytes 196616 | tf_op jit(solution)/shard_map/ppermute | solution.py:44
  45.8 7.5 %collective-permute-start.18 = (f32[64,256]{1,0:T(8,128)S(1)}, f32[64,256]{1,0:T(8,128)S(1)}, u32[]{:S(2)}, u32[]{:S(2)}) collective-permute-start(f32[64,256]{1,0:T(8,128)S(1)} %add_bitcast_fusion), channel_id=1, source_target_pairs={{0,96},{1,97},{2,98},{3,99},{4,0},{5,1},{6,2},{7,3},{8,32},{9,33},... | collective-permute-start | bytes 196616 | tf_op jit(solution)/shard_map/ppermute | solution.py:44
  51.5 7.0 %collective-permute-start.19 = (f32[64,256]{1,0:T(8,128)S(1)}, f32[64,256]{1,0:T(8,128)S(1)}, u32[]{:S(2)}, u32[]{:S(2)}) collective-permute-start(f32[64,256]{1,0:T(8,128)S(1)} %add_bitcast_fusion), channel_id=1, source_target_pairs={{0,64},{1,65},{2,66},{3,67},{4,96},{5,97},{6,98},{7,99},{8,0},{9,1... | collective-permute-start | bytes 196616 | tf_op jit(solution)/shard_map/ppermute | solution.py:44
  53.3 10.0 %collective-permute-start.20 = (f32[64,256]{1,0:T(8,128)S(1)}, f32[64,256]{1,0:T(8,128)S(1)}, u32[]{:S(2)}, u32[]{:S(2)}) collective-permute-start(f32[64,256]{1,0:T(8,128)S(1)} %add_bitcast_fusion), channel_id=1, source_target_pairs={{0,32},{1,33},{2,34},{3,35},{4,64},{5,65},{6,66},{7,67},{8,96},{9,... | collective-permute-start | bytes 196616 | tf_op jit(solution)/shard_map/ppermute | solution.py:44
  58.5 8.4 %collective-permute-start.21 = (f32[64,256]{1,0:T(8,128)S(1)}, f32[64,256]{1,0:T(8,128)S(1)}, u32[]{:S(2)}, u32[]{:S(2)}) collective-permute-start(f32[64,256]{1,0:T(8,128)S(1)} %collective-permute-done.17.refs_4_), channel_id=1, source_target_pairs={{0,16},{16,0},{1,17},{17,1},{2,18},{18,2},{3,19},{19,3},{4,20},{20... | collective-permute-start | bytes 196616 | tf_op jit(solution)/shard_map/ppermute | solution.py:18
  73.8 11.6 %collective-permute-start.25 = (f32[3,64,256]{2,1,0:T(8,128)S(1)}, f32[3,64,256]{2,1,0:T(8,128)S(1)}, u32[]{:S(2)}, u32[]{:S(2)}) collective-permute-start(f32[3,64,256]{2,1,0:T(8,128)S(1)} %get-tuple-element.35), channel_id=1, source_target_pairs={{0,4},{4,8},{8,12},{12,0},{1,5},{5,9},{9,13},{13,1},{2,6},{6,10},{... | collective-permute-start | bytes 589832 | tf_op jit(solution)/shard_map/ppermute | solution.py:54
  75.4 12.5 %collective-permute-start.26 = (f32[3,64,256]{2,1,0:T(8,128)S(1)}, f32[3,64,256]{2,1,0:T(8,128)S(1)}, u32[]{:S(2)}, u32[]{:S(2)}) collective-permute-start(f32[3,64,256]{2,1,0:T(8,128)S(1)} %get-tuple-element.36), channel_id=1, source_target_pairs={{0,8},{4,12},{8,0},{12,4},{1,9},{5,13},{9,1},{13,5},{2,10},{6,14},... | collective-permute-start | bytes 589832 | tf_op jit(solution)/shard_map/ppermute | solution.py:54
  75.4 13.2 %collective-permute-start.27 = (f32[3,64,256]{2,1,0:T(8,128)S(1)}, f32[3,64,256]{2,1,0:T(8,128)S(1)}, u32[]{:S(2)}, u32[]{:S(2)}) collective-permute-start(f32[3,64,256]{2,1,0:T(8,128)S(1)} %get-tuple-element.37), channel_id=1, source_target_pairs={{0,12},{4,0},{8,4},{12,8},{1,13},{5,1},{9,5},{13,9},{2,14},{6,2},{... | collective-permute-start | bytes 589832 | tf_op jit(solution)/shard_map/ppermute | solution.py:54
  88.7 6.1 %collective-permute-start.28 = (f32[64,256]{1,0:T(8,128)S(1)}, f32[64,256]{1,0:T(8,128)S(1)}, u32[]{:S(2)}, u32[]{:S(2)}) collective-permute-start(f32[64,256]{1,0:T(8,128)S(1)} %get-tuple-element.69.refs_1_), channel_id=1, source_target_pairs={{0,32},{32,64},{64,96},{96,0},{1,33},{33,65},{65,97},{97,1},{2,34}... | collective-permute-start | bytes 196616 | tf_op jit(solution)/shard_map/ppermute | solution.py:22
  88.8 8.9 %collective-permute-start.29 = (f32[64,256]{1,0:T(8,128)S(1)}, f32[64,256]{1,0:T(8,128)S(1)}, u32[]{:S(2)}, u32[]{:S(2)}) collective-permute-start(f32[64,256]{1,0:T(8,128)S(1)} %get-tuple-element.69.refs_1_), channel_id=1, source_target_pairs={{0,64},{32,96},{64,0},{96,32},{1,65},{33,97},{65,1},{97,33},{2,66}... | collective-permute-start | bytes 196616 | tf_op jit(solution)/shard_map/ppermute | solution.py:22
  89.0 8.7 %collective-permute-start.30 = (f32[64,256]{1,0:T(8,128)S(1)}, f32[64,256]{1,0:T(8,128)S(1)}, u32[]{:S(2)}, u32[]{:S(2)}) collective-permute-start(f32[64,256]{1,0:T(8,128)S(1)} %get-tuple-element.69.refs_1_), channel_id=1, source_target_pairs={{0,96},{32,0},{64,32},{96,64},{1,97},{33,1},{65,33},{97,65},{2,98}... | collective-permute-start | bytes 196616 | tf_op jit(solution)/shard_map/ppermute | solution.py:22
  91.4 8.7 %collective-permute-start.31 = (f32[64,256]{1,0:T(8,128)S(1)}, f32[64,256]{1,0:T(8,128)S(1)}, u32[]{:S(2)}, u32[]{:S(2)}) collective-permute-start(f32[64,256]{1,0:T(8,128)S(1)} %get-tuple-element.69.refs_1_), channel_id=1, source_target_pairs={{0,16},{16,0},{1,17},{17,1},{2,18},{18,2},{3,19},{19,3},{4,20},{20... | collective-permute-start | bytes 196616 | tf_op jit(solution)/shard_map/ppermute | solution.py:18
  94.8 5.4 %collective-permute-start.32 = (f32[64,256]{1,0:T(8,128)S(1)}, f32[64,256]{1,0:T(8,128)S(1)}, u32[]{:S(2)}, u32[]{:S(2)}) collective-permute-start(f32[64,256]{1,0:T(8,128)S(1)} %collective-permute-done.28.refs_2_), channel_id=1, source_target_pairs={{0,16},{16,0},{1,17},{17,1},{2,18},{18,2},{3,19},{19,3},{4,20},{20... | collective-permute-start | bytes 196616 | tf_op jit(solution)/shard_map/ppermute | solution.py:18
  101.0 5.8 %collective-permute-start.35 = (f32[64,256]{1,0:T(8,128)S(1)}, f32[64,256]{1,0:T(8,128)S(1)}, u32[]{:S(2)}, u32[]{:S(2)}) collective-permute-start(f32[64,256]{1,0:T(8,128)S(1)} %full_product.5.refs_1_), channel_id=1, source_target_pairs={{0,32},{32,64},{64,96},{96,0},{1,33},{33,65},{65,97},{97,1},{2,34}... | collective-permute-start | bytes 196616 | tf_op jit(solution)/shard_map/ppermute | solution.py:26
  102.1 5.7 %collective-permute-start.36 = (f32[64,256]{1,0:T(8,128)S(1)}, f32[64,256]{1,0:T(8,128)S(1)}, u32[]{:S(2)}, u32[]{:S(2)}) collective-permute-start(f32[64,256]{1,0:T(8,128)S(1)} %full_product.5.refs_1_), channel_id=1, source_target_pairs={{0,64},{32,96},{64,0},{96,32},{1,65},{33,97},{65,1},{97,33},{2,66}... | collective-permute-start | bytes 196616 | tf_op jit(solution)/shard_map/ppermute | solution.py:26
  111.1 6.4 %collective-permute-start.42 = (f32[64,256]{1,0:T(8,128)S(1)}, f32[64,256]{1,0:T(8,128)S(1)}, u32[]{:S(2)}, u32[]{:S(2)}) collective-permute-start(f32[64,256]{1,0:T(8,128)S(1)} %full_product.6.refs_1_), channel_id=1, source_target_pairs={{0,32},{32,64},{64,96},{96,0},{1,33},{33,65},{65,97},{97,1},{2,34}... | collective-permute-start | bytes 196616 | tf_op jit(solution)/shard_map/ppermute | solution.py:26
  111.4 6.2 %collective-permute-start.43 = (f32[64,256]{1,0:T(8,128)S(1)}, f32[64,256]{1,0:T(8,128)S(1)}, u32[]{:S(2)}, u32[]{:S(2)}) collective-permute-start(f32[64,256]{1,0:T(8,128)S(1)} %full_product.6.refs_1_), channel_id=1, source_target_pairs={{0,64},{32,96},{64,0},{96,32},{1,65},{33,97},{65,1},{97,33},{2,66}... | collective-permute-start | bytes 196616 | tf_op jit(solution)/shard_map/ppermute | solution.py:26
  121.0 4.7 %collective-permute-start.49 = (f32[64,256]{1,0:T(8,128)S(1)}, f32[64,256]{1,0:T(8,128)S(1)}, u32[]{:S(2)}, u32[]{:S(2)}) collective-permute-start(f32[64,256]{1,0:T(8,128)S(1)} %full_product.7.refs_10_), channel_id=1, source_target_pairs={{0,32},{32,64},{64,96},{96,0},{1,33},{33,65},{65,97},{97,1},{2,34}... | collective-permute-start | bytes 196616 | tf_op jit(solution)/shard_map/ppermute | solution.py:22
  121.6 5.7 %collective-permute-start.50 = (f32[64,256]{1,0:T(8,128)S(1)}, f32[64,256]{1,0:T(8,128)S(1)}, u32[]{:S(2)}, u32[]{:S(2)}) collective-permute-start(f32[64,256]{1,0:T(8,128)S(1)} %full_product.7.refs_10_), channel_id=1, source_target_pairs={{0,64},{32,96},{64,0},{96,32},{1,65},{33,97},{65,1},{97,33},{2,66}... | collective-permute-start | bytes 196616 | tf_op jit(solution)/shard_map/ppermute | solution.py:22
  124.7 4.7 %collective-permute-start.52 = (f32[64,256]{1,0:T(8,128)S(1)}, f32[64,256]{1,0:T(8,128)S(1)}, u32[]{:S(2)}, u32[]{:S(2)}) collective-permute-start(f32[64,256]{1,0:T(8,128)S(1)} %full_product.7.refs_10_), channel_id=1, source_target_pairs={{0,16},{16,0},{1,17},{17,1},{2,18},{18,2},{3,19},{19,3},{4,20},{20... | collective-permute-start | bytes 196616 | tf_op jit(solution)/shard_map/ppermute | solution.py:18
  130.3 11.0 %collective-permute-start.56 = (f32[3,64,128]{2,1,0:T(8,128)S(1)}, f32[3,64,128]{2,1,0:T(8,128)S(1)}, u32[]{:S(2)}, u32[]{:S(2)}) collective-permute-start(f32[3,64,128]{2,1,0:T(8,128)S(1)} %get-tuple-element.72), channel_id=1, source_target_pairs={{0,1},{1,0},{2,17},{3,16},{4,33},{5,32},{6,49},{7,48},{8,65},{9,64... | collective-permute-start | bytes 294920 | tf_op jit(solution)/shard_map/ppermute | solution.py:187
  133.3 14.4 %collective-permute-start.57 = (f32[3,64,128]{2,1,0:T(8,128)S(1)}, f32[3,64,128]{2,1,0:T(8,128)S(1)}, u32[]{:S(2)}, u32[]{:S(2)}) collective-permute-start(f32[3,64,128]{2,1,0:T(8,128)S(1)} %get-tuple-element.73), channel_id=1, source_target_pairs={{0,0},{1,1},{2,16},{3,17},{4,32},{5,33},{6,48},{7,49},{8,64},{9,65... | collective-permute-start | bytes 294920 | tf_op jit(solution)/shard_map/ppermute | solution.py:186
  147.8 7.5 %collective-permute-start.58 = (f32[3,128,128]{2,1,0:T(8,128)S(1)}, f32[3,128,128]{2,1,0:T(8,128)S(1)}, u32[]{:S(2)}, u32[]{:S(2)}) collective-permute-start(f32[3,128,128]{2,1,0:T(8,128)S(1)} %pad_maximum_fusion.5.refs_0_), channel_id=1, source_target_pairs={{0,32},{32,64},{64,96},{96,0},{1,33},{33,65},{65,97},{97,1},{2,34}... | collective-permute-start | bytes 589832 | tf_op jit(solution)/shard_map/ppermute | solution.py:22
  147.9 10.6 %collective-permute-start.59 = (f32[3,128,128]{2,1,0:T(8,128)S(1)}, f32[3,128,128]{2,1,0:T(8,128)S(1)}, u32[]{:S(2)}, u32[]{:S(2)}) collective-permute-start(f32[3,128,128]{2,1,0:T(8,128)S(1)} %pad_maximum_fusion.5.refs_0_), channel_id=1, source_target_pairs={{0,64},{32,96},{64,0},{96,32},{1,65},{33,97},{65,1},{97,33},{2,66}... | collective-permute-start | bytes 589832 | tf_op jit(solution)/shard_map/ppermute | solution.py:22
  150.8 7.9 %collective-permute-start.60 = (f32[3,128,128]{2,1,0:T(8,128)S(1)}, f32[3,128,128]{2,1,0:T(8,128)S(1)}, u32[]{:S(2)}, u32[]{:S(2)}) collective-permute-start(f32[3,128,128]{2,1,0:T(8,128)S(1)} %pad_maximum_fusion.5.refs_0_), channel_id=1, source_target_pairs={{0,96},{32,0},{64,32},{96,64},{1,97},{33,1},{65,33},{97,65},{2,98}... | collective-permute-start | bytes 589832 | tf_op jit(solution)/shard_map/ppermute | solution.py:22
  151.9 7.1 %collective-permute-start.61 = (f32[3,128,128]{2,1,0:T(8,128)S(1)}, f32[3,128,128]{2,1,0:T(8,128)S(1)}, u32[]{:S(2)}, u32[]{:S(2)}) collective-permute-start(f32[3,128,128]{2,1,0:T(8,128)S(1)} %pad_maximum_fusion.5.refs_0_), channel_id=1, source_target_pairs={{0,16},{16,0},{1,17},{17,1},{2,18},{18,2},{3,19},{19,3},{4,20},{20... | collective-permute-start | bytes 589832 | tf_op jit(solution)/shard_map/ppermute | solution.py:18
  166.2 6.3 %collective-permute-start.65 = (f32[64,256]{1,0:T(8,128)S(1)}, f32[64,256]{1,0:T(8,128)S(1)}, u32[]{:S(2)}, u32[]{:S(2)}) collective-permute-start(f32[64,256]{1,0:T(8,128)S(1)} %full_product.8.refs_1_), channel_id=1, source_target_pairs={{0,32},{32,64},{64,96},{96,0},{1,33},{33,65},{65,97},{97,1},{2,34}... | collective-permute-start | bytes 196616 | tf_op jit(solution)/shard_map/ppermute | solution.py:26
  167.6 5.4 %collective-permute-start.66 = (f32[64,256]{1,0:T(8,128)S(1)}, f32[64,256]{1,0:T(8,128)S(1)}, u32[]{:S(2)}, u32[]{:S(2)}) collective-permute-start(f32[64,256]{1,0:T(8,128)S(1)} %full_product.8.refs_1_), channel_id=1, source_target_pairs={{0,64},{32,96},{64,0},{96,32},{1,65},{33,97},{65,1},{97,33},{2,66}... | collective-permute-start | bytes 196616 | tf_op jit(solution)/shard_map/ppermute | solution.py:26
  169.0 4.8 %collective-permute-start.67 = (f32[64,256]{1,0:T(8,128)S(1)}, f32[64,256]{1,0:T(8,128)S(1)}, u32[]{:S(2)}, u32[]{:S(2)}) collective-permute-start(f32[64,256]{1,0:T(8,128)S(1)} %full_product.8.refs_1_), channel_id=1, source_target_pairs={{0,96},{32,0},{64,32},{96,64},{1,97},{33,1},{65,33},{97,65},{2,98}... | collective-permute-start | bytes 196616 | tf_op jit(solution)/shard_map/ppermute | solution.py:26
  177.6 6.7 %collective-permute-start.73 = (f32[1,64,128]{2,1,0:T(8,128)S(1)}, f32[1,64,128]{2,1,0:T(8,128)S(1)}, u32[]{:S(2)}, u32[]{:S(2)}) collective-permute-start(f32[1,64,128]{2,1,0:T(8,128)S(1)} %get-tuple-element.77), channel_id=1, source_target_pairs={{0,0},{1,1},{2,16},{3,17},{4,32},{5,33},{6,48},{7,49},{8,64},{9,65... | collective-permute-start | bytes 98312 | tf_op jit(solution)/shard_map/ppermute | solution.py:186
  184.3 13.3 %collective-permute-start.74 = (f32[1,128,128]{2,1,0:T(8,128)S(1)}, f32[1,128,128]{2,1,0:T(8,128)S(1)}, u32[]{:S(2)}, u32[]{:S(2)}) collective-permute-start(f32[1,128,128]{2,1,0:T(8,128)S(1)} %pad_maximum_fusion.6.refs_0_), channel_id=1, source_target_pairs={{0,32},{32,64},{64,96},{96,0},{1,33},{33,65},{65,97},{97,1},{2,34}... | collective-permute-start | bytes 196616 | tf_op jit(solution)/shard_map/ppermute | solution.py:22
  187.8 10.3 %collective-permute-start.75 = (f32[1,128,128]{2,1,0:T(8,128)S(1)}, f32[1,128,128]{2,1,0:T(8,128)S(1)}, u32[]{:S(2)}, u32[]{:S(2)}) collective-permute-start(f32[1,128,128]{2,1,0:T(8,128)S(1)} %pad_maximum_fusion.6.refs_0_), channel_id=1, source_target_pairs={{0,64},{32,96},{64,0},{96,32},{1,65},{33,97},{65,1},{97,33},{2,66}... | collective-permute-start | bytes 196616 | tf_op jit(solution)/shard_map/ppermute | solution.py:22
  (41 other events, 187.5 us)
Sparse Core Ops, SparseCore 0:
  10.4 78.4 all-gather.4
  91.6 69.8 all-gather.6
  216.1 93.0 reduce-scatter.3

commit v4 on v3

--- a/solution.py
+++ b/solution.py
@@ -180,12 +180,15 @@
 
 
 def spread(blocks):
-    n = blocks.shape[0]
     odd = lax.axis_index("y") % 2 == 1
     low, high = blocks[:, :, :128], blocks[:, :, 128:]
     same = lax.ppermute(jnp.where(odd, high, low), ALL, spread_to(0))
     cross = lax.ppermute(jnp.where(odd, low, high), ALL, spread_to(1))
-    gathered = row_gather(jnp.concatenate([jnp.where(odd, cross, same), jnp.where(odd, same, cross)], axis=1))
+    return row_gather(jnp.concatenate([jnp.where(odd, cross, same), jnp.where(odd, same, cross)], axis=1))
+
+
+def split_rows(gathered):
+    n = gathered[0].shape[0]
 
     def kernel(*refs):
         out = refs[-1]
@@ -248,10 +251,10 @@
     early = spread(jnp.stack([first, second, third]))
     early, far = lax.optimization_barrier((early, far))
     reduced = full_product(bases[2], [(fetch(far, 0), gathered_second), (fetch(far, 1), gathered)])
-    gathered, block = row_gather_beside(reduced, fetch(far, 2))
+    gathered, (block, early) = row_gather_beside(reduced, (fetch(far, 2), split_rows(early)))
     fourth = full_product(None, [(block, gathered)])
 
-    partial = trailing_product(trailing_factor.reshape(12, 1024, 128), early, spread(fourth[None]))
+    partial = trailing_product(trailing_factor.reshape(12, 1024, 128), early, split_rows(spread(fourth[None])))
     updated = jnp.transpose(trailing_columns, (0, 2, 1)) - lax.psum_scatter(partial, COL, scatter_dimension=0)
 
     whitened_t = jnp.stack([first, second, third, fourth])

time: 319 us -> 320 us (level)
  no operation moved by 1% of the time
where the time goes in v4:
time: 320 us; the launch traced here: 319 us
  waiting for transfers between devices  135 us (42%)
  starting transfers between devices  118 us (37%)
  Pallas kernels  30.6 us (10%)
  between operations  14.2 us (4%)
  blocking collectives  12.4 us (4%)
  other arithmetic  5.21 us (2%)
  local copies, waits for them, and re-layouts  4.23 us (1%)
    unnamed x4, waiting for transfers between devices  80.6 us
    ppermute x24, starting transfers between devices, both_cores(): return pieces + [lax.ppermute(piece, 'core', SWAP) for piece in pieces]  26.4 us
    ppermute x12, starting transfers between devices, row_gather(): lax.ppermute(block, 'x', RING[s])  23.7 us
    ppermute x8, starting transfers between devices, slab_gather(): return both_cores([lax.ppermute(block, ALL, turned(s)) for s in range(4)])  21.1 us
    pallas_call x1, Pallas kernels, trailing_product(): pl.pallas_call(kernel, grid=(6,), out_shape=jax.ShapeDtypeStruct((16, 12,...  14.9 us
    psum x1, blocking collectives, shards(): variance_drop = lax.psum(local_squares, ROW) / 8192  12.4 us
    ppermute x6, waiting for transfers between devices, z_sum(): total = total + lax.ppermute(parts[t], 'z', RING[t])  11.4 us
    ppermute x6, starting transfers between devices, z_sum(): total = total + lax.ppermute(parts[t], 'z', RING[t])  11.1 us
  transfers between devices with their start and end apart: 84, of which 36 were waited for; matrix products, arithmetic and copies ran while one was open for 1% of the time, Pallas kernels for 3%

profile of v4, /device:TPU:1, one launch (start us, length us, event | category | flops | bytes accessed | tf_op | source)
XLA Modules:
  0.0 319.4 jit_solution(17895455722364980520)
XLA Ops:
  11.3 2.1 collective-permute-start.6
  15.4 2.6 collective-permute-start.1
  18.0 7.1 %collective-permute-start.4 = (f32[64,256]{1,0:T(8,128)S(1)}, f32[64,256]{1,0:T(8,128)S(1)}, u32[]{:S(2)}, u32[]{:S(2)}) collective-permute-start(f32[64,256]{1,0:T(8,128)S(1)} %slice_bitcast_fusion.3), channel_id=1, source_target_pairs={{0,96},{1,97},{2,98},{3,99},{4,0},{5,1},{6,2},{7,3},{8,32},{9,33},... | collective-permute-start | bytes 196616 | tf_op jit(solution)/shard_map/ppermute | solution.py:44
  25.1 1.6 collective-permute-start.5
  27.8 2.6 collective-permute-start.10
  30.8 1.9 collective-permute-start.7
  34.6 7.0 %collective-permute-start.12 = (f32[1,64,256]{2,1,0:T(8,128)S(1)}, f32[1,64,256]{2,1,0:T(8,128)S(1)}, u32[]{:S(2)}, u32[]{:S(2)}) collective-permute-start(f32[1,64,256]{2,1,0:T(8,128)S(1)} %get-tuple-element.40), channel_id=1, source_target_pairs={{0,8},{4,12},{8,0},{12,4},{1,9},{5,13},{9,1},{13,5},{2,10},{6,14},... | collective-permute-start | bytes 196616 | tf_op jit(solution)/shard_map/ppermute | solution.py:54
  45.8 5.7 %collective-permute-start.18 = (f32[64,256]{1,0:T(8,128)S(1)}, f32[64,256]{1,0:T(8,128)S(1)}, u32[]{:S(2)}, u32[]{:S(2)}) collective-permute-start(f32[64,256]{1,0:T(8,128)S(1)} %add_bitcast_fusion), channel_id=1, source_target_pairs={{0,96},{1,97},{2,98},{3,99},{4,0},{5,1},{6,2},{7,3},{8,32},{9,33},... | collective-permute-start | bytes 196616 | tf_op jit(solution)/shard_map/ppermute | solution.py:44
  51.5 1.8 collective-permute-start.19
  54.8 3.7 %collective-permute-done.19.refs_6_ = f32[64,256]{1,0:T(8,128)S(1)} collective-permute-done((f32[64,256]{1,0:T(8,128)S(1)}, f32[64,256]{1,0:T(8,128)S(1)}, u32[]{:S(2)}, u32[]{:S(2)}) %collective-permute-start.19) | collective-permute-done | bytes 65568 | tf_op jit(solution)/shard_map/ppermute | solution.py:44
  58.5 4.8 %collective-permute-start.21 = (f32[64,256]{1,0:T(8,128)S(1)}, f32[64,256]{1,0:T(8,128)S(1)}, u32[]{:S(2)}, u32[]{:S(2)}) collective-permute-start(f32[64,256]{1,0:T(8,128)S(1)} %collective-permute-done.17.refs_4_), channel_id=1, source_target_pairs={{0,16},{16,0},{1,17},{17,1},{2,18},{18,2},{3,19},{19,3},{4,20},{20... | collective-permute-start | bytes 196616 | tf_op jit(solution)/shard_map/ppermute | solution.py:18
  63.3 3.6 %collective-permute-start.22 = (f32[64,256]{1,0:T(8,128)S(1)}, f32[64,256]{1,0:T(8,128)S(1)}, u32[]{:S(2)}, u32[]{:S(2)}) collective-permute-start(f32[64,256]{1,0:T(8,128)S(1)} %collective-permute-done.18.refs_5_), channel_id=1, source_target_pairs={{0,16},{16,0},{1,17},{17,1},{2,18},{18,2},{3,19},{19,3},{4,20},{20... | collective-permute-start | bytes 196616 | tf_op jit(solution)/shard_map/ppermute | solution.py:18
  69.0 3.9 %collective-permute-done.16.refs_3_ = f32[3,256,128]{2,1,0:T(8,128)S(1)} collective-permute-done((f32[3,256,128]{2,1,0:T(8,128)S(1)}, f32[3,256,128]{2,1,0:T(8,128)S(1)}, u32[]{:S(2)}, u32[]{:S(2)}) %collective-permute-start.16) | collective-permute-done | bytes 393248 | tf_op jit(solution)/shard_map/ppermute | solution.py:48
  73.8 1.5 collective-permute-start.25
  75.4 2.5 collective-permute-start.27
  77.9 7.5 %collective-permute-done.25 = f32[3,64,256]{2,1,0:T(8,128)S(1)} collective-permute-done((f32[3,64,256]{2,1,0:T(8,128)S(1)}, f32[3,64,256]{2,1,0:T(8,128)S(1)}, u32[]{:S(2)}, u32[]{:S(2)}) %collective-permute-start.25) | collective-permute-done | bytes 196640 | tf_op jit(solution)/shard_map/ppermute | solution.py:54
  85.4 2.4 collective-permute-done.26
  89.0 2.4 collective-permute-start.30
  91.4 3.3 %collective-permute-start.31 = (f32[64,256]{1,0:T(8,128)S(1)}, f32[64,256]{1,0:T(8,128)S(1)}, u32[]{:S(2)}, u32[]{:S(2)}) collective-permute-start(f32[64,256]{1,0:T(8,128)S(1)} %get-tuple-element.85.refs_1_), channel_id=1, source_target_pairs={{0,16},{16,0},{1,17},{17,1},{2,18},{18,2},{3,19},{19,3},{4,20},{20... | collective-permute-start | bytes 196616 | tf_op jit(solution)/shard_map/ppermute | solution.py:18
  94.8 2.9 collective-permute-start.32
  98.6 1.5 fetch.6.refs_0_
  102.1 2.2 collective-permute-start.36
  104.6 1.5 fetch.7.refs_0_
  111.4 2.7 collective-permute-start.43
  114.8 1.5 fetch.8.refs_0_
  121.6 2.6 collective-permute-start.50
  125.7 1.6 collective-permute-start.53
  130.3 3.0 collective-permute-start.56
  133.3 1.9 collective-permute-start.57
  135.2 6.1 %collective-permute-done.56 = f32[3,64,128]{2,1,0:T(8,128)S(1)} collective-permute-done((f32[3,64,128]{2,1,0:T(8,128)S(1)}, f32[3,64,128]{2,1,0:T(8,128)S(1)}, u32[]{:S(2)}, u32[]{:S(2)}) %collective-permute-start.56) | collective-permute-done | bytes 98336 | tf_op jit(solution)/shard_map/ppermute | solution.py:186
  141.4 6.4 %collective-permute-done.57 = f32[3,64,128]{2,1,0:T(8,128)S(1)} collective-permute-done((f32[3,64,128]{2,1,0:T(8,128)S(1)}, f32[3,64,128]{2,1,0:T(8,128)S(1)}, u32[]{:S(2)}, u32[]{:S(2)}) %collective-permute-start.57) | collective-permute-done | bytes 98336 | tf_op jit(solution)/shard_map/ppermute | solution.py:185
  147.9 3.0 collective-permute-start.59
  151.9 3.4 %collective-permute-done.58.refs_1_ = f32[3,128,128]{2,1,0:T(8,128)S(1)} collective-permute-done((f32[3,128,128]{2,1,0:T(8,128)S(1)}, f32[3,128,128]{2,1,0:T(8,128)S(1)}, u32[]{:S(2)}, u32[]{:S(2)}) %collective-permute-start.58) | collective-permute-done | bytes 196640 | tf_op jit(solution)/shard_map/ppermute | solution.py:22
  155.3 3.2 collective-permute-done.59.refs_2_
  159.0 2.5 all-gather.7.cloned.1.call-done
  161.5 1.6 fetch.9.refs_0_
  163.1 1.6 fetch.10.refs_9_
  168.9 1.5 fetch.11.refs_0_
  175.7 2.4 collective-permute-start.72
  178.1 2.7 collective-permute-start.73
  180.8 4.0 %collective-permute-done.73 = f32[1,64,128]{2,1,0:T(8,128)S(1)} collective-permute-done((f32[1,64,128]{2,1,0:T(8,128)S(1)}, f32[1,64,128]{2,1,0:T(8,128)S(1)}, u32[]{:S(2)}, u32[]{:S(2)}) %collective-permute-start.73) | collective-permute-done | bytes 32800 | tf_op jit(solution)/shard_map/ppermute | solution.py:185
  184.9 3.7 %collective-permute-start.74 = (f32[1,128,128]{2,1,0:T(8,128)S(1)}, f32[1,128,128]{2,1,0:T(8,128)S(1)}, u32[]{:S(2)}, u32[]{:S(2)}) collective-permute-start(f32[1,128,128]{2,1,0:T(8,128)S(1)} %pad_maximum_fusion.6.refs_0_), channel_id=1, source_target_pairs={{0,32},{32,64},{64,96},{96,0},{1,33},{33,65},{65,97},{97,1},{2,34}... | collective-permute-start | bytes 196616 | tf_op jit(solution)/shard_map/ppermute | solution.py:22
  188.6 7.5 %collective-permute-start.75 = (f32[1,128,128]{2,1,0:T(8,128)S(1)}, f32[1,128,128]{2,1,0:T(8,128)S(1)}, u32[]{:S(2)}, u32[]{:S(2)}) collective-permute-start(f32[1,128,128]{2,1,0:T(8,128)S(1)} %pad_maximum_fusion.6.refs_0_), channel_id=1, source_target_pairs={{0,64},{32,96},{64,0},{96,32},{1,65},{33,97},{65,1},{97,33},{2,66}... | collective-permute-start | bytes 196616 | tf_op jit(solution)/shard_map/ppermute | solution.py:22
  196.1 2.0 collective-permute-start.76
  201.5 14.9 %trailing_product.1 = f32[16,12,64,256]{3,2,1,0:T(8,128)} custom-call(f32[12,1024,128]{2,1,0:T(8,128)} %bitcast.45, bf16[1024,768]{1,0:T(8,128)(2,1)} %copy-done, bf16[1024,256]{1,0:T(8,128)(2,1)} %copy-done.1), custom_call_target="tpu_custom_call" | custom-call | flops 9663676416 | bytes 20971520 | tf_op jit(solution)/shard_map/trailing_product/pallas_call | solution.py:218
  217.2 12.4 %psum.7 = f32[64]{0:T(128)S(1)} all-reduce(f32[64]{0:T(128)S(1)} %get-tuple-element.81), channel_id=1, replica_groups=mesh['x'=4,'core'=2,'z'=4,'y'=4] {'x','core'}, use_global_device_ids=true, to_apply=%region_2.3 | all-reduce | flops 64 | bytes 512 | tf_op jit(solution)/shard_map/psum | solution.py:262
  230.1 80.6 %reduce-scatter.4.cloned.1.call-done = f32[1,12,64,256]{3,2,1,0:T(8,128)} async-done(((f32[16,12,64,256]{3,2,1,0:T(8,128)}), f32[1,12,64,256]{3,2,1,0:T(8,128)}) %reduce-scatter.4.cloned.1.call-update) | async-done | bytes 786448
  310.7 2.1 fusion
  (170 shorter events, 53.9 us)
Async XLA Ops:
  7.2 91.4 %all-gather.5.cloned.1.call-start = ((), (), s32[]{:S(2)}) async-start(), calls=%async_computation.1 | async-start | bytes 6684672 | tf_op jit(solution)/shard_map/all_gather | solution.py:239
  10.3 151.2 %all-gather.7.cloned.1.call-start = ((), (), s32[]{:S(2)}) async-start(), calls=%async_computation.2 | async-start | bytes 6684672 | tf_op jit(solution)/shard_map/all_gather | solution.py:240
  11.2 299.5 %reduce-scatter.4.cloned.1.call-start = ((), (), s32[]{:S(2)}) async-start(), calls=%async_computation.3 | async-start | bytes 13369344
  11.3 13.9 %collective-permute-start.6 = (f32[64,256]{1,0:T(8,128)S(1)}, f32[64,256]{1,0:T(8,128)S(1)}, u32[]{:S(2)}, u32[]{:S(2)}) collective-permute-start(f32[64,256]{1,0:T(8,128)S(1)} %slice_bitcast_fusion.3), channel_id=1, source_target_pairs={{0,32},{1,33},{2,34},{3,35},{4,64},{5,65},{6,66},{7,67},{8,96},{9,... | collective-permute-start | bytes 196616 | tf_op jit(solution)/shard_map/ppermute | solution.py:44
  13.4 13.3 %collective-permute-start.3 = (f32[64,256]{1,0:T(8,128)S(1)}, f32[64,256]{1,0:T(8,128)S(1)}, u32[]{:S(2)}, u32[]{:S(2)}) collective-permute-start(f32[64,256]{1,0:T(8,128)S(1)} %slice_bitcast_fusion.3), channel_id=1, source_target_pairs={{0,0},{1,1},{2,2},{3,3},{4,32},{5,33},{6,34},{7,35},{8,64},{9,65},... | collective-permute-start | bytes 196616 | tf_op jit(solution)/shard_map/ppermute | solution.py:44
  14.0 18.7 %collective-permute-start = (f32[1,256,128]{2,1,0:T(8,128)S(1)}, f32[1,256,128]{2,1,0:T(8,128)S(1)}, u32[]{:S(2)}, u32[]{:S(2)}) collective-permute-start(f32[1,256,128]{2,1,0:T(8,128)S(1)} %get-tuple-element.79.refs_0_), channel_id=1, source_target_pairs={{0,1},{1,2},{2,3},{3,0},{4,5},{5,6},{6,7},{7,4},{8,9},{9,10},{10,1... | collective-permute-start | bytes 393224 | tf_op jit(solution)/shard_map/ppermute | solution.py:48
  15.4 17.3 %collective-permute-start.1 = (f32[1,256,128]{2,1,0:T(8,128)S(1)}, f32[1,256,128]{2,1,0:T(8,128)S(1)}, u32[]{:S(2)}, u32[]{:S(2)}) collective-permute-start(f32[1,256,128]{2,1,0:T(8,128)S(1)} %get-tuple-element.79.refs_0_), channel_id=1, source_target_pairs={{0,2},{1,3},{2,0},{3,1},{4,6},{5,7},{6,4},{7,5},{8,10},{9,11},{10,... | collective-permute-start | bytes 393224 | tf_op jit(solution)/shard_map/ppermute | solution.py:48
  18.0 9.8 %collective-permute-start.4 = (f32[64,256]{1,0:T(8,128)S(1)}, f32[64,256]{1,0:T(8,128)S(1)}, u32[]{:S(2)}, u32[]{:S(2)}) collective-permute-start(f32[64,256]{1,0:T(8,128)S(1)} %slice_bitcast_fusion.3), channel_id=1, source_target_pairs={{0,96},{1,97},{2,98},{3,99},{4,0},{5,1},{6,2},{7,3},{8,32},{9,33},... | collective-permute-start | bytes 196616 | tf_op jit(solution)/shard_map/ppermute | solution.py:44
  25.1 5.7 %collective-permute-start.5 = (f32[64,256]{1,0:T(8,128)S(1)}, f32[64,256]{1,0:T(8,128)S(1)}, u32[]{:S(2)}, u32[]{:S(2)}) collective-permute-start(f32[64,256]{1,0:T(8,128)S(1)} %slice_bitcast_fusion.3), channel_id=1, source_target_pairs={{0,64},{1,65},{2,66},{3,67},{4,96},{5,97},{6,98},{7,99},{8,0},{9,1... | collective-permute-start | bytes 196616 | tf_op jit(solution)/shard_map/ppermute | solution.py:44
  26.7 6.5 %collective-permute-start.2 = (f32[1,256,128]{2,1,0:T(8,128)S(1)}, f32[1,256,128]{2,1,0:T(8,128)S(1)}, u32[]{:S(2)}, u32[]{:S(2)}) collective-permute-start(f32[1,256,128]{2,1,0:T(8,128)S(1)} %get-tuple-element.79.refs_0_), channel_id=1, source_target_pairs={{0,3},{1,0},{2,1},{3,2},{4,7},{5,4},{6,5},{7,6},{8,11},{9,8},{10,9... | collective-permute-start | bytes 393224 | tf_op jit(solution)/shard_map/ppermute | solution.py:48
  27.8 5.5 %collective-permute-start.10 = (f32[64,256]{1,0:T(8,128)S(1)}, f32[64,256]{1,0:T(8,128)S(1)}, u32[]{:S(2)}, u32[]{:S(2)}) collective-permute-start(f32[64,256]{1,0:T(8,128)S(1)} %collective-permute-done.6.refs_7_), channel_id=1, source_target_pairs={{0,16},{16,0},{1,17},{17,1},{2,18},{18,2},{3,19},{19,3},{4,20},{20... | collective-permute-start | bytes 196616 | tf_op jit(solution)/shard_map/ppermute | solution.py:18
  34.6 8.8 %collective-permute-start.11 = (f32[1,64,256]{2,1,0:T(8,128)S(1)}, f32[1,64,256]{2,1,0:T(8,128)S(1)}, u32[]{:S(2)}, u32[]{:S(2)}) collective-permute-start(f32[1,64,256]{2,1,0:T(8,128)S(1)} %get-tuple-element.39), channel_id=1, source_target_pairs={{0,4},{4,8},{8,12},{12,0},{1,5},{5,9},{9,13},{13,1},{2,6},{6,10},{... | collective-permute-start | bytes 196616 | tf_op jit(solution)/shard_map/ppermute | solution.py:54
  34.6 10.0 %collective-permute-start.12 = (f32[1,64,256]{2,1,0:T(8,128)S(1)}, f32[1,64,256]{2,1,0:T(8,128)S(1)}, u32[]{:S(2)}, u32[]{:S(2)}) collective-permute-start(f32[1,64,256]{2,1,0:T(8,128)S(1)} %get-tuple-element.40), channel_id=1, source_target_pairs={{0,8},{4,12},{8,0},{12,4},{1,9},{5,13},{9,1},{13,5},{2,10},{6,14},... | collective-permute-start | bytes 196616 | tf_op jit(solution)/shard_map/ppermute | solution.py:54
  41.7 27.3 %collective-permute-start.14 = (f32[3,256,128]{2,1,0:T(8,128)S(1)}, f32[3,256,128]{2,1,0:T(8,128)S(1)}, u32[]{:S(2)}, u32[]{:S(2)}) collective-permute-start(f32[3,256,128]{2,1,0:T(8,128)S(1)} %pad_maximum_fusion.1.refs_0_), channel_id=1, source_target_pairs={{0,1},{1,2},{2,3},{3,0},{4,5},{5,6},{6,7},{7,4},{8,9},{9,10},{10,1... | collective-permute-start | bytes 1179656 | tf_op jit(solution)/shard_map/ppermute | solution.py:48
  41.8 27.2 %collective-permute-start.15 = (f32[3,256,128]{2,1,0:T(8,128)S(1)}, f32[3,256,128]{2,1,0:T(8,128)S(1)}, u32[]{:S(2)}, u32[]{:S(2)}) collective-permute-start(f32[3,256,128]{2,1,0:T(8,128)S(1)} %pad_maximum_fusion.1.refs_0_), channel_id=1, source_target_pairs={{0,2},{1,3},{2,0},{3,1},{4,6},{5,7},{6,4},{7,5},{8,10},{9,11},{10,... | collective-permute-start | bytes 1179656 | tf_op jit(solution)/shard_map/ppermute | solution.py:48
  43.3 29.6 %collective-permute-start.16 = (f32[3,256,128]{2,1,0:T(8,128)S(1)}, f32[3,256,128]{2,1,0:T(8,128)S(1)}, u32[]{:S(2)}, u32[]{:S(2)}) collective-permute-start(f32[3,256,128]{2,1,0:T(8,128)S(1)} %pad_maximum_fusion.1.refs_0_), channel_id=1, source_target_pairs={{0,3},{1,0},{2,1},{3,2},{4,7},{5,4},{6,5},{7,6},{8,11},{9,8},{10,9... | collective-permute-start | bytes 1179656 | tf_op jit(solution)/shard_map/ppermute | solution.py:48
  45.1 6.4 %collective-permute-start.17 = (f32[64,256]{1,0:T(8,128)S(1)}, f32[64,256]{1,0:T(8,128)S(1)}, u32[]{:S(2)}, u32[]{:S(2)}) collective-permute-start(f32[64,256]{1,0:T(8,128)S(1)} %add_bitcast_fusion), channel_id=1, source_target_pairs={{0,0},{1,1},{2,2},{3,3},{4,32},{5,33},{6,34},{7,35},{8,64},{9,65},... | collective-permute-start | bytes 196616 | tf_op jit(solution)/shard_map/ppermute | solution.py:44
  45.8 7.5 %collective-permute-start.18 = (f32[64,256]{1,0:T(8,128)S(1)}, f32[64,256]{1,0:T(8,128)S(1)}, u32[]{:S(2)}, u32[]{:S(2)}) collective-permute-start(f32[64,256]{1,0:T(8,128)S(1)} %add_bitcast_fusion), channel_id=1, source_target_pairs={{0,96},{1,97},{2,98},{3,99},{4,0},{5,1},{6,2},{7,3},{8,32},{9,33},... | collective-permute-start | bytes 196616 | tf_op jit(solution)/shard_map/ppermute | solution.py:44
  51.5 7.0 %collective-permute-start.19 = (f32[64,256]{1,0:T(8,128)S(1)}, f32[64,256]{1,0:T(8,128)S(1)}, u32[]{:S(2)}, u32[]{:S(2)}) collective-permute-start(f32[64,256]{1,0:T(8,128)S(1)} %add_bitcast_fusion), channel_id=1, source_target_pairs={{0,64},{1,65},{2,66},{3,67},{4,96},{5,97},{6,98},{7,99},{8,0},{9,1... | collective-permute-start | bytes 196616 | tf_op jit(solution)/shard_map/ppermute | solution.py:44
  53.3 10.0 %collective-permute-start.20 = (f32[64,256]{1,0:T(8,128)S(1)}, f32[64,256]{1,0:T(8,128)S(1)}, u32[]{:S(2)}, u32[]{:S(2)}) collective-permute-start(f32[64,256]{1,0:T(8,128)S(1)} %add_bitcast_fusion), channel_id=1, source_target_pairs={{0,32},{1,33},{2,34},{3,35},{4,64},{5,65},{6,66},{7,67},{8,96},{9,... | collective-permute-start | bytes 196616 | tf_op jit(solution)/shard_map/ppermute | solution.py:44
  58.5 8.4 %collective-permute-start.21 = (f32[64,256]{1,0:T(8,128)S(1)}, f32[64,256]{1,0:T(8,128)S(1)}, u32[]{:S(2)}, u32[]{:S(2)}) collective-permute-start(f32[64,256]{1,0:T(8,128)S(1)} %collective-permute-done.17.refs_4_), channel_id=1, source_target_pairs={{0,16},{16,0},{1,17},{17,1},{2,18},{18,2},{3,19},{19,3},{4,20},{20... | collective-permute-start | bytes 196616 | tf_op jit(solution)/shard_map/ppermute | solution.py:18
  73.8 11.6 %collective-permute-start.25 = (f32[3,64,256]{2,1,0:T(8,128)S(1)}, f32[3,64,256]{2,1,0:T(8,128)S(1)}, u32[]{:S(2)}, u32[]{:S(2)}) collective-permute-start(f32[3,64,256]{2,1,0:T(8,128)S(1)} %get-tuple-element.43), channel_id=1, source_target_pairs={{0,4},{4,8},{8,12},{12,0},{1,5},{5,9},{9,13},{13,1},{2,6},{6,10},{... | collective-permute-start | bytes 589832 | tf_op jit(solution)/shard_map/ppermute | solution.py:54
  75.4 12.5 %collective-permute-start.26 = (f32[3,64,256]{2,1,0:T(8,128)S(1)}, f32[3,64,256]{2,1,0:T(8,128)S(1)}, u32[]{:S(2)}, u32[]{:S(2)}) collective-permute-start(f32[3,64,256]{2,1,0:T(8,128)S(1)} %get-tuple-element.44), channel_id=1, source_target_pairs={{0,8},{4,12},{8,0},{12,4},{1,9},{5,13},{9,1},{13,5},{2,10},{6,14},... | collective-permute-start | bytes 589832 | tf_op jit(solution)/shard_map/ppermute | solution.py:54
  75.4 13.2 %collective-permute-start.27 = (f32[3,64,256]{2,1,0:T(8,128)S(1)}, f32[3,64,256]{2,1,0:T(8,128)S(1)}, u32[]{:S(2)}, u32[]{:S(2)}) collective-permute-start(f32[3,64,256]{2,1,0:T(8,128)S(1)} %get-tuple-element.45), channel_id=1, source_target_pairs={{0,12},{4,0},{8,4},{12,8},{1,13},{5,1},{9,5},{13,9},{2,14},{6,2},{... | collective-permute-start | bytes 589832 | tf_op jit(solution)/shard_map/ppermute | solution.py:54
  88.7 6.1 %collective-permute-start.28 = (f32[64,256]{1,0:T(8,128)S(1)}, f32[64,256]{1,0:T(8,128)S(1)}, u32[]{:S(2)}, u32[]{:S(2)}) collective-permute-start(f32[64,256]{1,0:T(8,128)S(1)} %get-tuple-element.85.refs_1_), channel_id=1, source_target_pairs={{0,32},{32,64},{64,96},{96,0},{1,33},{33,65},{65,97},{97,1},{2,34}... | collective-permute-start | bytes 196616 | tf_op jit(solution)/shard_map/ppermute | solution.py:22
  88.8 8.9 %collective-permute-start.29 = (f32[64,256]{1,0:T(8,128)S(1)}, f32[64,256]{1,0:T(8,128)S(1)}, u32[]{:S(2)}, u32[]{:S(2)}) collective-permute-start(f32[64,256]{1,0:T(8,128)S(1)} %get-tuple-element.85.refs_1_), channel_id=1, source_target_pairs={{0,64},{32,96},{64,0},{96,32},{1,65},{33,97},{65,1},{97,33},{2,66}... | collective-permute-start | bytes 196616 | tf_op jit(solution)/shard_map/ppermute | solution.py:22
  89.0 8.7 %collective-permute-start.30 = (f32[64,256]{1,0:T(8,128)S(1)}, f32[64,256]{1,0:T(8,128)S(1)}, u32[]{:S(2)}, u32[]{:S(2)}) collective-permute-start(f32[64,256]{1,0:T(8,128)S(1)} %get-tuple-element.85.refs_1_), channel_id=1, source_target_pairs={{0,96},{32,0},{64,32},{96,64},{1,97},{33,1},{65,33},{97,65},{2,98}... | collective-permute-start | bytes 196616 | tf_op jit(solution)/shard_map/ppermute | solution.py:22
  91.4 8.7 %collective-permute-start.31 = (f32[64,256]{1,0:T(8,128)S(1)}, f32[64,256]{1,0:T(8,128)S(1)}, u32[]{:S(2)}, u32[]{:S(2)}) collective-permute-start(f32[64,256]{1,0:T(8,128)S(1)} %get-tuple-element.85.refs_1_), channel_id=1, source_target_pairs={{0,16},{16,0},{1,17},{17,1},{2,18},{18,2},{3,19},{19,3},{4,20},{20... | collective-permute-start | bytes 196616 | tf_op jit(solution)/shard_map/ppermute | solution.py:18
  94.8 5.4 %collective-permute-start.32 = (f32[64,256]{1,0:T(8,128)S(1)}, f32[64,256]{1,0:T(8,128)S(1)}, u32[]{:S(2)}, u32[]{:S(2)}) collective-permute-start(f32[64,256]{1,0:T(8,128)S(1)} %collective-permute-done.28.refs_2_), channel_id=1, source_target_pairs={{0,16},{16,0},{1,17},{17,1},{2,18},{18,2},{3,19},{19,3},{4,20},{20... | collective-permute-start | bytes 196616 | tf_op jit(solution)/shard_map/ppermute | solution.py:18
  101.0 5.8 %collective-permute-start.35 = (f32[64,256]{1,0:T(8,128)S(1)}, f32[64,256]{1,0:T(8,128)S(1)}, u32[]{:S(2)}, u32[]{:S(2)}) collective-permute-start(f32[64,256]{1,0:T(8,128)S(1)} %full_product.5.refs_1_), channel_id=1, source_target_pairs={{0,32},{32,64},{64,96},{96,0},{1,33},{33,65},{65,97},{97,1},{2,34}... | collective-permute-start | bytes 196616 | tf_op jit(solution)/shard_map/ppermute | solution.py:26
  102.1 5.7 %collective-permute-start.36 = (f32[64,256]{1,0:T(8,128)S(1)}, f32[64,256]{1,0:T(8,128)S(1)}, u32[]{:S(2)}, u32[]{:S(2)}) collective-permute-start(f32[64,256]{1,0:T(8,128)S(1)} %full_product.5.refs_1_), channel_id=1, source_target_pairs={{0,64},{32,96},{64,0},{96,32},{1,65},{33,97},{65,1},{97,33},{2,66}... | collective-permute-start | bytes 196616 | tf_op jit(solution)/shard_map/ppermute | solution.py:26
  111.1 6.4 %collective-permute-start.42 = (f32[64,256]{1,0:T(8,128)S(1)}, f32[64,256]{1,0:T(8,128)S(1)}, u32[]{:S(2)}, u32[]{:S(2)}) collective-permute-start(f32[64,256]{1,0:T(8,128)S(1)} %full_product.6.refs_1_), channel_id=1, source_target_pairs={{0,32},{32,64},{64,96},{96,0},{1,33},{33,65},{65,97},{97,1},{2,34}... | collective-permute-start | bytes 196616 | tf_op jit(solution)/shard_map/ppermute | solution.py:26
  111.4 6.2 %collective-permute-start.43 = (f32[64,256]{1,0:T(8,128)S(1)}, f32[64,256]{1,0:T(8,128)S(1)}, u32[]{:S(2)}, u32[]{:S(2)}) collective-permute-start(f32[64,256]{1,0:T(8,128)S(1)} %full_product.6.refs_1_), channel_id=1, source_target_pairs={{0,64},{32,96},{64,0},{96,32},{1,65},{33,97},{65,1},{97,33},{2,66}... | collective-permute-start | bytes 196616 | tf_op jit(solution)/shard_map/ppermute | solution.py:26
  121.6 5.7 %collective-permute-start.50 = (f32[64,256]{1,0:T(8,128)S(1)}, f32[64,256]{1,0:T(8,128)S(1)}, u32[]{:S(2)}, u32[]{:S(2)}) collective-permute-start(f32[64,256]{1,0:T(8,128)S(1)} %full_product.7.refs_10_), channel_id=1, source_target_pairs={{0,64},{32,96},{64,0},{96,32},{1,65},{33,97},{65,1},{97,33},{2,66}... | collective-permute-start | bytes 196616 | tf_op jit(solution)/shard_map/ppermute | solution.py:22
  130.3 11.0 %collective-permute-start.56 = (f32[3,64,128]{2,1,0:T(8,128)S(1)}, f32[3,64,128]{2,1,0:T(8,128)S(1)}, u32[]{:S(2)}, u32[]{:S(2)}) collective-permute-start(f32[3,64,128]{2,1,0:T(8,128)S(1)} %get-tuple-element.88), channel_id=1, source_target_pairs={{0,1},{1,0},{2,17},{3,16},{4,33},{5,32},{6,49},{7,48},{8,65},{9,64... | collective-permute-start | bytes 294920 | tf_op jit(solution)/shard_map/ppermute | solution.py:186
  133.3 14.4 %collective-permute-start.57 = (f32[3,64,128]{2,1,0:T(8,128)S(1)}, f32[3,64,128]{2,1,0:T(8,128)S(1)}, u32[]{:S(2)}, u32[]{:S(2)}) collective-permute-start(f32[3,64,128]{2,1,0:T(8,128)S(1)} %get-tuple-element.89), channel_id=1, source_target_pairs={{0,0},{1,1},{2,16},{3,17},{4,32},{5,33},{6,48},{7,49},{8,64},{9,65... | collective-permute-start | bytes 294920 | tf_op jit(solution)/shard_map/ppermute | solution.py:185
  147.8 7.5 %collective-permute-start.58 = (f32[3,128,128]{2,1,0:T(8,128)S(1)}, f32[3,128,128]{2,1,0:T(8,128)S(1)}, u32[]{:S(2)}, u32[]{:S(2)}) collective-permute-start(f32[3,128,128]{2,1,0:T(8,128)S(1)} %pad_maximum_fusion.5.refs_0_), channel_id=1, source_target_pairs={{0,32},{32,64},{64,96},{96,0},{1,33},{33,65},{65,97},{97,1},{2,34}... | collective-permute-start | bytes 589832 | tf_op jit(solution)/shard_map/ppermute | solution.py:22
  147.9 10.6 %collective-permute-start.59 = (f32[3,128,128]{2,1,0:T(8,128)S(1)}, f32[3,128,128]{2,1,0:T(8,128)S(1)}, u32[]{:S(2)}, u32[]{:S(2)}) collective-permute-start(f32[3,128,128]{2,1,0:T(8,128)S(1)} %pad_maximum_fusion.5.refs_0_), channel_id=1, source_target_pairs={{0,64},{32,96},{64,0},{96,32},{1,65},{33,97},{65,1},{97,33},{2,66}... | collective-permute-start | bytes 589832 | tf_op jit(solution)/shard_map/ppermute | solution.py:22
  150.8 7.9 %collective-permute-start.60 = (f32[3,128,128]{2,1,0:T(8,128)S(1)}, f32[3,128,128]{2,1,0:T(8,128)S(1)}, u32[]{:S(2)}, u32[]{:S(2)}) collective-permute-start(f32[3,128,128]{2,1,0:T(8,128)S(1)} %pad_maximum_fusion.5.refs_0_), channel_id=1, source_target_pairs={{0,96},{32,0},{64,32},{96,64},{1,97},{33,1},{65,33},{97,65},{2,98}... | collective-permute-start | bytes 589832 | tf_op jit(solution)/shard_map/ppermute | solution.py:22
  151.9 9.7 %collective-permute-start.61 = (f32[3,128,128]{2,1,0:T(8,128)S(1)}, f32[3,128,128]{2,1,0:T(8,128)S(1)}, u32[]{:S(2)}, u32[]{:S(2)}) collective-permute-start(f32[3,128,128]{2,1,0:T(8,128)S(1)} %pad_maximum_fusion.5.refs_0_), channel_id=1, source_target_pairs={{0,16},{16,0},{1,17},{17,1},{2,18},{18,2},{3,19},{19,3},{4,20},{20... | collective-permute-start | bytes 589832 | tf_op jit(solution)/shard_map/ppermute | solution.py:18
  155.3 6.2 %collective-permute-start.62 = (f32[3,128,128]{2,1,0:T(8,128)S(1)}, f32[3,128,128]{2,1,0:T(8,128)S(1)}, u32[]{:S(2)}, u32[]{:S(2)}) collective-permute-start(f32[3,128,128]{2,1,0:T(8,128)S(1)} %collective-permute-done.58.refs_1_), channel_id=1, source_target_pairs={{0,16},{16,0},{1,17},{17,1},{2,18},{18,2},{3,19},{19,3},{4,20},{20... | collective-permute-start | bytes 589832 | tf_op jit(solution)/shard_map/ppermute | solution.py:18
  166.2 7.0 %collective-permute-start.65 = (f32[64,256]{1,0:T(8,128)S(1)}, f32[64,256]{1,0:T(8,128)S(1)}, u32[]{:S(2)}, u32[]{:S(2)}) collective-permute-start(f32[64,256]{1,0:T(8,128)S(1)} %full_product.8.refs_1_), channel_id=1, source_target_pairs={{0,32},{32,64},{64,96},{96,0},{1,33},{33,65},{65,97},{97,1},{2,34}... | collective-permute-start | bytes 196616 | tf_op jit(solution)/shard_map/ppermute | solution.py:26
  166.3 7.1 %collective-permute-start.66 = (f32[64,256]{1,0:T(8,128)S(1)}, f32[64,256]{1,0:T(8,128)S(1)}, u32[]{:S(2)}, u32[]{:S(2)}) collective-permute-start(f32[64,256]{1,0:T(8,128)S(1)} %full_product.8.refs_1_), channel_id=1, source_target_pairs={{0,64},{32,96},{64,0},{96,32},{1,65},{33,97},{65,1},{97,33},{2,66}... | collective-permute-start | bytes 196616 | tf_op jit(solution)/shard_map/ppermute | solution.py:26
  167.6 6.0 %collective-permute-start.67 = (f32[64,256]{1,0:T(8,128)S(1)}, f32[64,256]{1,0:T(8,128)S(1)}, u32[]{:S(2)}, u32[]{:S(2)}) collective-permute-start(f32[64,256]{1,0:T(8,128)S(1)} %full_product.8.refs_1_), channel_id=1, source_target_pairs={{0,96},{32,0},{64,32},{96,64},{1,97},{33,1},{65,33},{97,65},{2,98}... | collective-permute-start | bytes 196616 | tf_op jit(solution)/shard_map/ppermute | solution.py:26
  175.7 5.1 %collective-permute-start.72 = (f32[1,64,128]{2,1,0:T(8,128)S(1)}, f32[1,64,128]{2,1,0:T(8,128)S(1)}, u32[]{:S(2)}, u32[]{:S(2)}) collective-permute-start(f32[1,64,128]{2,1,0:T(8,128)S(1)} %get-tuple-element.92), channel_id=1, source_target_pairs={{0,1},{1,0},{2,17},{3,16},{4,33},{5,32},{6,49},{7,48},{8,65},{9,64... | collective-permute-start | bytes 98312 | tf_op jit(solution)/shard_map/ppermute | solution.py:186
  178.1 6.7 %collective-permute-start.73 = (f32[1,64,128]{2,1,0:T(8,128)S(1)}, f32[1,64,128]{2,1,0:T(8,128)S(1)}, u32[]{:S(2)}, u32[]{:S(2)}) collective-permute-start(f32[1,64,128]{2,1,0:T(8,128)S(1)} %get-tuple-element.93), channel_id=1, source_target_pairs={{0,0},{1,1},{2,16},{3,17},{4,32},{5,33},{6,48},{7,49},{8,64},{9,65... | collective-permute-start | bytes 98312 | tf_op jit(solution)/shard_map/ppermute | solution.py:185
  184.9 13.2 %collective-permute-start.74 = (f32[1,128,128]{2,1,0:T(8,128)S(1)}, f32[1,128,128]{2,1,0:T(8,128)S(1)}, u32[]{:S(2)}, u32[]{:S(2)}) collective-permute-start(f32[1,128,128]{2,1,0:T(8,128)S(1)} %pad_maximum_fusion.6.refs_0_), channel_id=1, source_target_pairs={{0,32},{32,64},{64,96},{96,0},{1,33},{33,65},{65,97},{97,1},{2,34}... | collective-permute-start | bytes 196616 | tf_op jit(solution)/shard_map/ppermute | solution.py:22
  188.6 10.0 %collective-permute-start.75 = (f32[1,128,128]{2,1,0:T(8,128)S(1)}, f32[1,128,128]{2,1,0:T(8,128)S(1)}, u32[]{:S(2)}, u32[]{:S(2)}) collective-permute-start(f32[1,128,128]{2,1,0:T(8,128)S(1)} %pad_maximum_fusion.6.refs_0_), channel_id=1, source_target_pairs={{0,64},{32,96},{64,0},{96,32},{1,65},{33,97},{65,1},{97,33},{2,66}... | collective-permute-start | bytes 196616 | tf_op jit(solution)/shard_map/ppermute | solution.py:22
  (41 other events, 191.2 us)
Sparse Core Ops, SparseCore 0:
  10.4 78.4 all-gather.4
  91.6 69.8 all-gather.6
  216.5 94.1 reduce-scatter.3
